TPU v7x, 32 devices: a whole 2x2x4 slice. The times are simulated.
32 devices in a mesh: tm: 8 (over z, x), gz: 4 (over y, core).
Axes of the slice: x: 2, y: 2, z: 4, core: 2. Of those that a mesh axis runs over, the one named last changes fastest.
Arguments:
- states: float32 [8, 3, 64, 16, 128], P('tm', None, 'gz'), may hold values from -4 to 4
- rate: float32 [64, 16, 128], P('gz'), may hold values from 0.1 to 40
Outputs:
- new_states: float32 [8, 3, 64, 16, 128], P('tm', None, 'gz')
All inputs are finite; a program needn't handle non-finite values.
Results may differ from a plain program's by a relative error of at most 0.000044.
Values sent between devices are 32-bit elements; how exact they have to be, the bound alone decides.
No kernel may reach another device: no remote copies, remote signals or barrier semaphores. Data moves between devices by JAX's collectives and lax.ppermute only.
A program may use at most 128 MiB of HBM per device.

v0:
```python
import functools

import jax
import jax.numpy as jnp
from jax import lax
from jax.experimental import pallas as pl
from jax.experimental.pallas import tpu as pltpu
from jax.sharding import PartitionSpec as P

STEPS = 2
STAGES = 3 * STEPS
GROUP = 4
VISCOSITY = 0.05
TIME_STEP = 0.2
MIX = ((1.0, None), (0.25, 0.75), (2.0 / 3.0, 1.0 / 3.0))
VMEM = pl.BlockSpec(memory_space=pltpu.VMEM)
PARAMS = pltpu.CompilerParams(vmem_limit_bytes=16 * 1024 * 1024)


def call(kernel, out_shape, *args, scratch=(), flops=None):
    cost = None
    if flops is not None:
        cost = pl.CostEstimate(flops=flops, bytes_accessed=1 << 20, transcendentals=0)
    return pl.pallas_call(
        kernel,
        out_shape=out_shape,
        in_specs=[VMEM] * len(args),
        out_specs=jax.tree.map(lambda _: VMEM, out_shape),
        scratch_shapes=list(scratch),
        compiler_params=PARAMS,
        cost_estimate=cost,
    )(*args)


def f32(*shape):
    return jax.ShapeDtypeStruct(shape, jnp.float32)


def partner(k):
    return (GROUP - k) % GROUP


def spot():
    return lax.rem(lax.axis_index("tm"), GROUP)


def chunk_of(k):
    flip = 2 * lax.rem(lax.axis_index("tm") // GROUP, 2)
    return lax.bitwise_xor(lax.bitwise_xor(spot(), flip), partner(k))


def near_side():
    return 1 - lax.rem(lax.axis_index("gz"), 2)


def split_rows(ref, *lead):
    half = ref.shape[-2] // 2
    return [ref[(*lead, pl.ds(odd, half, stride=2), slice(None))] for odd in (0, 1)]


def join_rows(ref, lead, pair):
    half = ref.shape[-2] // 2
    for odd in (0, 1):
        ref[(*lead, pl.ds(odd, half, stride=2), slice(None))] = pair[odd]


def load(ref, *lead):
    return [[ref[(*lead, c, odd)] for odd in (0, 1)] for c in range(3)]


def store(ref, lead, value):
    for c in range(3):
        for odd in (0, 1):
            ref[(*lead, c, odd)] = value[c][odd]


def advance(last, here, ahead, alpha, upward=1.0):
    diffuse = alpha * TIME_STEP * VISCOSITY
    carry = alpha * TIME_STEP * 0.5
    result = [[None, None] for _ in range(3)]
    for odd in (0, 1):
        speed = [here[0][odd] * carry, here[1][odd] * carry, here[2][odd] * (carry * upward)]
        to_next = [diffuse - s for s in speed]
        to_last = [diffuse + s for s in speed]
        for c in range(3):
            w = here[c][odd]
            rows, width = w.shape
            other = here[c][1 - odd]
            if odd:
                y_next, y_last = pltpu.roll(other, rows - 1, 0), other
            else:
                y_next, y_last = other, pltpu.roll(other, 1, 0)
            total = (alpha - 6.0 * diffuse) * w
            total = total + (
                to_next[0] * pltpu.roll(w, width - 1, 1) + to_last[0] * pltpu.roll(w, 1, 1)
            )
            total = total + (to_next[1] * y_next + to_last[1] * y_last)
            total = total + (to_next[2] * ahead[c][odd] + to_last[2] * last[c][odd])
            result[c][odd] = total
    return result


def blend(new, beta, base):
    return [[new[c][odd] + beta * base[c][odd] for odd in (0, 1)] for c in range(3)]


def faces_kernel(own_ref, far_ref, near_ref):
    layers, width = own_ref.shape[1], near_ref.shape[1]
    near = near_side()
    top = layers - width
    far_ref[...] = own_ref[:, pl.ds((1 - near) * top, width)]
    near_ref[...] = own_ref[:, pl.ds(near * top, width)]


def inside_kernel(own_ref, rate_ref, edges, middle, faded, damp_ref, kept, damps, *fields):
    layers = own_ref.shape[1]
    half = layers // 2
    slices = lax.axis_size("tm")
    keep = (lax.axis_index("tm") != 0).astype(jnp.float32)

    def save(stage, z, value):
        low, high = z - stage, layers - 1 - stage - z
        if low < 3:
            store(edges, (stage, 0, low), value)
        if high < 3:
            store(edges, (stage, 1, high), value)

    for z in range(layers):
        side, slot = (0, z) if z < half else (1, layers - 1 - z)
        damp = [jnp.exp(r * (-1.0 / slices)) for r in split_rows(rate_ref, z)]
        start = [split_rows(own_ref, c, z) for c in range(3)]
        store(fields[0], (z,), start)
        store(kept, (side, slot), start)
        save(0, z, start)
        for odd in (0, 1):
            damps[side, slot, odd] = damp[odd]
        lost = [[damp[odd] * keep * start[c][odd] for odd in (0, 1)] for c in range(3)]
        if slot < STAGES:
            store(faded, (side, slot), lost)
        else:
            store(middle, (side, slot - STAGES), lost)

    for stage in range(1, STAGES + 1):
        kind = (stage - 1) % 3
        alpha, beta = MIX[kind]
        source, target = fields[kind], fields[(kind + 1) % 3]
        below, here = load(source, stage - 1), load(source, stage)
        for z in range(stage, layers - stage):
            above = load(source, z + 1)
            new = advance(below, here, above, alpha)
            if beta is not None:
                new = blend(new, beta, load(fields[0], z))
            if stage < STAGES:
                store(target, (z,), new)
                save(stage, z, new)
            else:
                side, slot = (0, z) if z < half else (1, layers - 1 - z)
                lost = load(middle, side, slot - STAGES)
                store(
                    middle,
                    (side, slot - STAGES),
                    [[new[c][odd] - lost[c][odd] for odd in (0, 1)] for c in range(3)],
                )
            below, here = here, above

    share = half // GROUP
    for far in (0, 1):
        side = far + (1 - 2 * far) * near_side()
        damp_ref[far] = damps[side, pl.ds(chunk_of(0) * share, share)]


def border(side, face_ref, edges, middle, faded, jumps, strip):
    width = STAGES
    upward = 1.0 - 2.0 * side.astype(jnp.float32)
    for slot in range(width):
        layer = slot + side * (width - 1 - 2 * slot)
        store(strip, (0, slot), [split_rows(face_ref, c, layer) for c in range(3)])

    def at(stage, slot):
        if slot < width:
            return load(strip, stage, slot)
        return load(edges, stage, side, slot - width)

    def step(turn, _):
        for kind, (alpha, beta) in enumerate(MIX):
            stage = 3 * turn + kind
            last, here = at(stage, 0), at(stage, 1)
            for slot in range(width):
                ahead = at(stage, slot + 2)
                new = advance(last, here, ahead, alpha, upward)
                if beta is not None:
                    new = blend(new, beta, at(3 * turn, slot + 1 + kind))
                store(strip, (stage + 1, slot), new)
                last, here = here, ahead
        return 0

    lax.fori_loop(0, STEPS, step, 0)
    for slot in range(jumps.shape[0]):
        if slot < width:
            end, lost = load(strip, STAGES, slot), load(faded, side, slot)
            store(jumps, (slot,), [[end[c][odd] - lost[c][odd] for odd in (0, 1)] for c in range(3)])
        else:
            store(jumps, (slot,), load(middle, side, slot - width))


def jumps_kernel(far, face_ref, edges, middle, faded, *refs):
    outs, strip, jumps = refs[:GROUP], refs[-2], refs[-1]
    side = far + (1 - 2 * far) * near_side()
    border(side, face_ref, edges, middle, faded, jumps, strip)
    share = outs[0].shape[0]
    for k, out in enumerate(outs):
        out[...] = jumps[pl.ds(chunk_of(k) * share, share)]


def sort_in(jumps, order):
    for k in range(GROUP):
        order[lax.bitwise_xor(spot(), partner(k))] = jumps[k][...]


def sort_out(order, outs):
    for k in range(GROUP):
        outs[k][...] = order[lax.bitwise_xor(spot(), partner(k))]


def run(order, damp, total):
    for j in range(GROUP):
        jump = order[j]
        order[j] = total
        total = damp * total + jump
    return total


def total_kernel(far, *refs):
    jumps, damp_ref, out, order = refs[:GROUP], refs[GROUP], refs[GROUP + 1], refs[GROUP + 2]
    sort_in(jumps, order)
    out[...] = run(order, damp_ref[far][:, None], jnp.zeros(out.shape, jnp.float32))


def spread_kernel(far, *refs):
    carry_ref, jumps, damp_ref = refs[0], refs[1 : 1 + GROUP], refs[1 + GROUP]
    outs, order = refs[GROUP + 2 : -1], refs[-1]
    sort_in(jumps, order)
    run(order, damp_ref[far][:, None], jnp.where(lax.axis_index("tm") < GROUP, 0.0, carry_ref[...]))
    sort_out(order, outs)


def finish_kernel(kept, *refs):
    out = refs[-1]
    layers = out.shape[1]
    half = layers // 2
    share = half // GROUP
    first_slice = lax.axis_index("tm") == 0

    def put(side, slot, layer_of):
        layer = slot + side * (layers - 1 - 2 * slot)
        for c in range(3):
            join_rows(out, (c, layer), layer_of[c])

    @pl.when(first_slice)
    def _():
        for side in (0, 1):
            for slot in range(half):
                put(side, slot, load(kept, side, slot))

    @pl.when(jnp.logical_not(first_slice))
    def _():
        for far in (0, 1):
            side = far + (1 - 2 * far) * near_side()
            for k in range(GROUP):
                for j in range(share):
                    put(side, chunk_of(k) * share + j, load(refs[(1 - far) * GROUP + k], j))


def shards(states, rate):
    slices = lax.axis_size("tm")
    slabs = lax.axis_size("gz")
    groups = slices // GROUP
    own = states[0]
    layers, rows, width = own.shape[1:]
    half, share = layers // 2, layers // 2 // GROUP
    tile = (3, 2, rows // 2, width)
    face = f32(3, STAGES, rows, width)
    piece = f32(share, *tile)
    team = lax.axis_index("tm") // GROUP

    def halo(value, pairs):
        return lax.ppermute(value, "gz", [(i, j % slabs) for i, j in pairs])

    def swap(parts):
        return [parts[0]] + [
            lax.ppermute(parts[k], "tm", [(i, i ^ partner(k)) for i in range(slices)])
            for k in range(1, GROUP)
        ]

    def onward(value, distance):
        flip = 2 * (distance % 2)
        pairs = [(i, ((i ^ flip) + distance * GROUP) % slices) for i in range(slices)]
        return lax.ppermute(value, "tm", pairs)

    far_face, near_face = call(faces_kernel, [face, face], own)
    near_face = halo(near_face, [(i, i ^ 1) for i in range(slabs)])
    far_face = halo(far_face, [(i, i + 1 if i % 2 else i - 1 + slabs) for i in range(slabs)])
    edges, middle, faded, damp, kept = call(
        inside_kernel,
        [
            f32(STAGES, 2, 3, *tile),
            f32(2, half - STAGES, *tile),
            f32(2, STAGES, *tile),
            f32(2, share, *tile[1:]),
            f32(2, half, *tile),
        ],
        own, rate,
        scratch=[pltpu.VMEM((2, half, *tile[1:]), jnp.float32)]
        + [pltpu.VMEM((layers, *tile), jnp.float32)] * 3,
        flops=1 << 26,
    )
    strip = pltpu.VMEM((STAGES + 1, STAGES, *tile), jnp.float32)
    order = pltpu.VMEM((GROUP, *piece.shape), jnp.float32)

    def after(value, earlier):
        return lax.optimization_barrier((value, earlier))[0]

    halves = []
    for far, face_ref in enumerate((near_face, far_face)):
        jumps = call(
            functools.partial(jumps_kernel, far), [piece] * GROUP, face_ref, edges, middle, faded,
            scratch=[strip, pltpu.VMEM((half, *tile), jnp.float32)],
            flops=1 << 32,
        )
        halves.append(swap(jumps))

    carries, total = [], None
    for far, jumps in enumerate(halves):
        if far:
            jumps[0] = after(jumps[0], total)
        total = call(
            functools.partial(total_kernel, far), piece, *jumps, damp, scratch=[order]
        )
        carry = onward(total, 1)
        if groups > 2:
            carry = jnp.where(team < 1, 0.0, carry)
            fade, distance = damp[far][:, None] ** GROUP, 1
            while distance < groups - 1:
                carry = carry + jnp.where(team < distance, 0.0, fade * onward(carry, distance))
                distance, fade = 2 * distance, fade * fade
        carries.append(carry)

    pieces, news = [], None
    for far, (jumps, carry) in enumerate(zip(halves, carries)):
        if far:
            jumps[0] = after(jumps[0], news[0])
        news = call(
            functools.partial(spread_kernel, far), [piece] * GROUP, carry, *jumps, damp,
            scratch=[order],
            flops=1 << 32,
        )
        pieces = swap(news) + pieces
    updated = call(finish_kernel, f32(*own.shape), kept, *pieces)
    return updated[None]


def solution(mesh):
    return jax.shard_map(
        shards,
        mesh=mesh,
        in_specs=(P("tm", None, "gz", None, None), P("gz", None, None)),
        out_specs=P("tm", None, "gz", None, None),
        check_vma=False,
    )
```

profile of v0, /device:TPU:0, one launch (start us, length us, event | category | flops | bytes accessed | tf_op | source)
XLA Modules:
  0.0 31.7 jit_solution(10642397573632207003)
XLA Ops:
  0.0 1.0 %copy-done = f32[1,3,16,16,128]{4,3,2,1,0:T(8,128)S(1)} copy-done((f32[1,3,16,16,128]{4,3,2,1,0:T(8,128)S(1)}, f32[1,3,16,16,128]{4,3,2,1,0:T(8,128)}, u32[]{:S(2)}) %copy-start) | copy-done | bytes 393240
  1.0 0.5 %collective-permute-start.1 = (f32[3,6,16,128]{3,2,1,0:T(8,128)S(1)}, f32[3,6,16,128]{3,2,1,0:T(8,128)S(1)}, u32[]{:S(2)}, u32[]{:S(2)}) collective-permute-start(f32[3,6,16,128]{3,2,1,0:T(8,128)S(1)} %get-tuple-element.36), channel_id=1, source_target_pairs={{0,1},{1,0},{2,3},{3,2},{4,5},{5,4},{6,7},{7,6},{8,9},{9,8},{10,11... | collective-permute-start | bytes 442376 | tf_op jit(solution)/shard_map/ppermute | solution.py:287
  1.5 2.6 %collective-permute-start = (f32[3,6,16,128]{3,2,1,0:T(8,128)S(1)}, f32[3,6,16,128]{3,2,1,0:T(8,128)S(1)}, u32[]{:S(2)}, u32[]{:S(2)}) collective-permute-start(f32[3,6,16,128]{3,2,1,0:T(8,128)S(1)} %get-tuple-element.31), channel_id=1, source_target_pairs={{0,3},{1,2},{2,1},{3,0},{4,7},{5,6},{6,5},{7,4},{8,11},{9,10},{10,... | collective-permute-start | bytes 442376 | tf_op jit(solution)/shard_map/ppermute | solution.py:287
  4.2 0.8 %shard_map.28 = (f32[6,2,3,3,2,8,128]{6,5,4,3,2,1,0:T(8,128)S(1)}, f32[2,2,3,2,8,128]{5,4,3,2,1,0:T(8,128)S(1)}, f32[2,6,3,2,8,128]{5,4,3,2,1,0:T(8,128)S(1)}, f...) custom-call(f32[3,16,16,128]{3,2,1,0:T(8,128)S(1)} %bitcast.3, f32[16,16,128]{2,1,0:T(8,128)S(1)} %copy-done.1), custom_call_target="tpu_custom_call" | custom-call | flops 67108864 | bytes 1048576 | tf_op jit(solution)/shard_map/pallas_call | solution.py:24
  5.0 0.0 collective-permute-done.1.face_ref
  5.0 0.7 %shard_map.31 = (f32[2,3,2,8,128]{4,3,2,1,0:T(8,128)S(1)}, f32[2,3,2,8,128]{4,3,2,1,0:T(8,128)S(1)}, f32[2,3,2,8,128]{4,3,2,1,0:T(8,128)S(1)}, f32[2,3,2,8,128]{4,3,2,1,0:T(8,128)S(1)}) custom-call(f32[3,6,16,128]{3,2,1,0:T(8,128)S(1)} %collective-permute-done.1.face_ref, f32[6,2,3,3,2,8,128]{6,5,4,3,2,1,0:T(8,128)S(1)} %get-tuple-element.32.edges, ...), custom_call_target="tpu_custom_call" | custom-call | flops 4294967296 | bytes 1048576 | tf_op jit(solution)/shard_map/pallas_call | solution.py:24
  5.8 2.6 %collective-permute-start.2 = (f32[2,3,2,8,128]{4,3,2,1,0:T(8,128)S(1)}, f32[2,3,2,8,128]{4,3,2,1,0:T(8,128)S(1)}, u32[]{:S(2)}, u32[]{:S(2)}) collective-permute-start(f32[2,3,2,8,128]{4,3,2,1,0:T(8,128)S(1)} %get-tuple-element.38), channel_id=1, source_target_pairs={{0,12},{4,8},{8,4},{12,0},{16,28},{20,24},{24,20},{28,16},{1,13},{... | collective-permute-start | bytes 147464 | tf_op jit(solution)/shard_map/ppermute | solution.py:291
  8.3 0.4 %collective-permute-start.3 = (f32[2,3,2,8,128]{4,3,2,1,0:T(8,128)S(1)}, f32[2,3,2,8,128]{4,3,2,1,0:T(8,128)S(1)}, u32[]{:S(2)}, u32[]{:S(2)}) collective-permute-start(f32[2,3,2,8,128]{4,3,2,1,0:T(8,128)S(1)} %get-tuple-element.39), channel_id=1, source_target_pairs={{0,8},{4,12},{8,0},{12,4},{16,24},{20,28},{24,16},{28,20},{1,9},{5... | collective-permute-start | bytes 147464 | tf_op jit(solution)/shard_map/ppermute | solution.py:291
  8.8 0.5 %collective-permute-start.4 = (f32[2,3,2,8,128]{4,3,2,1,0:T(8,128)S(1)}, f32[2,3,2,8,128]{4,3,2,1,0:T(8,128)S(1)}, u32[]{:S(2)}, u32[]{:S(2)}) collective-permute-start(f32[2,3,2,8,128]{4,3,2,1,0:T(8,128)S(1)} %get-tuple-element.40), channel_id=1, source_target_pairs={{0,4},{4,0},{8,12},{12,8},{16,20},{20,16},{24,28},{28,24},{1,5},{5... | collective-permute-start | bytes 147464 | tf_op jit(solution)/shard_map/ppermute | solution.py:291
  9.3 0.0 collective-permute-done.face_ref
  9.3 0.7 %shard_map.30 = (f32[2,3,2,8,128]{4,3,2,1,0:T(8,128)S(1)}, f32[2,3,2,8,128]{4,3,2,1,0:T(8,128)S(1)}, f32[2,3,2,8,128]{4,3,2,1,0:T(8,128)S(1)}, f32[2,3,2,8,128]{4,3,2,1,0:T(8,128)S(1)}) custom-call(f32[3,6,16,128]{3,2,1,0:T(8,128)S(1)} %collective-permute-done.face_ref, f32[6,2,3,3,2,8,128]{6,5,4,3,2,1,0:T(8,128)S(1)} %get-tuple-element.32.edges, ...), custom_call_target="tpu_custom_call" | custom-call | flops 4294967296 | bytes 1048576 | tf_op jit(solution)/shard_map/pallas_call | solution.py:24
  10.0 2.6 %collective-permute-start.5 = (f32[2,3,2,8,128]{4,3,2,1,0:T(8,128)S(1)}, f32[2,3,2,8,128]{4,3,2,1,0:T(8,128)S(1)}, u32[]{:S(2)}, u32[]{:S(2)}) collective-permute-start(f32[2,3,2,8,128]{4,3,2,1,0:T(8,128)S(1)} %get-tuple-element.43), channel_id=1, source_target_pairs={{0,12},{4,8},{8,4},{12,0},{16,28},{20,24},{24,20},{28,16},{1,13},{... | collective-permute-start | bytes 147464 | tf_op jit(solution)/shard_map/ppermute | solution.py:291
  12.6 0.4 %collective-permute-start.6 = (f32[2,3,2,8,128]{4,3,2,1,0:T(8,128)S(1)}, f32[2,3,2,8,128]{4,3,2,1,0:T(8,128)S(1)}, u32[]{:S(2)}, u32[]{:S(2)}) collective-permute-start(f32[2,3,2,8,128]{4,3,2,1,0:T(8,128)S(1)} %get-tuple-element.44), channel_id=1, source_target_pairs={{0,8},{4,12},{8,0},{12,4},{16,24},{20,28},{24,16},{28,20},{1,9},{5... | collective-permute-start | bytes 147464 | tf_op jit(solution)/shard_map/ppermute | solution.py:291
  13.1 0.5 %collective-permute-start.7 = (f32[2,3,2,8,128]{4,3,2,1,0:T(8,128)S(1)}, f32[2,3,2,8,128]{4,3,2,1,0:T(8,128)S(1)}, u32[]{:S(2)}, u32[]{:S(2)}) collective-permute-start(f32[2,3,2,8,128]{4,3,2,1,0:T(8,128)S(1)} %get-tuple-element.45), channel_id=1, source_target_pairs={{0,4},{4,0},{8,12},{12,8},{16,20},{20,16},{24,28},{28,24},{1,5},{5... | collective-permute-start | bytes 147464 | tf_op jit(solution)/shard_map/ppermute | solution.py:291
  13.6 3.7 %collective-permute-start.9 = (f32[2,3,2,8,128]{4,3,2,1,0:T(8,128)S(1)}, f32[2,3,2,8,128]{4,3,2,1,0:T(8,128)S(1)}, u32[]{:S(2)}, u32[]{:S(2)}) collective-permute-start(f32[2,3,2,8,128]{4,3,2,1,0:T(8,128)S(1)} %shard_map.32), channel_id=1, source_target_pairs={{0,24},{4,28},{8,16},{12,20},{16,8},{20,12},{24,0},{28,4},{1,25},{... | collective-permute-start | bytes 147464 | tf_op jit(solution)/shard_map/ppermute | solution.py:298
  17.3 0.0 collective-permute-done.7.refs_3_.refs_4_
  17.4 3.5 %collective-permute-start.8 = (f32[2,3,2,8,128]{4,3,2,1,0:T(8,128)S(1)}, f32[2,3,2,8,128]{4,3,2,1,0:T(8,128)S(1)}, u32[]{:S(2)}, u32[]{:S(2)}) collective-permute-start(f32[2,3,2,8,128]{4,3,2,1,0:T(8,128)S(1)} %shard_map.33), channel_id=1, source_target_pairs={{0,24},{4,28},{8,16},{12,20},{16,8},{20,12},{24,0},{28,4},{1,25},{... | collective-permute-start | bytes 147464 | tf_op jit(solution)/shard_map/ppermute | solution.py:298
  20.9 0.0 collective-permute-done.9.refs_0_
  20.9 0.1 shard_map.34
  20.9 0.1 collective-permute-start.13
  21.0 2.0 %collective-permute-start.14 = (f32[2,3,2,8,128]{4,3,2,1,0:T(8,128)S(1)}, f32[2,3,2,8,128]{4,3,2,1,0:T(8,128)S(1)}, u32[]{:S(2)}, u32[]{:S(2)}) collective-permute-start(f32[2,3,2,8,128]{4,3,2,1,0:T(8,128)S(1)} %get-tuple-element.53), channel_id=1, source_target_pairs={{0,8},{4,12},{8,0},{12,4},{16,24},{20,28},{24,16},{28,20},{1,9},{5... | collective-permute-start | bytes 147464 | tf_op jit(solution)/shard_map/ppermute | solution.py:291
  23.0 1.5 %collective-permute-start.15 = (f32[2,3,2,8,128]{4,3,2,1,0:T(8,128)S(1)}, f32[2,3,2,8,128]{4,3,2,1,0:T(8,128)S(1)}, u32[]{:S(2)}, u32[]{:S(2)}) collective-permute-start(f32[2,3,2,8,128]{4,3,2,1,0:T(8,128)S(1)} %get-tuple-element.54), channel_id=1, source_target_pairs={{0,4},{4,0},{8,12},{12,8},{16,20},{20,16},{24,28},{28,24},{1,5},{5... | collective-permute-start | bytes 147464 | tf_op jit(solution)/shard_map/ppermute | solution.py:291
  24.5 0.1 shard_map.35
  24.5 0.1 collective-permute-start.10
  24.7 2.2 %collective-permute-start.11 = (f32[2,3,2,8,128]{4,3,2,1,0:T(8,128)S(1)}, f32[2,3,2,8,128]{4,3,2,1,0:T(8,128)S(1)}, u32[]{:S(2)}, u32[]{:S(2)}) collective-permute-start(f32[2,3,2,8,128]{4,3,2,1,0:T(8,128)S(1)} %get-tuple-element.50), channel_id=1, source_target_pairs={{0,8},{4,12},{8,0},{12,4},{16,24},{20,28},{24,16},{28,20},{1,9},{5... | collective-permute-start | bytes 147464 | tf_op jit(solution)/shard_map/ppermute | solution.py:291
  26.9 0.0 collective-permute-done.13.refs_5_
  26.9 1.2 %collective-permute-start.12 = (f32[2,3,2,8,128]{4,3,2,1,0:T(8,128)S(1)}, f32[2,3,2,8,128]{4,3,2,1,0:T(8,128)S(1)}, u32[]{:S(2)}, u32[]{:S(2)}) collective-permute-start(f32[2,3,2,8,128]{4,3,2,1,0:T(8,128)S(1)} %get-tuple-element.51), channel_id=1, source_target_pairs={{0,4},{4,0},{8,12},{12,8},{16,20},{20,16},{24,28},{28,24},{1,5},{5... | collective-permute-start | bytes 147464 | tf_op jit(solution)/shard_map/ppermute | solution.py:291
  28.1 0.0 collective-permute-done.15.refs_7_
  28.1 1.5 %collective-permute-done.10.refs_1_ = f32[2,3,2,8,128]{4,3,2,1,0:T(8,128)S(1)} collective-permute-done((f32[2,3,2,8,128]{4,3,2,1,0:T(8,128)S(1)}, f32[2,3,2,8,128]{4,3,2,1,0:T(8,128)S(1)}, u32[]{:S(2)}, u32[]{:S(2)}) %collective-permute-start.10) | collective-permute-done | bytes 49184 | tf_op jit(solution)/shard_map/ppermute | solution.py:291
  29.6 0.0 collective-permute-done.11.refs_2_
  29.6 1.4 %collective-permute-done.12.refs_3_ = f32[2,3,2,8,128]{4,3,2,1,0:T(8,128)S(1)} collective-permute-done((f32[2,3,2,8,128]{4,3,2,1,0:T(8,128)S(1)}, f32[2,3,2,8,128]{4,3,2,1,0:T(8,128)S(1)}, u32[]{:S(2)}, u32[]{:S(2)}) %collective-permute-start.12) | collective-permute-done | bytes 49184 | tf_op jit(solution)/shard_map/ppermute | solution.py:291
  31.0 0.8 %shard_map.36 = f32[3,16,16,128]{3,2,1,0:T(8,128)} custom-call(f32[2,8,3,2,8,128]{5,4,3,2,1,0:T(8,128)S(1)} %get-tuple-element.30.kept, f32[2,3,2,8,128]{4,3,2,1,0:T(8,128)S(1)} %get-tuple-element.48.refs_0_, f32[2,3,2,8,128]{4,3,2,1,0:T(8,128)S(1)} %collective-permute-done.10.refs_1_, f32[2,3,2,8,128]{4,3,2,1,0:T(8,128)S(1)} %collective-permute-done.11.refs_2_, ...), custom_call_target="tpu_custom_call" | custom-call | tf_op jit(solution)/shard_map/pallas_call | solution.py:24
  (13 shorter events, 0.1 us)
Async XLA Ops:
  0.0 1.0 %copy-start = (f32[1,3,16,16,128]{4,3,2,1,0:T(8,128)S(1)}, f32[1,3,16,16,128]{4,3,2,1,0:T(8,128)}, u32[]{:S(2)}) copy-start(f32[1,3,16,16,128]{4,3,2,1,0:T(8,128)} %param.2) | copy-start | bytes 1179652
  1.0 3.2 %copy-start.1 = (f32[16,16,128]{2,1,0:T(8,128)S(1)}, f32[16,16,128]{2,1,0:T(8,128)}, u32[]{:S(2)}) copy-start(f32[16,16,128]{2,1,0:T(8,128)} %rate_ref.1) | copy-start | bytes 393220
  1.0 4.0 %collective-permute-start.1 = (f32[3,6,16,128]{3,2,1,0:T(8,128)S(1)}, f32[3,6,16,128]{3,2,1,0:T(8,128)S(1)}, u32[]{:S(2)}, u32[]{:S(2)}) collective-permute-start(f32[3,6,16,128]{3,2,1,0:T(8,128)S(1)} %get-tuple-element.36), channel_id=1, source_target_pairs={{0,1},{1,0},{2,3},{3,2},{4,5},{5,4},{6,7},{7,6},{8,9},{9,8},{10,11... | collective-permute-start | bytes 442376 | tf_op jit(solution)/shard_map/ppermute | solution.py:287
  1.5 7.8 %collective-permute-start = (f32[3,6,16,128]{3,2,1,0:T(8,128)S(1)}, f32[3,6,16,128]{3,2,1,0:T(8,128)S(1)}, u32[]{:S(2)}, u32[]{:S(2)}) collective-permute-start(f32[3,6,16,128]{3,2,1,0:T(8,128)S(1)} %get-tuple-element.31), channel_id=1, source_target_pairs={{0,3},{1,2},{2,1},{3,0},{4,7},{5,6},{6,5},{7,4},{8,11},{9,10},{10,... | collective-permute-start | bytes 442376 | tf_op jit(solution)/shard_map/ppermute | solution.py:287
  5.8 7.3 %collective-permute-start.2 = (f32[2,3,2,8,128]{4,3,2,1,0:T(8,128)S(1)}, f32[2,3,2,8,128]{4,3,2,1,0:T(8,128)S(1)}, u32[]{:S(2)}, u32[]{:S(2)}) collective-permute-start(f32[2,3,2,8,128]{4,3,2,1,0:T(8,128)S(1)} %get-tuple-element.38), channel_id=1, source_target_pairs={{0,12},{4,8},{8,4},{12,0},{16,28},{20,24},{24,20},{28,16},{1,13},{... | collective-permute-start | bytes 147464 | tf_op jit(solution)/shard_map/ppermute | solution.py:291
  8.3 5.2 %collective-permute-start.3 = (f32[2,3,2,8,128]{4,3,2,1,0:T(8,128)S(1)}, f32[2,3,2,8,128]{4,3,2,1,0:T(8,128)S(1)}, u32[]{:S(2)}, u32[]{:S(2)}) collective-permute-start(f32[2,3,2,8,128]{4,3,2,1,0:T(8,128)S(1)} %get-tuple-element.39), channel_id=1, source_target_pairs={{0,8},{4,12},{8,0},{12,4},{16,24},{20,28},{24,16},{28,20},{1,9},{5... | collective-permute-start | bytes 147464 | tf_op jit(solution)/shard_map/ppermute | solution.py:291
  8.8 4.8 %collective-permute-start.4 = (f32[2,3,2,8,128]{4,3,2,1,0:T(8,128)S(1)}, f32[2,3,2,8,128]{4,3,2,1,0:T(8,128)S(1)}, u32[]{:S(2)}, u32[]{:S(2)}) collective-permute-start(f32[2,3,2,8,128]{4,3,2,1,0:T(8,128)S(1)} %get-tuple-element.40), channel_id=1, source_target_pairs={{0,4},{4,0},{8,12},{12,8},{16,20},{20,16},{24,28},{28,24},{1,5},{5... | collective-permute-start | bytes 147464 | tf_op jit(solution)/shard_map/ppermute | solution.py:291
  10.0 7.3 %collective-permute-start.5 = (f32[2,3,2,8,128]{4,3,2,1,0:T(8,128)S(1)}, f32[2,3,2,8,128]{4,3,2,1,0:T(8,128)S(1)}, u32[]{:S(2)}, u32[]{:S(2)}) collective-permute-start(f32[2,3,2,8,128]{4,3,2,1,0:T(8,128)S(1)} %get-tuple-element.43), channel_id=1, source_target_pairs={{0,12},{4,8},{8,4},{12,0},{16,28},{20,24},{24,20},{28,16},{1,13},{... | collective-permute-start | bytes 147464 | tf_op jit(solution)/shard_map/ppermute | solution.py:291
  12.6 4.7 %collective-permute-start.6 = (f32[2,3,2,8,128]{4,3,2,1,0:T(8,128)S(1)}, f32[2,3,2,8,128]{4,3,2,1,0:T(8,128)S(1)}, u32[]{:S(2)}, u32[]{:S(2)}) collective-permute-start(f32[2,3,2,8,128]{4,3,2,1,0:T(8,128)S(1)} %get-tuple-element.44), channel_id=1, source_target_pairs={{0,8},{4,12},{8,0},{12,4},{16,24},{20,28},{24,16},{28,20},{1,9},{5... | collective-permute-start | bytes 147464 | tf_op jit(solution)/shard_map/ppermute | solution.py:291
  13.1 4.3 %collective-permute-start.7 = (f32[2,3,2,8,128]{4,3,2,1,0:T(8,128)S(1)}, f32[2,3,2,8,128]{4,3,2,1,0:T(8,128)S(1)}, u32[]{:S(2)}, u32[]{:S(2)}) collective-permute-start(f32[2,3,2,8,128]{4,3,2,1,0:T(8,128)S(1)} %get-tuple-element.45), channel_id=1, source_target_pairs={{0,4},{4,0},{8,12},{12,8},{16,20},{20,16},{24,28},{28,24},{1,5},{5... | collective-permute-start | bytes 147464 | tf_op jit(solution)/shard_map/ppermute | solution.py:291
  13.6 7.2 %collective-permute-start.9 = (f32[2,3,2,8,128]{4,3,2,1,0:T(8,128)S(1)}, f32[2,3,2,8,128]{4,3,2,1,0:T(8,128)S(1)}, u32[]{:S(2)}, u32[]{:S(2)}) collective-permute-start(f32[2,3,2,8,128]{4,3,2,1,0:T(8,128)S(1)} %shard_map.32), channel_id=1, source_target_pairs={{0,24},{4,28},{8,16},{12,20},{16,8},{20,12},{24,0},{28,4},{1,25},{... | collective-permute-start | bytes 147464 | tf_op jit(solution)/shard_map/ppermute | solution.py:298
  17.4 7.1 %collective-permute-start.8 = (f32[2,3,2,8,128]{4,3,2,1,0:T(8,128)S(1)}, f32[2,3,2,8,128]{4,3,2,1,0:T(8,128)S(1)}, u32[]{:S(2)}, u32[]{:S(2)}) collective-permute-start(f32[2,3,2,8,128]{4,3,2,1,0:T(8,128)S(1)} %shard_map.33), channel_id=1, source_target_pairs={{0,24},{4,28},{8,16},{12,20},{16,8},{20,12},{24,0},{28,4},{1,25},{... | collective-permute-start | bytes 147464 | tf_op jit(solution)/shard_map/ppermute | solution.py:298
  20.9 5.9 %collective-permute-start.13 = (f32[2,3,2,8,128]{4,3,2,1,0:T(8,128)S(1)}, f32[2,3,2,8,128]{4,3,2,1,0:T(8,128)S(1)}, u32[]{:S(2)}, u32[]{:S(2)}) collective-permute-start(f32[2,3,2,8,128]{4,3,2,1,0:T(8,128)S(1)} %get-tuple-element.52), channel_id=1, source_target_pairs={{0,12},{4,8},{8,4},{12,0},{16,28},{20,24},{24,20},{28,16},{1,13},{... | collective-permute-start | bytes 147464 | tf_op jit(solution)/shard_map/ppermute | solution.py:291
  21.0 7.1 %collective-permute-start.14 = (f32[2,3,2,8,128]{4,3,2,1,0:T(8,128)S(1)}, f32[2,3,2,8,128]{4,3,2,1,0:T(8,128)S(1)}, u32[]{:S(2)}, u32[]{:S(2)}) collective-permute-start(f32[2,3,2,8,128]{4,3,2,1,0:T(8,128)S(1)} %get-tuple-element.53), channel_id=1, source_target_pairs={{0,8},{4,12},{8,0},{12,4},{16,24},{20,28},{24,16},{28,20},{1,9},{5... | collective-permute-start | bytes 147464 | tf_op jit(solution)/shard_map/ppermute | solution.py:291
  23.0 5.1 %collective-permute-start.15 = (f32[2,3,2,8,128]{4,3,2,1,0:T(8,128)S(1)}, f32[2,3,2,8,128]{4,3,2,1,0:T(8,128)S(1)}, u32[]{:S(2)}, u32[]{:S(2)}) collective-permute-start(f32[2,3,2,8,128]{4,3,2,1,0:T(8,128)S(1)} %get-tuple-element.54), channel_id=1, source_target_pairs={{0,4},{4,0},{8,12},{12,8},{16,20},{20,16},{24,28},{28,24},{1,5},{5... | collective-permute-start | bytes 147464 | tf_op jit(solution)/shard_map/ppermute | solution.py:291
  24.5 5.1 %collective-permute-start.10 = (f32[2,3,2,8,128]{4,3,2,1,0:T(8,128)S(1)}, f32[2,3,2,8,128]{4,3,2,1,0:T(8,128)S(1)}, u32[]{:S(2)}, u32[]{:S(2)}) collective-permute-start(f32[2,3,2,8,128]{4,3,2,1,0:T(8,128)S(1)} %get-tuple-element.49), channel_id=1, source_target_pairs={{0,12},{4,8},{8,4},{12,0},{16,28},{20,24},{24,20},{28,16},{1,13},{... | collective-permute-start | bytes 147464 | tf_op jit(solution)/shard_map/ppermute | solution.py:291
  24.7 4.9 %collective-permute-start.11 = (f32[2,3,2,8,128]{4,3,2,1,0:T(8,128)S(1)}, f32[2,3,2,8,128]{4,3,2,1,0:T(8,128)S(1)}, u32[]{:S(2)}, u32[]{:S(2)}) collective-permute-start(f32[2,3,2,8,128]{4,3,2,1,0:T(8,128)S(1)} %get-tuple-element.50), channel_id=1, source_target_pairs={{0,8},{4,12},{8,0},{12,4},{16,24},{20,28},{24,16},{28,20},{1,9},{5... | collective-permute-start | bytes 147464 | tf_op jit(solution)/shard_map/ppermute | solution.py:291
  26.9 4.1 %collective-permute-start.12 = (f32[2,3,2,8,128]{4,3,2,1,0:T(8,128)S(1)}, f32[2,3,2,8,128]{4,3,2,1,0:T(8,128)S(1)}, u32[]{:S(2)}, u32[]{:S(2)}) collective-permute-start(f32[2,3,2,8,128]{4,3,2,1,0:T(8,128)S(1)} %get-tuple-element.51), channel_id=1, source_target_pairs={{0,4},{4,0},{8,12},{12,8},{16,20},{20,16},{24,28},{28,24},{1,5},{5... | collective-permute-start | bytes 147464 | tf_op jit(solution)/shard_map/ppermute | solution.py:291
where the time goes:
time: 31.9 us; the launch traced here: 31.7 us
  starting transfers between devices  24.5 us (77%)
  Pallas kernels  3.24 us (10%)
  waiting for transfers between devices  2.88 us (9%)
  local copies, waits for them, and re-layouts  1 us (3%)
    ppermute x12, starting transfers between devices, swap(): lax.ppermute(parts[k], 'tm', [(i, i ^ partner(k)) for i in range(slices)])  14.2 us
    ppermute x2, starting transfers between devices, onward(): return lax.ppermute(value, 'tm', pairs)  7.15 us
    pallas_call x9, Pallas kernels, call(): pl.pallas_call(kernel, out_shape=out_shape, in_specs=[VMEM] * len(args),...  3.24 us
    ppermute x2, starting transfers between devices, halo(): return lax.ppermute(value, 'gz', [(i, j % slabs) for i, j in pairs])  3.16 us
    ppermute x12, waiting for transfers between devices, swap(): lax.ppermute(parts[k], 'tm', [(i, i ^ partner(k)) for i in range(slices)])  2.87 us
    unnamed x4, local copies, waits for them, and re-layouts  1 us
  transfers between devices with their start and end apart: 16, of which 2 were waited for; matrix products, arithmetic and copies ran while one was open for 0% of the time, Pallas kernels for 8%

commit v1 on v0

--- a/solution.py
+++ b/solution.py
@@ -45,8 +45,7 @@
 
 
 def chunk_of(k):
-    flip = 2 * lax.rem(lax.axis_index("tm") // GROUP, 2)
-    return lax.bitwise_xor(lax.bitwise_xor(spot(), flip), partner(k))
+    return lax.bitwise_xor(spot(), partner(k))
 
 
 def near_side():
@@ -293,9 +292,8 @@
         ]
 
     def onward(value, distance):
-        flip = 2 * (distance % 2)
-        pairs = [(i, ((i ^ flip) + distance * GROUP) % slices) for i in range(slices)]
-        return lax.ppermute(value, "tm", pairs)
+        step = distance * GROUP
+        return lax.ppermute(value, "tm", [(i, (i + step) % slices) for i in range(slices)])
 
     far_face, near_face = call(faces_kernel, [face, face], own)
     near_face = halo(near_face, [(i, i ^ 1) for i in range(slabs)])

time: 31.9 us -> 30.8 us (0.966)
  starting transfers between devices: 24.5 us -> 22.7 us
  waiting for transfers between devices: 2.88 us -> 3.69 us
    ppermute x2, starting transfers between devices: 7.15 us -> 5.31 us  [onward(): lax.ppermute(value, 'tm', [(i, (i + step) % slices) for i in range(slices)])]
    ppermute x12, waiting for transfers between devices: 2.87 us -> 3.68 us  [swap(): lax.ppermute(parts[k], 'tm', [(i, i ^ partner(k)) for i in range(slices)])]
  transfers between devices with their start and end apart: 16 -> 16, of which waited for: 2 -> 5; matrix products, arithmetic and copies ran while one was open for 0% -> 0% of each run, Pallas kernels for 8% -> 8%
where the time goes in v1:
time: 30.8 us; the launch traced here: 30.7 us
  starting transfers between devices  22.7 us (74%)
  waiting for transfers between devices  3.69 us (12%)
  Pallas kernels  3.24 us (11%)
  local copies, waits for them, and re-layouts  1 us (3%)
    ppermute x12, starting transfers between devices, swap(): lax.ppermute(parts[k], 'tm', [(i, i ^ partner(k)) for i in range(slices)])  14.2 us
    ppermute x2, starting transfers between devices, onward(): lax.ppermute(value, 'tm', [(i, (i + step) % slices) for i in range(slices)])  5.31 us
    ppermute x12, waiting for transfers between devices, swap(): lax.ppermute(parts[k], 'tm', [(i, i ^ partner(k)) for i in range(slices)])  3.68 us
    pallas_call x9, Pallas kernels, call(): pl.pallas_call(kernel, out_shape=out_shape, in_specs=[VMEM] * len(args),...  3.24 us
    ppermute x2, starting transfers between devices, halo(): return lax.ppermute(value, 'gz', [(i, j % slabs) for i, j in pairs])  3.16 us
    unnamed x4, local copies, waits for them, and re-layouts  1 us
  transfers between devices with their start and end apart: 16, of which 5 were waited for; matrix products, arithmetic and copies ran while one was open for 0% of the time, Pallas kernels for 8%

profile of v1, /device:TPU:0, one launch (start us, length us, event | category | flops | bytes accessed | tf_op | source)
XLA Modules:
  0.0 30.7 jit_solution(13283954360753547872)
XLA Ops:
  0.0 1.0 %copy-done = f32[1,3,16,16,128]{4,3,2,1,0:T(8,128)S(1)} copy-done((f32[1,3,16,16,128]{4,3,2,1,0:T(8,128)S(1)}, f32[1,3,16,16,128]{4,3,2,1,0:T(8,128)}, u32[]{:S(2)}) %copy-start) | copy-done | bytes 393240
  1.0 0.5 %collective-permute-start.1 = (f32[3,6,16,128]{3,2,1,0:T(8,128)S(1)}, f32[3,6,16,128]{3,2,1,0:T(8,128)S(1)}, u32[]{:S(2)}, u32[]{:S(2)}) collective-permute-start(f32[3,6,16,128]{3,2,1,0:T(8,128)S(1)} %get-tuple-element.36), channel_id=1, source_target_pairs={{0,1},{1,0},{2,3},{3,2},{4,5},{5,4},{6,7},{7,6},{8,9},{9,8},{10,11... | collective-permute-start | bytes 442376 | tf_op jit(solution)/shard_map/ppermute | solution.py:286
  1.5 2.6 %collective-permute-start = (f32[3,6,16,128]{3,2,1,0:T(8,128)S(1)}, f32[3,6,16,128]{3,2,1,0:T(8,128)S(1)}, u32[]{:S(2)}, u32[]{:S(2)}) collective-permute-start(f32[3,6,16,128]{3,2,1,0:T(8,128)S(1)} %get-tuple-element.31), channel_id=1, source_target_pairs={{0,3},{1,2},{2,1},{3,0},{4,7},{5,6},{6,5},{7,4},{8,11},{9,10},{10,... | collective-permute-start | bytes 442376 | tf_op jit(solution)/shard_map/ppermute | solution.py:286
  4.2 0.8 %shard_map.28 = (f32[6,2,3,3,2,8,128]{6,5,4,3,2,1,0:T(8,128)S(1)}, f32[2,2,3,2,8,128]{5,4,3,2,1,0:T(8,128)S(1)}, f32[2,6,3,2,8,128]{5,4,3,2,1,0:T(8,128)S(1)}, f...) custom-call(f32[3,16,16,128]{3,2,1,0:T(8,128)S(1)} %bitcast.3, f32[16,16,128]{2,1,0:T(8,128)S(1)} %copy-done.1), custom_call_target="tpu_custom_call" | custom-call | flops 67108864 | bytes 1048576 | tf_op jit(solution)/shard_map/pallas_call | solution.py:24
  5.0 0.7 %shard_map.31 = (f32[2,3,2,8,128]{4,3,2,1,0:T(8,128)S(1)}, f32[2,3,2,8,128]{4,3,2,1,0:T(8,128)S(1)}, f32[2,3,2,8,128]{4,3,2,1,0:T(8,128)S(1)}, f32[2,3,2,8,128]{4,3,2,1,0:T(8,128)S(1)}) custom-call(f32[3,6,16,128]{3,2,1,0:T(8,128)S(1)} %collective-permute-done.1.face_ref, f32[6,2,3,3,2,8,128]{6,5,4,3,2,1,0:T(8,128)S(1)} %get-tuple-element.32.edges, ...), custom_call_target="tpu_custom_call" | custom-call | flops 4294967296 | bytes 1048576 | tf_op jit(solution)/shard_map/pallas_call | solution.py:24
  5.8 2.6 %collective-permute-start.2 = (f32[2,3,2,8,128]{4,3,2,1,0:T(8,128)S(1)}, f32[2,3,2,8,128]{4,3,2,1,0:T(8,128)S(1)}, u32[]{:S(2)}, u32[]{:S(2)}) collective-permute-start(f32[2,3,2,8,128]{4,3,2,1,0:T(8,128)S(1)} %get-tuple-element.38), channel_id=1, source_target_pairs={{0,12},{4,8},{8,4},{12,0},{16,28},{20,24},{24,20},{28,16},{1,13},{... | collective-permute-start | bytes 147464 | tf_op jit(solution)/shard_map/ppermute | solution.py:290
  8.3 0.4 %collective-permute-start.3 = (f32[2,3,2,8,128]{4,3,2,1,0:T(8,128)S(1)}, f32[2,3,2,8,128]{4,3,2,1,0:T(8,128)S(1)}, u32[]{:S(2)}, u32[]{:S(2)}) collective-permute-start(f32[2,3,2,8,128]{4,3,2,1,0:T(8,128)S(1)} %get-tuple-element.39), channel_id=1, source_target_pairs={{0,8},{4,12},{8,0},{12,4},{16,24},{20,28},{24,16},{28,20},{1,9},{5... | collective-permute-start | bytes 147464 | tf_op jit(solution)/shard_map/ppermute | solution.py:290
  8.8 0.5 %collective-permute-start.4 = (f32[2,3,2,8,128]{4,3,2,1,0:T(8,128)S(1)}, f32[2,3,2,8,128]{4,3,2,1,0:T(8,128)S(1)}, u32[]{:S(2)}, u32[]{:S(2)}) collective-permute-start(f32[2,3,2,8,128]{4,3,2,1,0:T(8,128)S(1)} %get-tuple-element.40), channel_id=1, source_target_pairs={{0,4},{4,0},{8,12},{12,8},{16,20},{20,16},{24,28},{28,24},{1,5},{5... | collective-permute-start | bytes 147464 | tf_op jit(solution)/shard_map/ppermute | solution.py:290
  9.3 0.0 collective-permute-done.face_ref
  9.3 0.7 %shard_map.30 = (f32[2,3,2,8,128]{4,3,2,1,0:T(8,128)S(1)}, f32[2,3,2,8,128]{4,3,2,1,0:T(8,128)S(1)}, f32[2,3,2,8,128]{4,3,2,1,0:T(8,128)S(1)}, f32[2,3,2,8,128]{4,3,2,1,0:T(8,128)S(1)}) custom-call(f32[3,6,16,128]{3,2,1,0:T(8,128)S(1)} %collective-permute-done.face_ref, f32[6,2,3,3,2,8,128]{6,5,4,3,2,1,0:T(8,128)S(1)} %get-tuple-element.32.edges, ...), custom_call_target="tpu_custom_call" | custom-call | flops 4294967296 | bytes 1048576 | tf_op jit(solution)/shard_map/pallas_call | solution.py:24
  10.0 2.6 %collective-permute-start.5 = (f32[2,3,2,8,128]{4,3,2,1,0:T(8,128)S(1)}, f32[2,3,2,8,128]{4,3,2,1,0:T(8,128)S(1)}, u32[]{:S(2)}, u32[]{:S(2)}) collective-permute-start(f32[2,3,2,8,128]{4,3,2,1,0:T(8,128)S(1)} %get-tuple-element.43), channel_id=1, source_target_pairs={{0,12},{4,8},{8,4},{12,0},{16,28},{20,24},{24,20},{28,16},{1,13},{... | collective-permute-start | bytes 147464 | tf_op jit(solution)/shard_map/ppermute | solution.py:290
  12.6 0.4 %collective-permute-start.6 = (f32[2,3,2,8,128]{4,3,2,1,0:T(8,128)S(1)}, f32[2,3,2,8,128]{4,3,2,1,0:T(8,128)S(1)}, u32[]{:S(2)}, u32[]{:S(2)}) collective-permute-start(f32[2,3,2,8,128]{4,3,2,1,0:T(8,128)S(1)} %get-tuple-element.44), channel_id=1, source_target_pairs={{0,8},{4,12},{8,0},{12,4},{16,24},{20,28},{24,16},{28,20},{1,9},{5... | collective-permute-start | bytes 147464 | tf_op jit(solution)/shard_map/ppermute | solution.py:290
  13.1 0.0 collective-permute-done.2.refs_1_.refs_2_
  13.1 0.5 %collective-permute-start.7 = (f32[2,3,2,8,128]{4,3,2,1,0:T(8,128)S(1)}, f32[2,3,2,8,128]{4,3,2,1,0:T(8,128)S(1)}, u32[]{:S(2)}, u32[]{:S(2)}) collective-permute-start(f32[2,3,2,8,128]{4,3,2,1,0:T(8,128)S(1)} %get-tuple-element.45), channel_id=1, source_target_pairs={{0,4},{4,0},{8,12},{12,8},{16,20},{20,16},{24,28},{28,24},{1,5},{5... | collective-permute-start | bytes 147464 | tf_op jit(solution)/shard_map/ppermute | solution.py:290
  13.6 0.0 collective-permute-done.3.refs_2_.refs_3_
  13.6 0.0 collective-permute-done.4.refs_3_.refs_4_
  13.6 2.7 %collective-permute-start.9 = (f32[2,3,2,8,128]{4,3,2,1,0:T(8,128)S(1)}, f32[2,3,2,8,128]{4,3,2,1,0:T(8,128)S(1)}, u32[]{:S(2)}, u32[]{:S(2)}) collective-permute-start(f32[2,3,2,8,128]{4,3,2,1,0:T(8,128)S(1)} %shard_map.32), channel_id=1, source_target_pairs={{0,16},{4,20},{8,24},{12,28},{16,0},{20,4},{24,8},{28,12},{1,17},{... | collective-permute-start | bytes 147464 | tf_op jit(solution)/shard_map/ppermute | solution.py:296
  16.3 0.4 %collective-permute-done.6.refs_2_.refs_3_ = f32[2,3,2,8,128]{4,3,2,1,0:T(8,128)S(1)} collective-permute-done((f32[2,3,2,8,128]{4,3,2,1,0:T(8,128)S(1)}, f32[2,3,2,8,128]{4,3,2,1,0:T(8,128)S(1)}, u32[]{:S(2)}, u32[]{:S(2)}) %collective-permute-start.6) | collective-permute-done | bytes 49184 | tf_op jit(solution)/shard_map/ppermute | solution.py:290
  16.7 0.5 %collective-permute-done.7.refs_3_.refs_4_ = f32[2,3,2,8,128]{4,3,2,1,0:T(8,128)S(1)} collective-permute-done((f32[2,3,2,8,128]{4,3,2,1,0:T(8,128)S(1)}, f32[2,3,2,8,128]{4,3,2,1,0:T(8,128)S(1)}, u32[]{:S(2)}, u32[]{:S(2)}) %collective-permute-start.7) | collective-permute-done | bytes 49184 | tf_op jit(solution)/shard_map/ppermute | solution.py:290
  17.2 2.7 %collective-permute-start.8 = (f32[2,3,2,8,128]{4,3,2,1,0:T(8,128)S(1)}, f32[2,3,2,8,128]{4,3,2,1,0:T(8,128)S(1)}, u32[]{:S(2)}, u32[]{:S(2)}) collective-permute-start(f32[2,3,2,8,128]{4,3,2,1,0:T(8,128)S(1)} %shard_map.33), channel_id=1, source_target_pairs={{0,16},{4,20},{8,24},{12,28},{16,0},{20,4},{24,8},{28,12},{1,17},{... | collective-permute-start | bytes 147464 | tf_op jit(solution)/shard_map/ppermute | solution.py:296
  19.9 0.1 shard_map.34
  19.9 1.9 %collective-permute-start.13 = (f32[2,3,2,8,128]{4,3,2,1,0:T(8,128)S(1)}, f32[2,3,2,8,128]{4,3,2,1,0:T(8,128)S(1)}, u32[]{:S(2)}, u32[]{:S(2)}) collective-permute-start(f32[2,3,2,8,128]{4,3,2,1,0:T(8,128)S(1)} %get-tuple-element.52), channel_id=1, source_target_pairs={{0,12},{4,8},{8,4},{12,0},{16,28},{20,24},{24,20},{28,16},{1,13},{... | collective-permute-start | bytes 147464 | tf_op jit(solution)/shard_map/ppermute | solution.py:290
  21.8 0.4 %collective-permute-start.14 = (f32[2,3,2,8,128]{4,3,2,1,0:T(8,128)S(1)}, f32[2,3,2,8,128]{4,3,2,1,0:T(8,128)S(1)}, u32[]{:S(2)}, u32[]{:S(2)}) collective-permute-start(f32[2,3,2,8,128]{4,3,2,1,0:T(8,128)S(1)} %get-tuple-element.53), channel_id=1, source_target_pairs={{0,8},{4,12},{8,0},{12,4},{16,24},{20,28},{24,16},{28,20},{1,9},{5... | collective-permute-start | bytes 147464 | tf_op jit(solution)/shard_map/ppermute | solution.py:290
  22.2 1.3 %collective-permute-start.15 = (f32[2,3,2,8,128]{4,3,2,1,0:T(8,128)S(1)}, f32[2,3,2,8,128]{4,3,2,1,0:T(8,128)S(1)}, u32[]{:S(2)}, u32[]{:S(2)}) collective-permute-start(f32[2,3,2,8,128]{4,3,2,1,0:T(8,128)S(1)} %get-tuple-element.54), channel_id=1, source_target_pairs={{0,4},{4,0},{8,12},{12,8},{16,20},{20,16},{24,28},{28,24},{1,5},{5... | collective-permute-start | bytes 147464 | tf_op jit(solution)/shard_map/ppermute | solution.py:290
  23.5 0.1 shard_map.35
  23.5 1.9 %collective-permute-start.10 = (f32[2,3,2,8,128]{4,3,2,1,0:T(8,128)S(1)}, f32[2,3,2,8,128]{4,3,2,1,0:T(8,128)S(1)}, u32[]{:S(2)}, u32[]{:S(2)}) collective-permute-start(f32[2,3,2,8,128]{4,3,2,1,0:T(8,128)S(1)} %get-tuple-element.49), channel_id=1, source_target_pairs={{0,12},{4,8},{8,4},{12,0},{16,28},{20,24},{24,20},{28,16},{1,13},{... | collective-permute-start | bytes 147464 | tf_op jit(solution)/shard_map/ppermute | solution.py:290
  25.4 0.4 %collective-permute-start.11 = (f32[2,3,2,8,128]{4,3,2,1,0:T(8,128)S(1)}, f32[2,3,2,8,128]{4,3,2,1,0:T(8,128)S(1)}, u32[]{:S(2)}, u32[]{:S(2)}) collective-permute-start(f32[2,3,2,8,128]{4,3,2,1,0:T(8,128)S(1)} %get-tuple-element.50), channel_id=1, source_target_pairs={{0,8},{4,12},{8,0},{12,4},{16,24},{20,28},{24,16},{28,20},{1,9},{5... | collective-permute-start | bytes 147464 | tf_op jit(solution)/shard_map/ppermute | solution.py:290
  25.8 1.3 %collective-permute-start.12 = (f32[2,3,2,8,128]{4,3,2,1,0:T(8,128)S(1)}, f32[2,3,2,8,128]{4,3,2,1,0:T(8,128)S(1)}, u32[]{:S(2)}, u32[]{:S(2)}) collective-permute-start(f32[2,3,2,8,128]{4,3,2,1,0:T(8,128)S(1)} %get-tuple-element.51), channel_id=1, source_target_pairs={{0,4},{4,0},{8,12},{12,8},{16,20},{20,16},{24,28},{28,24},{1,5},{5... | collective-permute-start | bytes 147464 | tf_op jit(solution)/shard_map/ppermute | solution.py:290
  27.1 1.5 %collective-permute-done.10.refs_1_ = f32[2,3,2,8,128]{4,3,2,1,0:T(8,128)S(1)} collective-permute-done((f32[2,3,2,8,128]{4,3,2,1,0:T(8,128)S(1)}, f32[2,3,2,8,128]{4,3,2,1,0:T(8,128)S(1)}, u32[]{:S(2)}, u32[]{:S(2)}) %collective-permute-start.10) | collective-permute-done | bytes 49184 | tf_op jit(solution)/shard_map/ppermute | solution.py:290
  28.6 0.9 %collective-permute-done.11.refs_2_ = f32[2,3,2,8,128]{4,3,2,1,0:T(8,128)S(1)} collective-permute-done((f32[2,3,2,8,128]{4,3,2,1,0:T(8,128)S(1)}, f32[2,3,2,8,128]{4,3,2,1,0:T(8,128)S(1)}, u32[]{:S(2)}, u32[]{:S(2)}) %collective-permute-start.11) | collective-permute-done | bytes 49184 | tf_op jit(solution)/shard_map/ppermute | solution.py:290
  29.5 0.4 %collective-permute-done.12.refs_3_ = f32[2,3,2,8,128]{4,3,2,1,0:T(8,128)S(1)} collective-permute-done((f32[2,3,2,8,128]{4,3,2,1,0:T(8,128)S(1)}, f32[2,3,2,8,128]{4,3,2,1,0:T(8,128)S(1)}, u32[]{:S(2)}, u32[]{:S(2)}) %collective-permute-start.12) | collective-permute-done | bytes 49184 | tf_op jit(solution)/shard_map/ppermute | solution.py:290
  29.9 0.8 %shard_map.36 = f32[3,16,16,128]{3,2,1,0:T(8,128)} custom-call(f32[2,8,3,2,8,128]{5,4,3,2,1,0:T(8,128)S(1)} %get-tuple-element.30.kept, f32[2,3,2,8,128]{4,3,2,1,0:T(8,128)S(1)} %get-tuple-element.48.refs_0_, f32[2,3,2,8,128]{4,3,2,1,0:T(8,128)S(1)} %collective-permute-done.10.refs_1_, f32[2,3,2,8,128]{4,3,2,1,0:T(8,128)S(1)} %collective-permute-done.11.refs_2_, ...), custom_call_target="tpu_custom_call" | custom-call | tf_op jit(solution)/shard_map/pallas_call | solution.py:24
  (13 shorter events, 0.1 us)
Async XLA Ops:
  0.0 1.0 %copy-start = (f32[1,3,16,16,128]{4,3,2,1,0:T(8,128)S(1)}, f32[1,3,16,16,128]{4,3,2,1,0:T(8,128)}, u32[]{:S(2)}) copy-start(f32[1,3,16,16,128]{4,3,2,1,0:T(8,128)} %param.2) | copy-start | bytes 1179652
  1.0 3.2 %copy-start.1 = (f32[16,16,128]{2,1,0:T(8,128)S(1)}, f32[16,16,128]{2,1,0:T(8,128)}, u32[]{:S(2)}) copy-start(f32[16,16,128]{2,1,0:T(8,128)} %rate_ref.1) | copy-start | bytes 393220
  1.0 4.0 %collective-permute-start.1 = (f32[3,6,16,128]{3,2,1,0:T(8,128)S(1)}, f32[3,6,16,128]{3,2,1,0:T(8,128)S(1)}, u32[]{:S(2)}, u32[]{:S(2)}) collective-permute-start(f32[3,6,16,128]{3,2,1,0:T(8,128)S(1)} %get-tuple-element.36), channel_id=1, source_target_pairs={{0,1},{1,0},{2,3},{3,2},{4,5},{5,4},{6,7},{7,6},{8,9},{9,8},{10,11... | collective-permute-start | bytes 442376 | tf_op jit(solution)/shard_map/ppermute | solution.py:286
  1.5 7.8 %collective-permute-start = (f32[3,6,16,128]{3,2,1,0:T(8,128)S(1)}, f32[3,6,16,128]{3,2,1,0:T(8,128)S(1)}, u32[]{:S(2)}, u32[]{:S(2)}) collective-permute-start(f32[3,6,16,128]{3,2,1,0:T(8,128)S(1)} %get-tuple-element.31), channel_id=1, source_target_pairs={{0,3},{1,2},{2,1},{3,0},{4,7},{5,6},{6,5},{7,4},{8,11},{9,10},{10,... | collective-permute-start | bytes 442376 | tf_op jit(solution)/shard_map/ppermute | solution.py:286
  5.8 7.3 %collective-permute-start.2 = (f32[2,3,2,8,128]{4,3,2,1,0:T(8,128)S(1)}, f32[2,3,2,8,128]{4,3,2,1,0:T(8,128)S(1)}, u32[]{:S(2)}, u32[]{:S(2)}) collective-permute-start(f32[2,3,2,8,128]{4,3,2,1,0:T(8,128)S(1)} %get-tuple-element.38), channel_id=1, source_target_pairs={{0,12},{4,8},{8,4},{12,0},{16,28},{20,24},{24,20},{28,16},{1,13},{... | collective-permute-start | bytes 147464 | tf_op jit(solution)/shard_map/ppermute | solution.py:290
  8.3 5.2 %collective-permute-start.3 = (f32[2,3,2,8,128]{4,3,2,1,0:T(8,128)S(1)}, f32[2,3,2,8,128]{4,3,2,1,0:T(8,128)S(1)}, u32[]{:S(2)}, u32[]{:S(2)}) collective-permute-start(f32[2,3,2,8,128]{4,3,2,1,0:T(8,128)S(1)} %get-tuple-element.39), channel_id=1, source_target_pairs={{0,8},{4,12},{8,0},{12,4},{16,24},{20,28},{24,16},{28,20},{1,9},{5... | collective-permute-start | bytes 147464 | tf_op jit(solution)/shard_map/ppermute | solution.py:290
  8.8 4.8 %collective-permute-start.4 = (f32[2,3,2,8,128]{4,3,2,1,0:T(8,128)S(1)}, f32[2,3,2,8,128]{4,3,2,1,0:T(8,128)S(1)}, u32[]{:S(2)}, u32[]{:S(2)}) collective-permute-start(f32[2,3,2,8,128]{4,3,2,1,0:T(8,128)S(1)} %get-tuple-element.40), channel_id=1, source_target_pairs={{0,4},{4,0},{8,12},{12,8},{16,20},{20,16},{24,28},{28,24},{1,5},{5... | collective-permute-start | bytes 147464 | tf_op jit(solution)/shard_map/ppermute | solution.py:290
  10.0 6.3 %collective-permute-start.5 = (f32[2,3,2,8,128]{4,3,2,1,0:T(8,128)S(1)}, f32[2,3,2,8,128]{4,3,2,1,0:T(8,128)S(1)}, u32[]{:S(2)}, u32[]{:S(2)}) collective-permute-start(f32[2,3,2,8,128]{4,3,2,1,0:T(8,128)S(1)} %get-tuple-element.43), channel_id=1, source_target_pairs={{0,12},{4,8},{8,4},{12,0},{16,28},{20,24},{24,20},{28,16},{1,13},{... | collective-permute-start | bytes 147464 | tf_op jit(solution)/shard_map/ppermute | solution.py:290
  12.6 4.1 %collective-permute-start.6 = (f32[2,3,2,8,128]{4,3,2,1,0:T(8,128)S(1)}, f32[2,3,2,8,128]{4,3,2,1,0:T(8,128)S(1)}, u32[]{:S(2)}, u32[]{:S(2)}) collective-permute-start(f32[2,3,2,8,128]{4,3,2,1,0:T(8,128)S(1)} %get-tuple-element.44), channel_id=1, source_target_pairs={{0,8},{4,12},{8,0},{12,4},{16,24},{20,28},{24,16},{28,20},{1,9},{5... | collective-permute-start | bytes 147464 | tf_op jit(solution)/shard_map/ppermute | solution.py:290
  13.1 4.1 %collective-permute-start.7 = (f32[2,3,2,8,128]{4,3,2,1,0:T(8,128)S(1)}, f32[2,3,2,8,128]{4,3,2,1,0:T(8,128)S(1)}, u32[]{:S(2)}, u32[]{:S(2)}) collective-permute-start(f32[2,3,2,8,128]{4,3,2,1,0:T(8,128)S(1)} %get-tuple-element.45), channel_id=1, source_target_pairs={{0,4},{4,0},{8,12},{12,8},{16,20},{20,16},{24,28},{28,24},{1,5},{5... | collective-permute-start | bytes 147464 | tf_op jit(solution)/shard_map/ppermute | solution.py:290
  13.6 6.2 %collective-permute-start.9 = (f32[2,3,2,8,128]{4,3,2,1,0:T(8,128)S(1)}, f32[2,3,2,8,128]{4,3,2,1,0:T(8,128)S(1)}, u32[]{:S(2)}, u32[]{:S(2)}) collective-permute-start(f32[2,3,2,8,128]{4,3,2,1,0:T(8,128)S(1)} %shard_map.32), channel_id=1, source_target_pairs={{0,16},{4,20},{8,24},{12,28},{16,0},{20,4},{24,8},{28,12},{1,17},{... | collective-permute-start | bytes 147464 | tf_op jit(solution)/shard_map/ppermute | solution.py:296
  17.2 6.3 %collective-permute-start.8 = (f32[2,3,2,8,128]{4,3,2,1,0:T(8,128)S(1)}, f32[2,3,2,8,128]{4,3,2,1,0:T(8,128)S(1)}, u32[]{:S(2)}, u32[]{:S(2)}) collective-permute-start(f32[2,3,2,8,128]{4,3,2,1,0:T(8,128)S(1)} %shard_map.33), channel_id=1, source_target_pairs={{0,16},{4,20},{8,24},{12,28},{16,0},{20,4},{24,8},{28,12},{1,17},{... | collective-permute-start | bytes 147464 | tf_op jit(solution)/shard_map/ppermute | solution.py:296
  19.9 5.9 %collective-permute-start.13 = (f32[2,3,2,8,128]{4,3,2,1,0:T(8,128)S(1)}, f32[2,3,2,8,128]{4,3,2,1,0:T(8,128)S(1)}, u32[]{:S(2)}, u32[]{:S(2)}) collective-permute-start(f32[2,3,2,8,128]{4,3,2,1,0:T(8,128)S(1)} %get-tuple-element.52), channel_id=1, source_target_pairs={{0,12},{4,8},{8,4},{12,0},{16,28},{20,24},{24,20},{28,16},{1,13},{... | collective-permute-start | bytes 147464 | tf_op jit(solution)/shard_map/ppermute | solution.py:290
  21.8 5.3 %collective-permute-start.14 = (f32[2,3,2,8,128]{4,3,2,1,0:T(8,128)S(1)}, f32[2,3,2,8,128]{4,3,2,1,0:T(8,128)S(1)}, u32[]{:S(2)}, u32[]{:S(2)}) collective-permute-start(f32[2,3,2,8,128]{4,3,2,1,0:T(8,128)S(1)} %get-tuple-element.53), channel_id=1, source_target_pairs={{0,8},{4,12},{8,0},{12,4},{16,24},{20,28},{24,16},{28,20},{1,9},{5... | collective-permute-start | bytes 147464 | tf_op jit(solution)/shard_map/ppermute | solution.py:290
  22.2 4.9 %collective-permute-start.15 = (f32[2,3,2,8,128]{4,3,2,1,0:T(8,128)S(1)}, f32[2,3,2,8,128]{4,3,2,1,0:T(8,128)S(1)}, u32[]{:S(2)}, u32[]{:S(2)}) collective-permute-start(f32[2,3,2,8,128]{4,3,2,1,0:T(8,128)S(1)} %get-tuple-element.54), channel_id=1, source_target_pairs={{0,4},{4,0},{8,12},{12,8},{16,20},{20,16},{24,28},{28,24},{1,5},{5... | collective-permute-start | bytes 147464 | tf_op jit(solution)/shard_map/ppermute | solution.py:290
  23.5 5.1 %collective-permute-start.10 = (f32[2,3,2,8,128]{4,3,2,1,0:T(8,128)S(1)}, f32[2,3,2,8,128]{4,3,2,1,0:T(8,128)S(1)}, u32[]{:S(2)}, u32[]{:S(2)}) collective-permute-start(f32[2,3,2,8,128]{4,3,2,1,0:T(8,128)S(1)} %get-tuple-element.49), channel_id=1, source_target_pairs={{0,12},{4,8},{8,4},{12,0},{16,28},{20,24},{24,20},{28,16},{1,13},{... | collective-permute-start | bytes 147464 | tf_op jit(solution)/shard_map/ppermute | solution.py:290
  25.4 4.1 %collective-permute-start.11 = (f32[2,3,2,8,128]{4,3,2,1,0:T(8,128)S(1)}, f32[2,3,2,8,128]{4,3,2,1,0:T(8,128)S(1)}, u32[]{:S(2)}, u32[]{:S(2)}) collective-permute-start(f32[2,3,2,8,128]{4,3,2,1,0:T(8,128)S(1)} %get-tuple-element.50), channel_id=1, source_target_pairs={{0,8},{4,12},{8,0},{12,4},{16,24},{20,28},{24,16},{28,20},{1,9},{5... | collective-permute-start | bytes 147464 | tf_op jit(solution)/shard_map/ppermute | solution.py:290
  25.8 4.1 %collective-permute-start.12 = (f32[2,3,2,8,128]{4,3,2,1,0:T(8,128)S(1)}, f32[2,3,2,8,128]{4,3,2,1,0:T(8,128)S(1)}, u32[]{:S(2)}, u32[]{:S(2)}) collective-permute-start(f32[2,3,2,8,128]{4,3,2,1,0:T(8,128)S(1)} %get-tuple-element.51), channel_id=1, source_target_pairs={{0,4},{4,0},{8,12},{12,8},{16,20},{20,16},{24,28},{28,24},{1,5},{5... | collective-permute-start | bytes 147464 | tf_op jit(solution)/shard_map/ppermute | solution.py:290

commit v2 on v1

--- a/solution.py
+++ b/solution.py
@@ -9,11 +9,13 @@
 
 STEPS = 2
 STAGES = 3 * STEPS
+BUSY = 1 << 32
 GROUP = 4
 VISCOSITY = 0.05
 TIME_STEP = 0.2
 MIX = ((1.0, None), (0.25, 0.75), (2.0 / 3.0, 1.0 / 3.0))
 VMEM = pl.BlockSpec(memory_space=pltpu.VMEM)
+ANY = pl.BlockSpec(memory_space=pl.ANY)
 PARAMS = pltpu.CompilerParams(vmem_limit_bytes=16 * 1024 * 1024)
 
 
@@ -46,6 +48,11 @@
 
 def chunk_of(k):
     return lax.bitwise_xor(spot(), partner(k))
+
+
+def share_of(ref, k, count):
+    chunk = chunk_of(k)
+    return ref[chunk // 2, pl.ds(lax.rem(chunk, 2) * count, count)]
 
 
 def near_side():
@@ -111,11 +118,17 @@
     near_ref[...] = own_ref[:, pl.ds(near * top, width)]
 
 
-def inside_kernel(own_ref, rate_ref, edges, middle, faded, damp_ref, kept, damps, *fields):
+def inside_kernel(own_ref, rate_ref, edges, middle, faded, early_damp, late_damp, kept, damps, inner, *fields):
     layers = own_ref.shape[1]
-    half = layers // 2
+    near = near_side()
     slices = lax.axis_size("tm")
     keep = (lax.axis_index("tm") != 0).astype(jnp.float32)
+
+    def side_of(z):
+        return (0, z) if z < layers - 1 - z else (1, layers - 1 - z)
+
+    def from_near(z):
+        return z - STAGES + near * (layers - 1 - 2 * z)
 
     def save(stage, z, value):
         low, high = z - stage, layers - 1 - stage - z
@@ -125,19 +138,21 @@
             store(edges, (stage, 1, high), value)
 
     for z in range(layers):
-        side, slot = (0, z) if z < half else (1, layers - 1 - z)
+        side, slot = side_of(z)
         damp = [jnp.exp(r * (-1.0 / slices)) for r in split_rows(rate_ref, z)]
         start = [split_rows(own_ref, c, z) for c in range(3)]
         store(fields[0], (z,), start)
-        store(kept, (side, slot), start)
+        store(kept, (z,), start)
         save(0, z, start)
-        for odd in (0, 1):
-            damps[side, slot, odd] = damp[odd]
         lost = [[damp[odd] * keep * start[c][odd] for odd in (0, 1)] for c in range(3)]
         if slot < STAGES:
             store(faded, (side, slot), lost)
+            for odd in (0, 1):
+                damps[side, odd, slot] = damp[odd]
         else:
-            store(middle, (side, slot - STAGES), lost)
+            store(middle, (from_near(z),), lost)
+            for odd in (0, 1):
+                inner[odd, STAGES + from_near(z)] = damp[odd]
 
     for stage in range(1, STAGES + 1):
         kind = (stage - 1) % 3
@@ -153,19 +168,18 @@
                 store(target, (z,), new)
                 save(stage, z, new)
             else:
-                side, slot = (0, z) if z < half else (1, layers - 1 - z)
-                lost = load(middle, side, slot - STAGES)
+                lost = load(middle, from_near(z))
                 store(
                     middle,
-                    (side, slot - STAGES),
+                    (from_near(z),),
                     [[new[c][odd] - lost[c][odd] for odd in (0, 1)] for c in range(3)],
                 )
             below, here = here, above
 
-    share = half // GROUP
-    for far in (0, 1):
-        side = far + (1 - 2 * far) * near_side()
-        damp_ref[far] = damps[side, pl.ds(chunk_of(0) * share, share)]
+    for odd in (0, 1):
+        inner[odd, :STAGES] = damps[near, odd]
+    early_damp[...] = share_of(inner, 0, early_damp.shape[0])
+    late_damp[...] = share_of(damps.at[1 - near], 0, late_damp.shape[0])
 
 
 def border(side, face_ref, edges, middle, faded, jumps, strip):
@@ -194,21 +208,23 @@
         return 0
 
     lax.fori_loop(0, STEPS, step, 0)
-    for slot in range(jumps.shape[0]):
+    for slot in range(jumps.shape[1]):
         if slot < width:
             end, lost = load(strip, STAGES, slot), load(faded, side, slot)
-            store(jumps, (slot,), [[end[c][odd] - lost[c][odd] for odd in (0, 1)] for c in range(3)])
+            jump = [[end[c][odd] - lost[c][odd] for odd in (0, 1)] for c in range(3)]
         else:
-            store(jumps, (slot,), load(middle, side, slot - width))
+            jump = load(middle, slot - width)
+        for odd in (0, 1):
+            for c in range(3):
+                jumps[odd, slot, c] = jump[c][odd]
 
 
 def jumps_kernel(far, face_ref, edges, middle, faded, *refs):
     outs, strip, jumps = refs[:GROUP], refs[-2], refs[-1]
     side = far + (1 - 2 * far) * near_side()
     border(side, face_ref, edges, middle, faded, jumps, strip)
-    share = outs[0].shape[0]
     for k, out in enumerate(outs):
-        out[...] = jumps[pl.ds(chunk_of(k) * share, share)]
+        out[...] = share_of(jumps, k, out.shape[0])
 
 
 def sort_in(jumps, order):
@@ -229,45 +245,52 @@
     return total
 
 
-def total_kernel(far, *refs):
+def total_kernel(*refs):
     jumps, damp_ref, out, order = refs[:GROUP], refs[GROUP], refs[GROUP + 1], refs[GROUP + 2]
     sort_in(jumps, order)
-    out[...] = run(order, damp_ref[far][:, None], jnp.zeros(out.shape, jnp.float32))
-
-
-def spread_kernel(far, *refs):
+    out[...] = run(order, damp_ref[...][:, None], jnp.zeros(out.shape, jnp.float32))
+
+
+def spread_kernel(*refs):
     carry_ref, jumps, damp_ref = refs[0], refs[1 : 1 + GROUP], refs[1 + GROUP]
     outs, order = refs[GROUP + 2 : -1], refs[-1]
     sort_in(jumps, order)
-    run(order, damp_ref[far][:, None], jnp.where(lax.axis_index("tm") < GROUP, 0.0, carry_ref[...]))
+    run(order, damp_ref[...][:, None], jnp.where(lax.axis_index("tm") < GROUP, 0.0, carry_ref[...]))
     sort_out(order, outs)
 
 
-def finish_kernel(kept, *refs):
-    out = refs[-1]
-    layers = out.shape[1]
-    half = layers // 2
-    share = half // GROUP
+def finish_kernel(far, kept, *refs):
+    pieces, (out, part, sem) = refs[:GROUP], refs[-3:]
+    layers, count = out.shape[1], part.shape[1]
+    rows = out.shape[2] // 2
+    down = far + (1 - 2 * far) * near_side()
+    base = down * (layers - count)
     first_slice = lax.axis_index("tm") == 0
-
-    def put(side, slot, layer_of):
-        layer = slot + side * (layers - 1 - 2 * slot)
-        for c in range(3):
-            join_rows(out, (c, layer), layer_of[c])
 
     @pl.when(first_slice)
     def _():
-        for side in (0, 1):
-            for slot in range(half):
-                put(side, slot, load(kept, side, slot))
+        for layer in range(count):
+            pair = load(kept, base + layer)
+            for c in range(3):
+                join_rows(part, (c, layer), pair[c])
 
     @pl.when(jnp.logical_not(first_slice))
     def _():
-        for far in (0, 1):
-            side = far + (1 - 2 * far) * near_side()
-            for k in range(GROUP):
-                for j in range(share):
-                    put(side, chunk_of(k) * share + j, load(refs[(1 - far) * GROUP + k], j))
+        for k, piece in enumerate(pieces):
+            chunk, share = chunk_of(k), piece.shape[0]
+            for odd in (0, 1):
+
+                @pl.when(chunk // 2 == odd)
+                def _():
+                    for j in range(share):
+                        slot = lax.rem(chunk, 2) * share + j
+                        layer = slot + down * (count - 1 - 2 * slot)
+                        for c in range(3):
+                            part[c, layer, pl.ds(odd, rows, stride=2), :] = piece[j, c]
+
+    copy = pltpu.make_async_copy(part, out.at[:, pl.ds(base, count)], sem)
+    copy.start()
+    copy.wait()
 
 
 def shards(states, rate):
@@ -276,10 +299,10 @@
     groups = slices // GROUP
     own = states[0]
     layers, rows, width = own.shape[1:]
-    half, share = layers // 2, layers // 2 // GROUP
+    middle_layers = layers - 2 * STAGES
     tile = (3, 2, rows // 2, width)
     face = f32(3, STAGES, rows, width)
-    piece = f32(share, *tile)
+    sizes = ((layers - STAGES) // 2, STAGES // 2)
     team = lax.axis_index("tm") // GROUP
 
     def halo(value, pairs):
@@ -298,22 +321,27 @@
     far_face, near_face = call(faces_kernel, [face, face], own)
     near_face = halo(near_face, [(i, i ^ 1) for i in range(slabs)])
     far_face = halo(far_face, [(i, i + 1 if i % 2 else i - 1 + slabs) for i in range(slabs)])
-    edges, middle, faded, damp, kept = call(
+    row = (rows // 2, width)
+    edges, middle, faded, *damps, kept = call(
         inside_kernel,
         [
             f32(STAGES, 2, 3, *tile),
-            f32(2, half - STAGES, *tile),
+            f32(middle_layers, *tile),
             f32(2, STAGES, *tile),
-            f32(2, share, *tile[1:]),
-            f32(2, half, *tile),
+            *[f32(size, *row) for size in sizes],
+            f32(layers, *tile),
         ],
         own, rate,
-        scratch=[pltpu.VMEM((2, half, *tile[1:]), jnp.float32)]
+        scratch=[
+            pltpu.VMEM((2, 2, STAGES, *row), jnp.float32),
+            pltpu.VMEM((2, layers - STAGES, *row), jnp.float32),
+        ]
         + [pltpu.VMEM((layers, *tile), jnp.float32)] * 3,
         flops=1 << 26,
     )
     strip = pltpu.VMEM((STAGES + 1, STAGES, *tile), jnp.float32)
-    order = pltpu.VMEM((GROUP, *piece.shape), jnp.float32)
+    shares = [f32(size, 3, *row) for size in sizes]
+    orders = [pltpu.VMEM((GROUP, *share.shape), jnp.float32) for share in shares]
 
     def after(value, earlier):
         return lax.optimization_barrier((value, earlier))[0]
@@ -321,39 +349,53 @@
     halves = []
     for far, face_ref in enumerate((near_face, far_face)):
         jumps = call(
-            functools.partial(jumps_kernel, far), [piece] * GROUP, face_ref, edges, middle, faded,
-            scratch=[strip, pltpu.VMEM((half, *tile), jnp.float32)],
-            flops=1 << 32,
+            functools.partial(jumps_kernel, far), [shares[far]] * GROUP,
+            face_ref, edges, middle, faded,
+            scratch=[strip, pltpu.VMEM((2, 2 * sizes[far], 3, *row), jnp.float32)],
+            flops=BUSY,
         )
         halves.append(swap(jumps))
 
-    carries, total = [], None
+    carries, total = [], halves[1][0]
     for far, jumps in enumerate(halves):
-        if far:
-            jumps[0] = after(jumps[0], total)
+        jumps[0] = after(jumps[0], total)
         total = call(
-            functools.partial(total_kernel, far), piece, *jumps, damp, scratch=[order]
+            total_kernel, shares[far], *jumps, damps[far], scratch=[orders[far]], flops=BUSY
         )
         carry = onward(total, 1)
         if groups > 2:
             carry = jnp.where(team < 1, 0.0, carry)
-            fade, distance = damp[far][:, None] ** GROUP, 1
+            fade, distance = damps[far][:, None] ** GROUP, 1
             while distance < groups - 1:
                 carry = carry + jnp.where(team < distance, 0.0, fade * onward(carry, distance))
                 distance, fade = 2 * distance, fade * fade
         carries.append(carry)
 
-    pieces, news = [], None
+    updated, news = None, None
     for far, (jumps, carry) in enumerate(zip(halves, carries)):
         if far:
             jumps[0] = after(jumps[0], news[0])
         news = call(
-            functools.partial(spread_kernel, far), [piece] * GROUP, carry, *jumps, damp,
-            scratch=[order],
-            flops=1 << 32,
+            spread_kernel, [shares[far]] * GROUP, carry, *jumps, damps[far],
+            scratch=[orders[far]],
+            flops=BUSY,
         )
-        pieces = swap(news) + pieces
-    updated = call(finish_kernel, f32(*own.shape), kept, *pieces)
+        halves[far] = swap(news)
+    for far, pieces in enumerate(halves):
+        args = [kept, *pieces] + ([updated] if far else [])
+        updated = pl.pallas_call(
+            functools.partial(finish_kernel, far),
+            out_shape=f32(*own.shape),
+            in_specs=[VMEM] * (1 + GROUP) + [ANY] * far,
+            out_specs=ANY,
+            scratch_shapes=[
+                pltpu.VMEM((3, 2 * sizes[far], rows, width), jnp.float32),
+                pltpu.SemaphoreType.DMA,
+            ],
+            input_output_aliases={1 + GROUP: 0} if far else {},
+            compiler_params=PARAMS,
+            cost_estimate=pl.CostEstimate(flops=BUSY, bytes_accessed=1 << 20, transcendentals=0),
+        )(*args)
     return updated[None]
 
 

time: 30.8 us -> 30.6 us (level)
  waiting for transfers between devices: 3.69 us -> 2.82 us
  Pallas kernels: 3.24 us -> 3.89 us
    pallas_call x0 -> x2, Pallas kernels: none -> 1.4 us  [shards(): pl.pallas_call(functools.partial(finish_kernel, far), out_shape=f32(*own....]
    ppermute x12, waiting for transfers between devices: 3.68 us -> 2.81 us  [swap(): lax.ppermute(parts[k], 'tm', [(i, i ^ partner(k)) for i in range(slices)])]
    pallas_call x9 -> x8, Pallas kernels: 3.24 us -> 2.48 us  [call(): pl.pallas_call(kernel, out_shape=out_shape, in_specs=[VMEM] * len(args),...]
  transfers between devices with their start and end apart: 16 -> 16, of which waited for: 5 -> 5; matrix products, arithmetic and copies ran while one was open for 0% -> 0% of each run, Pallas kernels for 8% -> 10%
where the time goes in v2:
time: 30.6 us; the launch traced here: 30.5 us
  starting transfers between devices  22.7 us (74%)
  Pallas kernels  3.89 us (13%)
  waiting for transfers between devices  2.82 us (9%)
  local copies, waits for them, and re-layouts  1 us (3%)
    ppermute x12, starting transfers between devices, swap(): lax.ppermute(parts[k], 'tm', [(i, i ^ partner(k)) for i in range(slices)])  14.2 us
    ppermute x2, starting transfers between devices, onward(): lax.ppermute(value, 'tm', [(i, (i + step) % slices) for i in range(slices)])  5.31 us
    ppermute x2, starting transfers between devices, halo(): return lax.ppermute(value, 'gz', [(i, j % slabs) for i, j in pairs])  3.16 us
    ppermute x12, waiting for transfers between devices, swap(): lax.ppermute(parts[k], 'tm', [(i, i ^ partner(k)) for i in range(slices)])  2.81 us
    pallas_call x8, Pallas kernels, call(): pl.pallas_call(kernel, out_shape=out_shape, in_specs=[VMEM] * len(args),...  2.48 us
    pallas_call x2, Pallas kernels, shards(): pl.pallas_call(functools.partial(finish_kernel, far), out_shape=f32(*own....  1.4 us
    unnamed x4, local copies, waits for them, and re-layouts  1 us
  transfers between devices with their start and end apart: 16, of which 5 were waited for; matrix products, arithmetic and copies ran while one was open for 0% of the time, Pallas kernels for 10%

profile of v2, /device:TPU:0, one launch (start us, length us, event | category | flops | bytes accessed | tf_op | source)
XLA Modules:
  0.0 30.5 jit_solution(4157757473626665002)
XLA Ops:
  0.0 1.0 %copy-done = f32[1,3,16,16,128]{4,3,2,1,0:T(8,128)S(1)} copy-done((f32[1,3,16,16,128]{4,3,2,1,0:T(8,128)S(1)}, f32[1,3,16,16,128]{4,3,2,1,0:T(8,128)}, u32[]{:S(2)}) %copy-start) | copy-done | bytes 393240
  1.0 0.5 %collective-permute-start.1 = (f32[3,6,16,128]{3,2,1,0:T(8,128)S(1)}, f32[3,6,16,128]{3,2,1,0:T(8,128)S(1)}, u32[]{:S(2)}, u32[]{:S(2)}) collective-permute-start(f32[3,6,16,128]{3,2,1,0:T(8,128)S(1)} %get-tuple-element.38), channel_id=1, source_target_pairs={{0,1},{1,0},{2,3},{3,2},{4,5},{5,4},{6,7},{7,6},{8,9},{9,8},{10,11... | collective-permute-start | bytes 442376 | tf_op jit(solution)/shard_map/ppermute | solution.py:309
  1.5 2.6 %collective-permute-start = (f32[3,6,16,128]{3,2,1,0:T(8,128)S(1)}, f32[3,6,16,128]{3,2,1,0:T(8,128)S(1)}, u32[]{:S(2)}, u32[]{:S(2)}) collective-permute-start(f32[3,6,16,128]{3,2,1,0:T(8,128)S(1)} %get-tuple-element.33), channel_id=1, source_target_pairs={{0,3},{1,2},{2,1},{3,0},{4,7},{5,6},{6,5},{7,4},{8,11},{9,10},{10,... | collective-permute-start | bytes 442376 | tf_op jit(solution)/shard_map/ppermute | solution.py:309
  4.2 0.8 %shard_map.28 = (f32[6,2,3,3,2,8,128]{6,5,4,3,2,1,0:T(8,128)S(1)}, f32[4,3,2,8,128]{4,3,2,1,0:T(8,128)S(1)}, f32[2,6,3,2,8,128]{5,4,3,2,1,0:T(8,128)S(1)}, f32[5...) custom-call(f32[3,16,16,128]{3,2,1,0:T(8,128)S(1)} %bitcast.3, ...), custom_call_target="tpu_custom_call" | custom-call | flops 67108864 | bytes 1048576 | tf_op jit(solution)/shard_map/pallas_call | solution.py:26
  5.1 0.7 %shard_map.31 = (f32[5,3,8,128]{3,2,1,0:T(8,128)S(1)}, f32[5,3,8,128]{3,2,1,0:T(8,128)S(1)}, f32[5,3,8,128]{3,2,1,0:T(8,128)S(1)}, f32[5,3,8,128]{3,2,1,0:T(8,128)S(1)}) custom-call(f32[3,6,16,128]{3,2,1,0:T(8,128)S(1)} %collective-permute-done.1.face_ref, f32[6,2,3,3,2,8,128]{6,5,4,3,2,1,0:T(8,128)S(1)} %get-tuple-element.34.edges, ...), custom_call_target="tpu_custom_call" | custom-call | flops 4294967296 | bytes 1048576 | tf_op jit(solution)/shard_map/pallas_call | solution.py:26
  5.8 2.6 %collective-permute-start.2 = (f32[5,3,8,128]{3,2,1,0:T(8,128)S(1)}, f32[5,3,8,128]{3,2,1,0:T(8,128)S(1)}, u32[]{:S(2)}, u32[]{:S(2)}) collective-permute-start(f32[5,3,8,128]{3,2,1,0:T(8,128)S(1)} %get-tuple-element.41), channel_id=1, source_target_pairs={{0,12},{4,8},{8,4},{12,0},{16,28},{20,24},{24,20},{28,16},{1,13},{... | collective-permute-start | bytes 184328 | tf_op jit(solution)/shard_map/ppermute | solution.py:313
  8.4 0.4 %collective-permute-start.3 = (f32[5,3,8,128]{3,2,1,0:T(8,128)S(1)}, f32[5,3,8,128]{3,2,1,0:T(8,128)S(1)}, u32[]{:S(2)}, u32[]{:S(2)}) collective-permute-start(f32[5,3,8,128]{3,2,1,0:T(8,128)S(1)} %get-tuple-element.42), channel_id=1, source_target_pairs={{0,8},{4,12},{8,0},{12,4},{16,24},{20,28},{24,16},{28,20},{1,9},{5... | collective-permute-start | bytes 184328 | tf_op jit(solution)/shard_map/ppermute | solution.py:313
  8.8 0.5 %collective-permute-start.4 = (f32[5,3,8,128]{3,2,1,0:T(8,128)S(1)}, f32[5,3,8,128]{3,2,1,0:T(8,128)S(1)}, u32[]{:S(2)}, u32[]{:S(2)}) collective-permute-start(f32[5,3,8,128]{3,2,1,0:T(8,128)S(1)} %get-tuple-element.43), channel_id=1, source_target_pairs={{0,4},{4,0},{8,12},{12,8},{16,20},{20,16},{24,28},{28,24},{1,5},{5... | collective-permute-start | bytes 184328 | tf_op jit(solution)/shard_map/ppermute | solution.py:313
  9.3 0.0 collective-permute-done.face_ref
  9.3 0.7 %shard_map.30 = (f32[3,3,8,128]{3,2,1,0:T(8,128)S(1)}, f32[3,3,8,128]{3,2,1,0:T(8,128)S(1)}, f32[3,3,8,128]{3,2,1,0:T(8,128)S(1)}, f32[3,3,8,128]{3,2,1,0:T(8,128)S(1)}) custom-call(f32[3,6,16,128]{3,2,1,0:T(8,128)S(1)} %collective-permute-done.face_ref, f32[6,2,3,3,2,8,128]{6,5,4,3,2,1,0:T(8,128)S(1)} %get-tuple-element.34.edges, ...), custom_call_target="tpu_custom_call" | custom-call | flops 4294967296 | bytes 1048576 | tf_op jit(solution)/shard_map/pallas_call | solution.py:26
  10.0 2.6 %collective-permute-start.5 = (f32[3,3,8,128]{3,2,1,0:T(8,128)S(1)}, f32[3,3,8,128]{3,2,1,0:T(8,128)S(1)}, u32[]{:S(2)}, u32[]{:S(2)}) collective-permute-start(f32[3,3,8,128]{3,2,1,0:T(8,128)S(1)} %get-tuple-element.46), channel_id=1, source_target_pairs={{0,12},{4,8},{8,4},{12,0},{16,28},{20,24},{24,20},{28,16},{1,13},{... | collective-permute-start | bytes 110600 | tf_op jit(solution)/shard_map/ppermute | solution.py:313
  12.6 0.4 %collective-permute-start.6 = (f32[3,3,8,128]{3,2,1,0:T(8,128)S(1)}, f32[3,3,8,128]{3,2,1,0:T(8,128)S(1)}, u32[]{:S(2)}, u32[]{:S(2)}) collective-permute-start(f32[3,3,8,128]{3,2,1,0:T(8,128)S(1)} %get-tuple-element.47), channel_id=1, source_target_pairs={{0,8},{4,12},{8,0},{12,4},{16,24},{20,28},{24,16},{28,20},{1,9},{5... | collective-permute-start | bytes 110600 | tf_op jit(solution)/shard_map/ppermute | solution.py:313
  13.1 0.0 collective-permute-done.2.refs_1_.refs_2_
  13.1 0.5 %collective-permute-start.7 = (f32[3,3,8,128]{3,2,1,0:T(8,128)S(1)}, f32[3,3,8,128]{3,2,1,0:T(8,128)S(1)}, u32[]{:S(2)}, u32[]{:S(2)}) collective-permute-start(f32[3,3,8,128]{3,2,1,0:T(8,128)S(1)} %get-tuple-element.48), channel_id=1, source_target_pairs={{0,4},{4,0},{8,12},{12,8},{16,20},{20,16},{24,28},{28,24},{1,5},{5... | collective-permute-start | bytes 110600 | tf_op jit(solution)/shard_map/ppermute | solution.py:313
  13.6 0.0 collective-permute-done.3.refs_2_.refs_3_
  13.6 0.1 shard_map.32
  13.7 2.7 %collective-permute-start.9 = (f32[5,3,8,128]{3,2,1,0:T(8,128)S(1)}, f32[5,3,8,128]{3,2,1,0:T(8,128)S(1)}, u32[]{:S(2)}, u32[]{:S(2)}) collective-permute-start(f32[5,3,8,128]{3,2,1,0:T(8,128)S(1)} %shard_map.32), channel_id=1, source_target_pairs={{0,16},{4,20},{8,24},{12,28},{16,0},{20,4},{24,8},{28,12},{1,17},{... | collective-permute-start | bytes 184328 | tf_op jit(solution)/shard_map/ppermute | solution.py:319
  16.3 0.3 %collective-permute-done.6.refs_2_.refs_3_ = f32[3,3,8,128]{3,2,1,0:T(8,128)S(1)} collective-permute-done((f32[3,3,8,128]{3,2,1,0:T(8,128)S(1)}, f32[3,3,8,128]{3,2,1,0:T(8,128)S(1)}, u32[]{:S(2)}, u32[]{:S(2)}) %collective-permute-start.6) | collective-permute-done | bytes 36896 | tf_op jit(solution)/shard_map/ppermute | solution.py:313
  16.7 0.4 %collective-permute-done.7.refs_3_.refs_4_ = f32[3,3,8,128]{3,2,1,0:T(8,128)S(1)} collective-permute-done((f32[3,3,8,128]{3,2,1,0:T(8,128)S(1)}, f32[3,3,8,128]{3,2,1,0:T(8,128)S(1)}, u32[]{:S(2)}, u32[]{:S(2)}) %collective-permute-start.7) | collective-permute-done | bytes 36896 | tf_op jit(solution)/shard_map/ppermute | solution.py:313
  17.1 2.7 %collective-permute-start.8 = (f32[3,3,8,128]{3,2,1,0:T(8,128)S(1)}, f32[3,3,8,128]{3,2,1,0:T(8,128)S(1)}, u32[]{:S(2)}, u32[]{:S(2)}) collective-permute-start(f32[3,3,8,128]{3,2,1,0:T(8,128)S(1)} %shard_map.33), channel_id=1, source_target_pairs={{0,16},{4,20},{8,24},{12,28},{16,0},{20,4},{24,8},{28,12},{1,17},{... | collective-permute-start | bytes 110600 | tf_op jit(solution)/shard_map/ppermute | solution.py:319
  19.7 0.1 shard_map.34
  19.8 2.0 %collective-permute-start.13 = (f32[5,3,8,128]{3,2,1,0:T(8,128)S(1)}, f32[5,3,8,128]{3,2,1,0:T(8,128)S(1)}, u32[]{:S(2)}, u32[]{:S(2)}) collective-permute-start(f32[5,3,8,128]{3,2,1,0:T(8,128)S(1)} %get-tuple-element.56), channel_id=1, source_target_pairs={{0,12},{4,8},{8,4},{12,0},{16,28},{20,24},{24,20},{28,16},{1,13},{... | collective-permute-start | bytes 184328 | tf_op jit(solution)/shard_map/ppermute | solution.py:313
  21.8 0.4 %collective-permute-start.14 = (f32[5,3,8,128]{3,2,1,0:T(8,128)S(1)}, f32[5,3,8,128]{3,2,1,0:T(8,128)S(1)}, u32[]{:S(2)}, u32[]{:S(2)}) collective-permute-start(f32[5,3,8,128]{3,2,1,0:T(8,128)S(1)} %get-tuple-element.57), channel_id=1, source_target_pairs={{0,8},{4,12},{8,0},{12,4},{16,24},{20,28},{24,16},{28,20},{1,9},{5... | collective-permute-start | bytes 184328 | tf_op jit(solution)/shard_map/ppermute | solution.py:313
  22.2 1.1 %collective-permute-start.15 = (f32[5,3,8,128]{3,2,1,0:T(8,128)S(1)}, f32[5,3,8,128]{3,2,1,0:T(8,128)S(1)}, u32[]{:S(2)}, u32[]{:S(2)}) collective-permute-start(f32[5,3,8,128]{3,2,1,0:T(8,128)S(1)} %get-tuple-element.58), channel_id=1, source_target_pairs={{0,4},{4,0},{8,12},{12,8},{16,20},{20,16},{24,28},{28,24},{1,5},{5... | collective-permute-start | bytes 184328 | tf_op jit(solution)/shard_map/ppermute | solution.py:313
  23.4 2.0 %collective-permute-start.10 = (f32[3,3,8,128]{3,2,1,0:T(8,128)S(1)}, f32[3,3,8,128]{3,2,1,0:T(8,128)S(1)}, u32[]{:S(2)}, u32[]{:S(2)}) collective-permute-start(f32[3,3,8,128]{3,2,1,0:T(8,128)S(1)} %get-tuple-element.53), channel_id=1, source_target_pairs={{0,12},{4,8},{8,4},{12,0},{16,28},{20,24},{24,20},{28,16},{1,13},{... | collective-permute-start | bytes 110600 | tf_op jit(solution)/shard_map/ppermute | solution.py:313
  25.4 0.4 %collective-permute-start.11 = (f32[3,3,8,128]{3,2,1,0:T(8,128)S(1)}, f32[3,3,8,128]{3,2,1,0:T(8,128)S(1)}, u32[]{:S(2)}, u32[]{:S(2)}) collective-permute-start(f32[3,3,8,128]{3,2,1,0:T(8,128)S(1)} %get-tuple-element.54), channel_id=1, source_target_pairs={{0,8},{4,12},{8,0},{12,4},{16,24},{20,28},{24,16},{28,20},{1,9},{5... | collective-permute-start | bytes 110600 | tf_op jit(solution)/shard_map/ppermute | solution.py:313
  25.8 1.1 %collective-permute-start.12 = (f32[3,3,8,128]{3,2,1,0:T(8,128)S(1)}, f32[3,3,8,128]{3,2,1,0:T(8,128)S(1)}, u32[]{:S(2)}, u32[]{:S(2)}) collective-permute-start(f32[3,3,8,128]{3,2,1,0:T(8,128)S(1)} %get-tuple-element.55), channel_id=1, source_target_pairs={{0,4},{4,0},{8,12},{12,8},{16,20},{20,16},{24,28},{28,24},{1,5},{5... | collective-permute-start | bytes 110600 | tf_op jit(solution)/shard_map/ppermute | solution.py:313
  27.0 0.7 %shard_map.36.refs_4_ = f32[3,16,16,128]{3,2,1,0:T(8,128)} custom-call(f32[16,3,2,8,128]{4,3,2,1,0:T(8,128)S(1)} %get-tuple-element.32.kept, f32[5,3,8,128]{3,2,1,0:T(8,128)S(1)} %get-tuple-element.50.refs_0_, f32[5,3,8,128]{3,2,1,0:T(8,128)S(1)} %collective-permute-done.13.refs_1_, f32[5,3,8,128]{3,2,1,0:T(8,128)S(1)} %collective-permute-done.14.refs_2_, ...), custom_call_target="tpu_custom_call" | custom-call | flops 4294967296 | bytes 1048576 | tf_op jit(solution)/shard_map/pallas_call | solution.py:386
  27.7 0.6 %collective-permute-done.10.refs_1_ = f32[3,3,8,128]{3,2,1,0:T(8,128)S(1)} collective-permute-done((f32[3,3,8,128]{3,2,1,0:T(8,128)S(1)}, f32[3,3,8,128]{3,2,1,0:T(8,128)S(1)}, u32[]{:S(2)}, u32[]{:S(2)}) %collective-permute-start.10) | collective-permute-done | bytes 36896 | tf_op jit(solution)/shard_map/ppermute | solution.py:313
  28.3 1.0 %collective-permute-done.11.refs_2_ = f32[3,3,8,128]{3,2,1,0:T(8,128)S(1)} collective-permute-done((f32[3,3,8,128]{3,2,1,0:T(8,128)S(1)}, f32[3,3,8,128]{3,2,1,0:T(8,128)S(1)}, u32[]{:S(2)}, u32[]{:S(2)}) %collective-permute-start.11) | collective-permute-done | bytes 36896 | tf_op jit(solution)/shard_map/ppermute | solution.py:313
  29.4 0.4 %collective-permute-done.12.refs_3_ = f32[3,3,8,128]{3,2,1,0:T(8,128)S(1)} collective-permute-done((f32[3,3,8,128]{3,2,1,0:T(8,128)S(1)}, f32[3,3,8,128]{3,2,1,0:T(8,128)S(1)}, u32[]{:S(2)}, u32[]{:S(2)}) %collective-permute-start.12) | collective-permute-done | bytes 36896 | tf_op jit(solution)/shard_map/ppermute | solution.py:313
  29.8 0.7 %shard_map.37 = f32[3,16,16,128]{3,2,1,0:T(8,128)} custom-call(f32[16,3,2,8,128]{4,3,2,1,0:T(8,128)S(1)} %get-tuple-element.32.kept, f32[3,3,8,128]{3,2,1,0:T(8,128)S(1)} %get-tuple-element.52.refs_0_, f32[3,3,8,128]{3,2,1,0:T(8,128)S(1)} %collective-permute-done.10.refs_1_, ...), custom_call_target="tpu_custom_call", output_to_operand_aliasing={{}: (5, {})} | custom-call | flops 4294967296 | bytes 1048576 | tf_op jit(solution)/shard_map/pallas_call | solution.py:386
  (14 shorter events, 0.1 us)
Async XLA Ops:
  0.0 1.0 %copy-start = (f32[1,3,16,16,128]{4,3,2,1,0:T(8,128)S(1)}, f32[1,3,16,16,128]{4,3,2,1,0:T(8,128)}, u32[]{:S(2)}) copy-start(f32[1,3,16,16,128]{4,3,2,1,0:T(8,128)} %param.2) | copy-start | bytes 1179652
  1.0 3.2 %copy-start.1 = (f32[16,16,128]{2,1,0:T(8,128)S(1)}, f32[16,16,128]{2,1,0:T(8,128)}, u32[]{:S(2)}) copy-start(f32[16,16,128]{2,1,0:T(8,128)} %rate_ref.1) | copy-start | bytes 393220
  1.0 4.0 %collective-permute-start.1 = (f32[3,6,16,128]{3,2,1,0:T(8,128)S(1)}, f32[3,6,16,128]{3,2,1,0:T(8,128)S(1)}, u32[]{:S(2)}, u32[]{:S(2)}) collective-permute-start(f32[3,6,16,128]{3,2,1,0:T(8,128)S(1)} %get-tuple-element.38), channel_id=1, source_target_pairs={{0,1},{1,0},{2,3},{3,2},{4,5},{5,4},{6,7},{7,6},{8,9},{9,8},{10,11... | collective-permute-start | bytes 442376 | tf_op jit(solution)/shard_map/ppermute | solution.py:309
  1.5 7.8 %collective-permute-start = (f32[3,6,16,128]{3,2,1,0:T(8,128)S(1)}, f32[3,6,16,128]{3,2,1,0:T(8,128)S(1)}, u32[]{:S(2)}, u32[]{:S(2)}) collective-permute-start(f32[3,6,16,128]{3,2,1,0:T(8,128)S(1)} %get-tuple-element.33), channel_id=1, source_target_pairs={{0,3},{1,2},{2,1},{3,0},{4,7},{5,6},{6,5},{7,4},{8,11},{9,10},{10,... | collective-permute-start | bytes 442376 | tf_op jit(solution)/shard_map/ppermute | solution.py:309
  5.8 7.3 %collective-permute-start.2 = (f32[5,3,8,128]{3,2,1,0:T(8,128)S(1)}, f32[5,3,8,128]{3,2,1,0:T(8,128)S(1)}, u32[]{:S(2)}, u32[]{:S(2)}) collective-permute-start(f32[5,3,8,128]{3,2,1,0:T(8,128)S(1)} %get-tuple-element.41), channel_id=1, source_target_pairs={{0,12},{4,8},{8,4},{12,0},{16,28},{20,24},{24,20},{28,16},{1,13},{... | collective-permute-start | bytes 184328 | tf_op jit(solution)/shard_map/ppermute | solution.py:313
  8.4 5.3 %collective-permute-start.3 = (f32[5,3,8,128]{3,2,1,0:T(8,128)S(1)}, f32[5,3,8,128]{3,2,1,0:T(8,128)S(1)}, u32[]{:S(2)}, u32[]{:S(2)}) collective-permute-start(f32[5,3,8,128]{3,2,1,0:T(8,128)S(1)} %get-tuple-element.42), channel_id=1, source_target_pairs={{0,8},{4,12},{8,0},{12,4},{16,24},{20,28},{24,16},{28,20},{1,9},{5... | collective-permute-start | bytes 184328 | tf_op jit(solution)/shard_map/ppermute | solution.py:313
  8.8 4.8 %collective-permute-start.4 = (f32[5,3,8,128]{3,2,1,0:T(8,128)S(1)}, f32[5,3,8,128]{3,2,1,0:T(8,128)S(1)}, u32[]{:S(2)}, u32[]{:S(2)}) collective-permute-start(f32[5,3,8,128]{3,2,1,0:T(8,128)S(1)} %get-tuple-element.43), channel_id=1, source_target_pairs={{0,4},{4,0},{8,12},{12,8},{16,20},{20,16},{24,28},{28,24},{1,5},{5... | collective-permute-start | bytes 184328 | tf_op jit(solution)/shard_map/ppermute | solution.py:313
  10.0 6.3 %collective-permute-start.5 = (f32[3,3,8,128]{3,2,1,0:T(8,128)S(1)}, f32[3,3,8,128]{3,2,1,0:T(8,128)S(1)}, u32[]{:S(2)}, u32[]{:S(2)}) collective-permute-start(f32[3,3,8,128]{3,2,1,0:T(8,128)S(1)} %get-tuple-element.46), channel_id=1, source_target_pairs={{0,12},{4,8},{8,4},{12,0},{16,28},{20,24},{24,20},{28,16},{1,13},{... | collective-permute-start | bytes 110600 | tf_op jit(solution)/shard_map/ppermute | solution.py:313
  12.6 4.0 %collective-permute-start.6 = (f32[3,3,8,128]{3,2,1,0:T(8,128)S(1)}, f32[3,3,8,128]{3,2,1,0:T(8,128)S(1)}, u32[]{:S(2)}, u32[]{:S(2)}) collective-permute-start(f32[3,3,8,128]{3,2,1,0:T(8,128)S(1)} %get-tuple-element.47), channel_id=1, source_target_pairs={{0,8},{4,12},{8,0},{12,4},{16,24},{20,28},{24,16},{28,20},{1,9},{5... | collective-permute-start | bytes 110600 | tf_op jit(solution)/shard_map/ppermute | solution.py:313
  13.1 4.0 %collective-permute-start.7 = (f32[3,3,8,128]{3,2,1,0:T(8,128)S(1)}, f32[3,3,8,128]{3,2,1,0:T(8,128)S(1)}, u32[]{:S(2)}, u32[]{:S(2)}) collective-permute-start(f32[3,3,8,128]{3,2,1,0:T(8,128)S(1)} %get-tuple-element.48), channel_id=1, source_target_pairs={{0,4},{4,0},{8,12},{12,8},{16,20},{20,16},{24,28},{28,24},{1,5},{5... | collective-permute-start | bytes 110600 | tf_op jit(solution)/shard_map/ppermute | solution.py:313
  13.7 6.1 %collective-permute-start.9 = (f32[5,3,8,128]{3,2,1,0:T(8,128)S(1)}, f32[5,3,8,128]{3,2,1,0:T(8,128)S(1)}, u32[]{:S(2)}, u32[]{:S(2)}) collective-permute-start(f32[5,3,8,128]{3,2,1,0:T(8,128)S(1)} %shard_map.32), channel_id=1, source_target_pairs={{0,16},{4,20},{8,24},{12,28},{16,0},{20,4},{24,8},{28,12},{1,17},{... | collective-permute-start | bytes 184328 | tf_op jit(solution)/shard_map/ppermute | solution.py:319
  17.1 6.3 %collective-permute-start.8 = (f32[3,3,8,128]{3,2,1,0:T(8,128)S(1)}, f32[3,3,8,128]{3,2,1,0:T(8,128)S(1)}, u32[]{:S(2)}, u32[]{:S(2)}) collective-permute-start(f32[3,3,8,128]{3,2,1,0:T(8,128)S(1)} %shard_map.33), channel_id=1, source_target_pairs={{0,16},{4,20},{8,24},{12,28},{16,0},{20,4},{24,8},{28,12},{1,17},{... | collective-permute-start | bytes 110600 | tf_op jit(solution)/shard_map/ppermute | solution.py:319
  19.8 6.0 %collective-permute-start.13 = (f32[5,3,8,128]{3,2,1,0:T(8,128)S(1)}, f32[5,3,8,128]{3,2,1,0:T(8,128)S(1)}, u32[]{:S(2)}, u32[]{:S(2)}) collective-permute-start(f32[5,3,8,128]{3,2,1,0:T(8,128)S(1)} %get-tuple-element.56), channel_id=1, source_target_pairs={{0,12},{4,8},{8,4},{12,0},{16,28},{20,24},{24,20},{28,16},{1,13},{... | collective-permute-start | bytes 184328 | tf_op jit(solution)/shard_map/ppermute | solution.py:313
  21.8 5.2 %collective-permute-start.14 = (f32[5,3,8,128]{3,2,1,0:T(8,128)S(1)}, f32[5,3,8,128]{3,2,1,0:T(8,128)S(1)}, u32[]{:S(2)}, u32[]{:S(2)}) collective-permute-start(f32[5,3,8,128]{3,2,1,0:T(8,128)S(1)} %get-tuple-element.57), channel_id=1, source_target_pairs={{0,8},{4,12},{8,0},{12,4},{16,24},{20,28},{24,16},{28,20},{1,9},{5... | collective-permute-start | bytes 184328 | tf_op jit(solution)/shard_map/ppermute | solution.py:313
  22.2 4.7 %collective-permute-start.15 = (f32[5,3,8,128]{3,2,1,0:T(8,128)S(1)}, f32[5,3,8,128]{3,2,1,0:T(8,128)S(1)}, u32[]{:S(2)}, u32[]{:S(2)}) collective-permute-start(f32[5,3,8,128]{3,2,1,0:T(8,128)S(1)} %get-tuple-element.58), channel_id=1, source_target_pairs={{0,4},{4,0},{8,12},{12,8},{16,20},{20,16},{24,28},{28,24},{1,5},{5... | collective-permute-start | bytes 184328 | tf_op jit(solution)/shard_map/ppermute | solution.py:313
  23.4 4.9 %collective-permute-start.10 = (f32[3,3,8,128]{3,2,1,0:T(8,128)S(1)}, f32[3,3,8,128]{3,2,1,0:T(8,128)S(1)}, u32[]{:S(2)}, u32[]{:S(2)}) collective-permute-start(f32[3,3,8,128]{3,2,1,0:T(8,128)S(1)} %get-tuple-element.53), channel_id=1, source_target_pairs={{0,12},{4,8},{8,4},{12,0},{16,28},{20,24},{24,20},{28,16},{1,13},{... | collective-permute-start | bytes 110600 | tf_op jit(solution)/shard_map/ppermute | solution.py:313
  25.4 4.0 %collective-permute-start.11 = (f32[3,3,8,128]{3,2,1,0:T(8,128)S(1)}, f32[3,3,8,128]{3,2,1,0:T(8,128)S(1)}, u32[]{:S(2)}, u32[]{:S(2)}) collective-permute-start(f32[3,3,8,128]{3,2,1,0:T(8,128)S(1)} %get-tuple-element.54), channel_id=1, source_target_pairs={{0,8},{4,12},{8,0},{12,4},{16,24},{20,28},{24,16},{28,20},{1,9},{5... | collective-permute-start | bytes 110600 | tf_op jit(solution)/shard_map/ppermute | solution.py:313
  25.8 4.0 %collective-permute-start.12 = (f32[3,3,8,128]{3,2,1,0:T(8,128)S(1)}, f32[3,3,8,128]{3,2,1,0:T(8,128)S(1)}, u32[]{:S(2)}, u32[]{:S(2)}) collective-permute-start(f32[3,3,8,128]{3,2,1,0:T(8,128)S(1)} %get-tuple-element.55), channel_id=1, source_target_pairs={{0,4},{4,0},{8,12},{12,8},{16,20},{20,16},{24,28},{28,24},{1,5},{5... | collective-permute-start | bytes 110600 | tf_op jit(solution)/shard_map/ppermute | solution.py:313

commit v3 on v2

--- a/solution.py
+++ b/solution.py
@@ -261,23 +261,31 @@
 
 def finish_kernel(far, kept, *refs):
     pieces, (out, part, sem) = refs[:GROUP], refs[-3:]
-    layers, count = out.shape[1], part.shape[1]
-    rows = out.shape[2] // 2
+    layers, rows = out.shape[1], out.shape[2] // 2
+    share = pieces[0].shape[0]
+    count = 2 * share
     down = far + (1 - 2 * far) * near_side()
-    base = down * (layers - count)
     first_slice = lax.axis_index("tm") == 0
 
-    @pl.when(first_slice)
-    def _():
-        for layer in range(count):
-            pair = load(kept, base + layer)
-            for c in range(3):
-                join_rows(part, (c, layer), pair[c])
+    def write(base, count):
+        copy = pltpu.make_async_copy(part.at[:, pl.ds(0, count)], out.at[:, pl.ds(base, count)], sem)
+        copy.start()
+        copy.wait()
+
+    if not far:
+
+        @pl.when(first_slice)
+        def _():
+            for layer in range(layers):
+                pair = load(kept, layer)
+                for c in range(3):
+                    join_rows(part, (c, layer), pair[c])
+            write(0, layers)
 
     @pl.when(jnp.logical_not(first_slice))
     def _():
         for k, piece in enumerate(pieces):
-            chunk, share = chunk_of(k), piece.shape[0]
+            chunk = chunk_of(k)
             for odd in (0, 1):
 
                 @pl.when(chunk // 2 == odd)
@@ -287,10 +295,7 @@
                         layer = slot + down * (count - 1 - 2 * slot)
                         for c in range(3):
                             part[c, layer, pl.ds(odd, rows, stride=2), :] = piece[j, c]
-
-    copy = pltpu.make_async_copy(part, out.at[:, pl.ds(base, count)], sem)
-    copy.start()
-    copy.wait()
+        write(down * (layers - count), count)
 
 
 def shards(states, rate):
@@ -389,7 +394,7 @@
             in_specs=[VMEM] * (1 + GROUP) + [ANY] * far,
             out_specs=ANY,
             scratch_shapes=[
-                pltpu.VMEM((3, 2 * sizes[far], rows, width), jnp.float32),
+                pltpu.VMEM((3, 2 * sizes[far] if far else layers, rows, width), jnp.float32),
                 pltpu.SemaphoreType.DMA,
             ],
             input_output_aliases={1 + GROUP: 0} if far else {},

time: 30.6 us -> 29.9 us (0.977)
  Pallas kernels: 3.89 us -> 3.27 us
    pallas_call x2, Pallas kernels: 1.4 us -> 0.79 us  [shards(): pl.pallas_call(functools.partial(finish_kernel, far), out_shape=f32(*own....]
  transfers between devices with their start and end apart: 16 -> 16, of which waited for: 5 -> 5; matrix products, arithmetic and copies ran while one was open for 0% -> 0% of each run, Pallas kernels for 10% -> 11%
where the time goes in v3:
time: 29.9 us; the launch traced here: 29.8 us
  starting transfers between devices  22.7 us (76%)
  Pallas kernels  3.27 us (11%)
  waiting for transfers between devices  2.76 us (9%)
  local copies, waits for them, and re-layouts  1 us (3%)
    ppermute x12, starting transfers between devices, swap(): lax.ppermute(parts[k], 'tm', [(i, i ^ partner(k)) for i in range(slices)])  14.2 us
    ppermute x2, starting transfers between devices, onward(): lax.ppermute(value, 'tm', [(i, (i + step) % slices) for i in range(slices)])  5.31 us
    ppermute x2, starting transfers between devices, halo(): return lax.ppermute(value, 'gz', [(i, j % slabs) for i, j in pairs])  3.16 us
    ppermute x12, waiting for transfers between devices, swap(): lax.ppermute(parts[k], 'tm', [(i, i ^ partner(k)) for i in range(slices)])  2.75 us
    pallas_call x8, Pallas kernels, call(): pl.pallas_call(kernel, out_shape=out_shape, in_specs=[VMEM] * len(args),...  2.48 us
    unnamed x4, local copies, waits for them, and re-layouts  1 us
    pallas_call x2, Pallas kernels, shards(): pl.pallas_call(functools.partial(finish_kernel, far), out_shape=f32(*own....  0.79 us
  transfers between devices with their start and end apart: 16, of which 5 were waited for; matrix products, arithmetic and copies ran while one was open for 0% of the time, Pallas kernels for 11%

profile of v3, /device:TPU:0, one launch (start us, length us, event | category | flops | bytes accessed | tf_op | source)
XLA Modules:
  0.0 29.8 jit_solution(16353487426709634840)
XLA Ops:
  0.0 1.0 %copy-done = f32[1,3,16,16,128]{4,3,2,1,0:T(8,128)S(1)} copy-done((f32[1,3,16,16,128]{4,3,2,1,0:T(8,128)S(1)}, f32[1,3,16,16,128]{4,3,2,1,0:T(8,128)}, u32[]{:S(2)}) %copy-start) | copy-done | bytes 393240
  1.0 0.5 %collective-permute-start.1 = (f32[3,6,16,128]{3,2,1,0:T(8,128)S(1)}, f32[3,6,16,128]{3,2,1,0:T(8,128)S(1)}, u32[]{:S(2)}, u32[]{:S(2)}) collective-permute-start(f32[3,6,16,128]{3,2,1,0:T(8,128)S(1)} %get-tuple-element.38), channel_id=1, source_target_pairs={{0,1},{1,0},{2,3},{3,2},{4,5},{5,4},{6,7},{7,6},{8,9},{9,8},{10,11... | collective-permute-start | bytes 442376 | tf_op jit(solution)/shard_map/ppermute | solution.py:314
  1.5 2.6 %collective-permute-start = (f32[3,6,16,128]{3,2,1,0:T(8,128)S(1)}, f32[3,6,16,128]{3,2,1,0:T(8,128)S(1)}, u32[]{:S(2)}, u32[]{:S(2)}) collective-permute-start(f32[3,6,16,128]{3,2,1,0:T(8,128)S(1)} %get-tuple-element.33), channel_id=1, source_target_pairs={{0,3},{1,2},{2,1},{3,0},{4,7},{5,6},{6,5},{7,4},{8,11},{9,10},{10,... | collective-permute-start | bytes 442376 | tf_op jit(solution)/shard_map/ppermute | solution.py:314
  4.2 0.8 %shard_map.28 = (f32[6,2,3,3,2,8,128]{6,5,4,3,2,1,0:T(8,128)S(1)}, f32[4,3,2,8,128]{4,3,2,1,0:T(8,128)S(1)}, f32[2,6,3,2,8,128]{5,4,3,2,1,0:T(8,128)S(1)}, f32[5...) custom-call(f32[3,16,16,128]{3,2,1,0:T(8,128)S(1)} %bitcast.3, ...), custom_call_target="tpu_custom_call" | custom-call | flops 67108864 | bytes 1048576 | tf_op jit(solution)/shard_map/pallas_call | solution.py:26
  5.0 0.0 collective-permute-done.1.face_ref
  5.1 0.7 %shard_map.31 = (f32[5,3,8,128]{3,2,1,0:T(8,128)S(1)}, f32[5,3,8,128]{3,2,1,0:T(8,128)S(1)}, f32[5,3,8,128]{3,2,1,0:T(8,128)S(1)}, f32[5,3,8,128]{3,2,1,0:T(8,128)S(1)}) custom-call(f32[3,6,16,128]{3,2,1,0:T(8,128)S(1)} %collective-permute-done.1.face_ref, f32[6,2,3,3,2,8,128]{6,5,4,3,2,1,0:T(8,128)S(1)} %get-tuple-element.34.edges, ...), custom_call_target="tpu_custom_call" | custom-call | flops 4294967296 | bytes 1048576 | tf_op jit(solution)/shard_map/pallas_call | solution.py:26
  5.8 2.6 %collective-permute-start.2 = (f32[5,3,8,128]{3,2,1,0:T(8,128)S(1)}, f32[5,3,8,128]{3,2,1,0:T(8,128)S(1)}, u32[]{:S(2)}, u32[]{:S(2)}) collective-permute-start(f32[5,3,8,128]{3,2,1,0:T(8,128)S(1)} %get-tuple-element.41), channel_id=1, source_target_pairs={{0,12},{4,8},{8,4},{12,0},{16,28},{20,24},{24,20},{28,16},{1,13},{... | collective-permute-start | bytes 184328 | tf_op jit(solution)/shard_map/ppermute | solution.py:318
  8.4 0.4 %collective-permute-start.3 = (f32[5,3,8,128]{3,2,1,0:T(8,128)S(1)}, f32[5,3,8,128]{3,2,1,0:T(8,128)S(1)}, u32[]{:S(2)}, u32[]{:S(2)}) collective-permute-start(f32[5,3,8,128]{3,2,1,0:T(8,128)S(1)} %get-tuple-element.42), channel_id=1, source_target_pairs={{0,8},{4,12},{8,0},{12,4},{16,24},{20,28},{24,16},{28,20},{1,9},{5... | collective-permute-start | bytes 184328 | tf_op jit(solution)/shard_map/ppermute | solution.py:318
  8.8 0.5 %collective-permute-start.4 = (f32[5,3,8,128]{3,2,1,0:T(8,128)S(1)}, f32[5,3,8,128]{3,2,1,0:T(8,128)S(1)}, u32[]{:S(2)}, u32[]{:S(2)}) collective-permute-start(f32[5,3,8,128]{3,2,1,0:T(8,128)S(1)} %get-tuple-element.43), channel_id=1, source_target_pairs={{0,4},{4,0},{8,12},{12,8},{16,20},{20,16},{24,28},{28,24},{1,5},{5... | collective-permute-start | bytes 184328 | tf_op jit(solution)/shard_map/ppermute | solution.py:318
  9.3 0.0 collective-permute-done.face_ref
  9.3 0.7 %shard_map.30 = (f32[3,3,8,128]{3,2,1,0:T(8,128)S(1)}, f32[3,3,8,128]{3,2,1,0:T(8,128)S(1)}, f32[3,3,8,128]{3,2,1,0:T(8,128)S(1)}, f32[3,3,8,128]{3,2,1,0:T(8,128)S(1)}) custom-call(f32[3,6,16,128]{3,2,1,0:T(8,128)S(1)} %collective-permute-done.face_ref, f32[6,2,3,3,2,8,128]{6,5,4,3,2,1,0:T(8,128)S(1)} %get-tuple-element.34.edges, ...), custom_call_target="tpu_custom_call" | custom-call | flops 4294967296 | bytes 1048576 | tf_op jit(solution)/shard_map/pallas_call | solution.py:26
  10.0 2.6 %collective-permute-start.5 = (f32[3,3,8,128]{3,2,1,0:T(8,128)S(1)}, f32[3,3,8,128]{3,2,1,0:T(8,128)S(1)}, u32[]{:S(2)}, u32[]{:S(2)}) collective-permute-start(f32[3,3,8,128]{3,2,1,0:T(8,128)S(1)} %get-tuple-element.46), channel_id=1, source_target_pairs={{0,12},{4,8},{8,4},{12,0},{16,28},{20,24},{24,20},{28,16},{1,13},{... | collective-permute-start | bytes 110600 | tf_op jit(solution)/shard_map/ppermute | solution.py:318
  12.6 0.4 %collective-permute-start.6 = (f32[3,3,8,128]{3,2,1,0:T(8,128)S(1)}, f32[3,3,8,128]{3,2,1,0:T(8,128)S(1)}, u32[]{:S(2)}, u32[]{:S(2)}) collective-permute-start(f32[3,3,8,128]{3,2,1,0:T(8,128)S(1)} %get-tuple-element.47), channel_id=1, source_target_pairs={{0,8},{4,12},{8,0},{12,4},{16,24},{20,28},{24,16},{28,20},{1,9},{5... | collective-permute-start | bytes 110600 | tf_op jit(solution)/shard_map/ppermute | solution.py:318
  13.1 0.5 %collective-permute-start.7 = (f32[3,3,8,128]{3,2,1,0:T(8,128)S(1)}, f32[3,3,8,128]{3,2,1,0:T(8,128)S(1)}, u32[]{:S(2)}, u32[]{:S(2)}) collective-permute-start(f32[3,3,8,128]{3,2,1,0:T(8,128)S(1)} %get-tuple-element.48), channel_id=1, source_target_pairs={{0,4},{4,0},{8,12},{12,8},{16,20},{20,16},{24,28},{28,24},{1,5},{5... | collective-permute-start | bytes 110600 | tf_op jit(solution)/shard_map/ppermute | solution.py:318
  13.6 0.0 collective-permute-done.3.refs_2_.refs_3_
  13.6 0.0 collective-permute-done.4.refs_3_.refs_4_
  13.6 0.1 shard_map.32
  13.7 2.7 %collective-permute-start.9 = (f32[5,3,8,128]{3,2,1,0:T(8,128)S(1)}, f32[5,3,8,128]{3,2,1,0:T(8,128)S(1)}, u32[]{:S(2)}, u32[]{:S(2)}) collective-permute-start(f32[5,3,8,128]{3,2,1,0:T(8,128)S(1)} %shard_map.32), channel_id=1, source_target_pairs={{0,16},{4,20},{8,24},{12,28},{16,0},{20,4},{24,8},{28,12},{1,17},{... | collective-permute-start | bytes 184328 | tf_op jit(solution)/shard_map/ppermute | solution.py:324
  16.3 0.3 %collective-permute-done.6.refs_2_.refs_3_ = f32[3,3,8,128]{3,2,1,0:T(8,128)S(1)} collective-permute-done((f32[3,3,8,128]{3,2,1,0:T(8,128)S(1)}, f32[3,3,8,128]{3,2,1,0:T(8,128)S(1)}, u32[]{:S(2)}, u32[]{:S(2)}) %collective-permute-start.6) | collective-permute-done | bytes 36896 | tf_op jit(solution)/shard_map/ppermute | solution.py:318
  16.7 0.4 %collective-permute-done.7.refs_3_.refs_4_ = f32[3,3,8,128]{3,2,1,0:T(8,128)S(1)} collective-permute-done((f32[3,3,8,128]{3,2,1,0:T(8,128)S(1)}, f32[3,3,8,128]{3,2,1,0:T(8,128)S(1)}, u32[]{:S(2)}, u32[]{:S(2)}) %collective-permute-start.7) | collective-permute-done | bytes 36896 | tf_op jit(solution)/shard_map/ppermute | solution.py:318
  17.1 2.7 %collective-permute-start.8 = (f32[3,3,8,128]{3,2,1,0:T(8,128)S(1)}, f32[3,3,8,128]{3,2,1,0:T(8,128)S(1)}, u32[]{:S(2)}, u32[]{:S(2)}) collective-permute-start(f32[3,3,8,128]{3,2,1,0:T(8,128)S(1)} %shard_map.33), channel_id=1, source_target_pairs={{0,16},{4,20},{8,24},{12,28},{16,0},{20,4},{24,8},{28,12},{1,17},{... | collective-permute-start | bytes 110600 | tf_op jit(solution)/shard_map/ppermute | solution.py:324
  19.7 0.1 shard_map.34
  19.8 2.0 %collective-permute-start.13 = (f32[5,3,8,128]{3,2,1,0:T(8,128)S(1)}, f32[5,3,8,128]{3,2,1,0:T(8,128)S(1)}, u32[]{:S(2)}, u32[]{:S(2)}) collective-permute-start(f32[5,3,8,128]{3,2,1,0:T(8,128)S(1)} %get-tuple-element.56), channel_id=1, source_target_pairs={{0,12},{4,8},{8,4},{12,0},{16,28},{20,24},{24,20},{28,16},{1,13},{... | collective-permute-start | bytes 184328 | tf_op jit(solution)/shard_map/ppermute | solution.py:318
  21.8 0.4 %collective-permute-start.14 = (f32[5,3,8,128]{3,2,1,0:T(8,128)S(1)}, f32[5,3,8,128]{3,2,1,0:T(8,128)S(1)}, u32[]{:S(2)}, u32[]{:S(2)}) collective-permute-start(f32[5,3,8,128]{3,2,1,0:T(8,128)S(1)} %get-tuple-element.57), channel_id=1, source_target_pairs={{0,8},{4,12},{8,0},{12,4},{16,24},{20,28},{24,16},{28,20},{1,9},{5... | collective-permute-start | bytes 184328 | tf_op jit(solution)/shard_map/ppermute | solution.py:318
  22.2 1.1 %collective-permute-start.15 = (f32[5,3,8,128]{3,2,1,0:T(8,128)S(1)}, f32[5,3,8,128]{3,2,1,0:T(8,128)S(1)}, u32[]{:S(2)}, u32[]{:S(2)}) collective-permute-start(f32[5,3,8,128]{3,2,1,0:T(8,128)S(1)} %get-tuple-element.58), channel_id=1, source_target_pairs={{0,4},{4,0},{8,12},{12,8},{16,20},{20,16},{24,28},{28,24},{1,5},{5... | collective-permute-start | bytes 184328 | tf_op jit(solution)/shard_map/ppermute | solution.py:318
  23.4 2.0 %collective-permute-start.10 = (f32[3,3,8,128]{3,2,1,0:T(8,128)S(1)}, f32[3,3,8,128]{3,2,1,0:T(8,128)S(1)}, u32[]{:S(2)}, u32[]{:S(2)}) collective-permute-start(f32[3,3,8,128]{3,2,1,0:T(8,128)S(1)} %get-tuple-element.53), channel_id=1, source_target_pairs={{0,12},{4,8},{8,4},{12,0},{16,28},{20,24},{24,20},{28,16},{1,13},{... | collective-permute-start | bytes 110600 | tf_op jit(solution)/shard_map/ppermute | solution.py:318
  25.4 0.4 %collective-permute-start.11 = (f32[3,3,8,128]{3,2,1,0:T(8,128)S(1)}, f32[3,3,8,128]{3,2,1,0:T(8,128)S(1)}, u32[]{:S(2)}, u32[]{:S(2)}) collective-permute-start(f32[3,3,8,128]{3,2,1,0:T(8,128)S(1)} %get-tuple-element.54), channel_id=1, source_target_pairs={{0,8},{4,12},{8,0},{12,4},{16,24},{20,28},{24,16},{28,20},{1,9},{5... | collective-permute-start | bytes 110600 | tf_op jit(solution)/shard_map/ppermute | solution.py:318
  25.8 1.1 %collective-permute-start.12 = (f32[3,3,8,128]{3,2,1,0:T(8,128)S(1)}, f32[3,3,8,128]{3,2,1,0:T(8,128)S(1)}, u32[]{:S(2)}, u32[]{:S(2)}) collective-permute-start(f32[3,3,8,128]{3,2,1,0:T(8,128)S(1)} %get-tuple-element.55), channel_id=1, source_target_pairs={{0,4},{4,0},{8,12},{12,8},{16,20},{20,16},{24,28},{28,24},{1,5},{5... | collective-permute-start | bytes 110600 | tf_op jit(solution)/shard_map/ppermute | solution.py:318
  27.0 0.8 %shard_map.36.refs_4_ = f32[3,16,16,128]{3,2,1,0:T(8,128)} custom-call(f32[16,3,2,8,128]{4,3,2,1,0:T(8,128)S(1)} %get-tuple-element.32.kept, f32[5,3,8,128]{3,2,1,0:T(8,128)S(1)} %get-tuple-element.50.refs_0_, f32[5,3,8,128]{3,2,1,0:T(8,128)S(1)} %collective-permute-done.13.refs_1_, f32[5,3,8,128]{3,2,1,0:T(8,128)S(1)} %collective-permute-done.14.refs_2_, ...), custom_call_target="tpu_custom_call" | custom-call | flops 4294967296 | bytes 1048576 | tf_op jit(solution)/shard_map/pallas_call | solution.py:391
  27.8 0.6 %collective-permute-done.10.refs_1_ = f32[3,3,8,128]{3,2,1,0:T(8,128)S(1)} collective-permute-done((f32[3,3,8,128]{3,2,1,0:T(8,128)S(1)}, f32[3,3,8,128]{3,2,1,0:T(8,128)S(1)}, u32[]{:S(2)}, u32[]{:S(2)}) %collective-permute-start.10) | collective-permute-done | bytes 36896 | tf_op jit(solution)/shard_map/ppermute | solution.py:318
  28.3 1.0 %collective-permute-done.11.refs_2_ = f32[3,3,8,128]{3,2,1,0:T(8,128)S(1)} collective-permute-done((f32[3,3,8,128]{3,2,1,0:T(8,128)S(1)}, f32[3,3,8,128]{3,2,1,0:T(8,128)S(1)}, u32[]{:S(2)}, u32[]{:S(2)}) %collective-permute-start.11) | collective-permute-done | bytes 36896 | tf_op jit(solution)/shard_map/ppermute | solution.py:318
  29.4 0.4 %collective-permute-done.12.refs_3_ = f32[3,3,8,128]{3,2,1,0:T(8,128)S(1)} collective-permute-done((f32[3,3,8,128]{3,2,1,0:T(8,128)S(1)}, f32[3,3,8,128]{3,2,1,0:T(8,128)S(1)}, u32[]{:S(2)}, u32[]{:S(2)}) %collective-permute-start.12) | collective-permute-done | bytes 36896 | tf_op jit(solution)/shard_map/ppermute | solution.py:318
  (14 shorter events, 0.1 us)
Async XLA Ops:
  0.0 1.0 %copy-start = (f32[1,3,16,16,128]{4,3,2,1,0:T(8,128)S(1)}, f32[1,3,16,16,128]{4,3,2,1,0:T(8,128)}, u32[]{:S(2)}) copy-start(f32[1,3,16,16,128]{4,3,2,1,0:T(8,128)} %param.2) | copy-start | bytes 1179652
  1.0 3.2 %copy-start.1 = (f32[16,16,128]{2,1,0:T(8,128)S(1)}, f32[16,16,128]{2,1,0:T(8,128)}, u32[]{:S(2)}) copy-start(f32[16,16,128]{2,1,0:T(8,128)} %rate_ref.1) | copy-start | bytes 393220
  1.0 4.0 %collective-permute-start.1 = (f32[3,6,16,128]{3,2,1,0:T(8,128)S(1)}, f32[3,6,16,128]{3,2,1,0:T(8,128)S(1)}, u32[]{:S(2)}, u32[]{:S(2)}) collective-permute-start(f32[3,6,16,128]{3,2,1,0:T(8,128)S(1)} %get-tuple-element.38), channel_id=1, source_target_pairs={{0,1},{1,0},{2,3},{3,2},{4,5},{5,4},{6,7},{7,6},{8,9},{9,8},{10,11... | collective-permute-start | bytes 442376 | tf_op jit(solution)/shard_map/ppermute | solution.py:314
  1.5 7.8 %collective-permute-start = (f32[3,6,16,128]{3,2,1,0:T(8,128)S(1)}, f32[3,6,16,128]{3,2,1,0:T(8,128)S(1)}, u32[]{:S(2)}, u32[]{:S(2)}) collective-permute-start(f32[3,6,16,128]{3,2,1,0:T(8,128)S(1)} %get-tuple-element.33), channel_id=1, source_target_pairs={{0,3},{1,2},{2,1},{3,0},{4,7},{5,6},{6,5},{7,4},{8,11},{9,10},{10,... | collective-permute-start | bytes 442376 | tf_op jit(solution)/shard_map/ppermute | solution.py:314
  5.8 7.3 %collective-permute-start.2 = (f32[5,3,8,128]{3,2,1,0:T(8,128)S(1)}, f32[5,3,8,128]{3,2,1,0:T(8,128)S(1)}, u32[]{:S(2)}, u32[]{:S(2)}) collective-permute-start(f32[5,3,8,128]{3,2,1,0:T(8,128)S(1)} %get-tuple-element.41), channel_id=1, source_target_pairs={{0,12},{4,8},{8,4},{12,0},{16,28},{20,24},{24,20},{28,16},{1,13},{... | collective-permute-start | bytes 184328 | tf_op jit(solution)/shard_map/ppermute | solution.py:318
  8.4 5.3 %collective-permute-start.3 = (f32[5,3,8,128]{3,2,1,0:T(8,128)S(1)}, f32[5,3,8,128]{3,2,1,0:T(8,128)S(1)}, u32[]{:S(2)}, u32[]{:S(2)}) collective-permute-start(f32[5,3,8,128]{3,2,1,0:T(8,128)S(1)} %get-tuple-element.42), channel_id=1, source_target_pairs={{0,8},{4,12},{8,0},{12,4},{16,24},{20,28},{24,16},{28,20},{1,9},{5... | collective-permute-start | bytes 184328 | tf_op jit(solution)/shard_map/ppermute | solution.py:318
  8.8 4.8 %collective-permute-start.4 = (f32[5,3,8,128]{3,2,1,0:T(8,128)S(1)}, f32[5,3,8,128]{3,2,1,0:T(8,128)S(1)}, u32[]{:S(2)}, u32[]{:S(2)}) collective-permute-start(f32[5,3,8,128]{3,2,1,0:T(8,128)S(1)} %get-tuple-element.43), channel_id=1, source_target_pairs={{0,4},{4,0},{8,12},{12,8},{16,20},{20,16},{24,28},{28,24},{1,5},{5... | collective-permute-start | bytes 184328 | tf_op jit(solution)/shard_map/ppermute | solution.py:318
  10.0 6.3 %collective-permute-start.5 = (f32[3,3,8,128]{3,2,1,0:T(8,128)S(1)}, f32[3,3,8,128]{3,2,1,0:T(8,128)S(1)}, u32[]{:S(2)}, u32[]{:S(2)}) collective-permute-start(f32[3,3,8,128]{3,2,1,0:T(8,128)S(1)} %get-tuple-element.46), channel_id=1, source_target_pairs={{0,12},{4,8},{8,4},{12,0},{16,28},{20,24},{24,20},{28,16},{1,13},{... | collective-permute-start | bytes 110600 | tf_op jit(solution)/shard_map/ppermute | solution.py:318
  12.6 4.0 %collective-permute-start.6 = (f32[3,3,8,128]{3,2,1,0:T(8,128)S(1)}, f32[3,3,8,128]{3,2,1,0:T(8,128)S(1)}, u32[]{:S(2)}, u32[]{:S(2)}) collective-permute-start(f32[3,3,8,128]{3,2,1,0:T(8,128)S(1)} %get-tuple-element.47), channel_id=1, source_target_pairs={{0,8},{4,12},{8,0},{12,4},{16,24},{20,28},{24,16},{28,20},{1,9},{5... | collective-permute-start | bytes 110600 | tf_op jit(solution)/shard_map/ppermute | solution.py:318
  13.1 4.0 %collective-permute-start.7 = (f32[3,3,8,128]{3,2,1,0:T(8,128)S(1)}, f32[3,3,8,128]{3,2,1,0:T(8,128)S(1)}, u32[]{:S(2)}, u32[]{:S(2)}) collective-permute-start(f32[3,3,8,128]{3,2,1,0:T(8,128)S(1)} %get-tuple-element.48), channel_id=1, source_target_pairs={{0,4},{4,0},{8,12},{12,8},{16,20},{20,16},{24,28},{28,24},{1,5},{5... | collective-permute-start | bytes 110600 | tf_op jit(solution)/shard_map/ppermute | solution.py:318
  13.7 6.1 %collective-permute-start.9 = (f32[5,3,8,128]{3,2,1,0:T(8,128)S(1)}, f32[5,3,8,128]{3,2,1,0:T(8,128)S(1)}, u32[]{:S(2)}, u32[]{:S(2)}) collective-permute-start(f32[5,3,8,128]{3,2,1,0:T(8,128)S(1)} %shard_map.32), channel_id=1, source_target_pairs={{0,16},{4,20},{8,24},{12,28},{16,0},{20,4},{24,8},{28,12},{1,17},{... | collective-permute-start | bytes 184328 | tf_op jit(solution)/shard_map/ppermute | solution.py:324
  17.1 6.3 %collective-permute-start.8 = (f32[3,3,8,128]{3,2,1,0:T(8,128)S(1)}, f32[3,3,8,128]{3,2,1,0:T(8,128)S(1)}, u32[]{:S(2)}, u32[]{:S(2)}) collective-permute-start(f32[3,3,8,128]{3,2,1,0:T(8,128)S(1)} %shard_map.33), channel_id=1, source_target_pairs={{0,16},{4,20},{8,24},{12,28},{16,0},{20,4},{24,8},{28,12},{1,17},{... | collective-permute-start | bytes 110600 | tf_op jit(solution)/shard_map/ppermute | solution.py:324
  19.8 6.0 %collective-permute-start.13 = (f32[5,3,8,128]{3,2,1,0:T(8,128)S(1)}, f32[5,3,8,128]{3,2,1,0:T(8,128)S(1)}, u32[]{:S(2)}, u32[]{:S(2)}) collective-permute-start(f32[5,3,8,128]{3,2,1,0:T(8,128)S(1)} %get-tuple-element.56), channel_id=1, source_target_pairs={{0,12},{4,8},{8,4},{12,0},{16,28},{20,24},{24,20},{28,16},{1,13},{... | collective-permute-start | bytes 184328 | tf_op jit(solution)/shard_map/ppermute | solution.py:318
  21.8 5.2 %collective-permute-start.14 = (f32[5,3,8,128]{3,2,1,0:T(8,128)S(1)}, f32[5,3,8,128]{3,2,1,0:T(8,128)S(1)}, u32[]{:S(2)}, u32[]{:S(2)}) collective-permute-start(f32[5,3,8,128]{3,2,1,0:T(8,128)S(1)} %get-tuple-element.57), channel_id=1, source_target_pairs={{0,8},{4,12},{8,0},{12,4},{16,24},{20,28},{24,16},{28,20},{1,9},{5... | collective-permute-start | bytes 184328 | tf_op jit(solution)/shard_map/ppermute | solution.py:318
  22.2 4.7 %collective-permute-start.15 = (f32[5,3,8,128]{3,2,1,0:T(8,128)S(1)}, f32[5,3,8,128]{3,2,1,0:T(8,128)S(1)}, u32[]{:S(2)}, u32[]{:S(2)}) collective-permute-start(f32[5,3,8,128]{3,2,1,0:T(8,128)S(1)} %get-tuple-element.58), channel_id=1, source_target_pairs={{0,4},{4,0},{8,12},{12,8},{16,20},{20,16},{24,28},{28,24},{1,5},{5... | collective-permute-start | bytes 184328 | tf_op jit(solution)/shard_map/ppermute | solution.py:318
  23.4 4.9 %collective-permute-start.10 = (f32[3,3,8,128]{3,2,1,0:T(8,128)S(1)}, f32[3,3,8,128]{3,2,1,0:T(8,128)S(1)}, u32[]{:S(2)}, u32[]{:S(2)}) collective-permute-start(f32[3,3,8,128]{3,2,1,0:T(8,128)S(1)} %get-tuple-element.53), channel_id=1, source_target_pairs={{0,12},{4,8},{8,4},{12,0},{16,28},{20,24},{24,20},{28,16},{1,13},{... | collective-permute-start | bytes 110600 | tf_op jit(solution)/shard_map/ppermute | solution.py:318
  25.4 4.0 %collective-permute-start.11 = (f32[3,3,8,128]{3,2,1,0:T(8,128)S(1)}, f32[3,3,8,128]{3,2,1,0:T(8,128)S(1)}, u32[]{:S(2)}, u32[]{:S(2)}) collective-permute-start(f32[3,3,8,128]{3,2,1,0:T(8,128)S(1)} %get-tuple-element.54), channel_id=1, source_target_pairs={{0,8},{4,12},{8,0},{12,4},{16,24},{20,28},{24,16},{28,20},{1,9},{5... | collective-permute-start | bytes 110600 | tf_op jit(solution)/shard_map/ppermute | solution.py:318
  25.8 4.0 %collective-permute-start.12 = (f32[3,3,8,128]{3,2,1,0:T(8,128)S(1)}, f32[3,3,8,128]{3,2,1,0:T(8,128)S(1)}, u32[]{:S(2)}, u32[]{:S(2)}) collective-permute-start(f32[3,3,8,128]{3,2,1,0:T(8,128)S(1)} %get-tuple-element.55), channel_id=1, source_target_pairs={{0,4},{4,0},{8,12},{12,8},{16,20},{20,16},{24,28},{28,24},{1,5},{5... | collective-permute-start | bytes 110600 | tf_op jit(solution)/shard_map/ppermute | solution.py:318

commit v4 on v2

--- a/solution.py
+++ b/solution.py
@@ -118,7 +118,7 @@
     near_ref[...] = own_ref[:, pl.ds(near * top, width)]
 
 
-def inside_kernel(own_ref, rate_ref, edges, middle, faded, early_damp, late_damp, kept, damps, inner, *fields):
+def inside_kernel(own_ref, rate_ref, edges, middle, faded, damp_ref, kept, damps, inner, *fields):
     layers = own_ref.shape[1]
     near = near_side()
     slices = lax.axis_size("tm")
@@ -178,8 +178,9 @@
 
     for odd in (0, 1):
         inner[odd, :STAGES] = damps[near, odd]
-    early_damp[...] = share_of(inner, 0, early_damp.shape[0])
-    late_damp[...] = share_of(damps.at[1 - near], 0, late_damp.shape[0])
+    early, late = inner.shape[1] // 2, STAGES // 2
+    damp_ref[:early] = share_of(inner, 0, early)
+    damp_ref[early:] = share_of(damps.at[1 - near], 0, late)
 
 
 def border(side, face_ref, edges, middle, faded, jumps, strip):
@@ -227,9 +228,12 @@
         out[...] = share_of(jumps, k, out.shape[0])
 
 
-def sort_in(jumps, order):
+def sort_in(early, late, order):
+    split = early[0].shape[0]
     for k in range(GROUP):
-        order[lax.bitwise_xor(spot(), partner(k))] = jumps[k][...]
+        place = lax.bitwise_xor(spot(), partner(k))
+        order[place, :split] = early[k][...]
+        order[place, split:] = late[k][...]
 
 
 def sort_out(order, outs):
@@ -245,52 +249,77 @@
     return total
 
 
-def total_kernel(*refs):
-    jumps, damp_ref, out, order = refs[:GROUP], refs[GROUP], refs[GROUP + 1], refs[GROUP + 2]
-    sort_in(jumps, order)
-    out[...] = run(order, damp_ref[...][:, None], jnp.zeros(out.shape, jnp.float32))
+def total_of(jumps, damp):
+    total = None
+    for slice_ in range(GROUP):
+        jump = jumps[slice_]
+        total = jump if total is None else damp[:, None] * total + jump
+    return total
+
+
+def early_kernel(*refs):
+    jumps, (damp_ref, out, order) = refs[:GROUP], refs[GROUP:]
+    for k in range(GROUP):
+        order[lax.bitwise_xor(spot(), partner(k))] = jumps[k][...]
+    out[...] = total_of(order, damp_ref[: out.shape[0]])
+
+
+def total_kernel(early_ref, *refs):
+    jumps, (damp_ref, out, order) = refs[:GROUP], refs[GROUP:]
+    split = early_ref.shape[0]
+    for k in range(GROUP):
+        order[lax.bitwise_xor(spot(), partner(k))] = jumps[k][...]
+    out[:split] = early_ref[...]
+    out[split:] = total_of(order, damp_ref[split:])
 
 
 def spread_kernel(*refs):
-    carry_ref, jumps, damp_ref = refs[0], refs[1 : 1 + GROUP], refs[1 + GROUP]
-    outs, order = refs[GROUP + 2 : -1], refs[-1]
-    sort_in(jumps, order)
+    carry_ref, early, late = refs[0], refs[1 : 1 + GROUP], refs[1 + GROUP : 1 + 2 * GROUP]
+    damp_ref, outs, order = refs[1 + 2 * GROUP], refs[2 + 2 * GROUP : -1], refs[-1]
+    sort_in(early, late, order)
     run(order, damp_ref[...][:, None], jnp.where(lax.axis_index("tm") < GROUP, 0.0, carry_ref[...]))
     sort_out(order, outs)
 
 
-def finish_kernel(far, kept, *refs):
-    pieces, (out, part, sem) = refs[:GROUP], refs[-3:]
-    layers, count = out.shape[1], part.shape[1]
-    rows = out.shape[2] // 2
-    down = far + (1 - 2 * far) * near_side()
-    base = down * (layers - count)
-    first_slice = lax.axis_index("tm") == 0
-
-    @pl.when(first_slice)
+def write(whole, out, sem):
+    copy = pltpu.make_async_copy(whole, out, sem)
+    copy.start()
+    copy.wait()
+
+
+def first_kernel(kept, out, whole, sem):
+    @pl.when(lax.axis_index("tm") == 0)
     def _():
-        for layer in range(count):
-            pair = load(kept, base + layer)
+        for layer in range(out.shape[1]):
+            pair = load(kept, layer)
             for c in range(3):
-                join_rows(part, (c, layer), pair[c])
-
-    @pl.when(jnp.logical_not(first_slice))
+                join_rows(whole, (c, layer), pair[c])
+        write(whole, out, sem)
+
+
+def finish_kernel(*refs):
+    pieces, (_, out, whole, sem) = refs[:GROUP], refs[GROUP:]
+    layers, rows = out.shape[1], out.shape[2] // 2
+    split = (layers - STAGES) // 2
+    near = near_side()
+
+    @pl.when(lax.axis_index("tm") != 0)
     def _():
         for k, piece in enumerate(pieces):
-            chunk, share = chunk_of(k), piece.shape[0]
+            chunk = chunk_of(k)
             for odd in (0, 1):
 
                 @pl.when(chunk // 2 == odd)
                 def _():
-                    for j in range(share):
-                        slot = lax.rem(chunk, 2) * share + j
-                        layer = slot + down * (count - 1 - 2 * slot)
+                    for j in range(piece.shape[0]):
+                        if j < split:
+                            slot = lax.rem(chunk, 2) * split + j
+                        else:
+                            slot = layers - 1 - (lax.rem(chunk, 2) * (STAGES // 2) + j - split)
+                        layer = slot + near * (layers - 1 - 2 * slot)
                         for c in range(3):
-                            part[c, layer, pl.ds(odd, rows, stride=2), :] = piece[j, c]
-
-    copy = pltpu.make_async_copy(part, out.at[:, pl.ds(base, count)], sem)
-    copy.start()
-    copy.wait()
+                            whole[c, layer, pl.ds(odd, rows, stride=2), :] = piece[j, c]
+        write(whole, out, sem)
 
 
 def shards(states, rate):
@@ -322,13 +351,13 @@
     near_face = halo(near_face, [(i, i ^ 1) for i in range(slabs)])
     far_face = halo(far_face, [(i, i + 1 if i % 2 else i - 1 + slabs) for i in range(slabs)])
     row = (rows // 2, width)
-    edges, middle, faded, *damps, kept = call(
+    edges, middle, faded, damp, kept = call(
         inside_kernel,
         [
             f32(STAGES, 2, 3, *tile),
             f32(middle_layers, *tile),
             f32(2, STAGES, *tile),
-            *[f32(size, *row) for size in sizes],
+            f32(sum(sizes), *row),
             f32(layers, *tile),
         ],
         own, rate,
@@ -341,7 +370,8 @@
     )
     strip = pltpu.VMEM((STAGES + 1, STAGES, *tile), jnp.float32)
     shares = [f32(size, 3, *row) for size in sizes]
-    orders = [pltpu.VMEM((GROUP, *share.shape), jnp.float32) for share in shares]
+    whole_share = f32(sum(sizes), 3, *row)
+    order = pltpu.VMEM((GROUP, *whole_share.shape), jnp.float32)
 
     def after(value, earlier):
         return lax.optimization_barrier((value, earlier))[0]
@@ -356,46 +386,42 @@
         )
         halves.append(swap(jumps))
 
-    carries, total = [], halves[1][0]
-    for far, jumps in enumerate(halves):
-        jumps[0] = after(jumps[0], total)
-        total = call(
-            total_kernel, shares[far], *jumps, damps[far], scratch=[orders[far]], flops=BUSY
-        )
-        carry = onward(total, 1)
-        if groups > 2:
-            carry = jnp.where(team < 1, 0.0, carry)
-            fade, distance = damps[far][:, None] ** GROUP, 1
-            while distance < groups - 1:
-                carry = carry + jnp.where(team < distance, 0.0, fade * onward(carry, distance))
-                distance, fade = 2 * distance, fade * fade
-        carries.append(carry)
-
-    updated, news = None, None
-    for far, (jumps, carry) in enumerate(zip(halves, carries)):
-        if far:
-            jumps[0] = after(jumps[0], news[0])
-        news = call(
-            spread_kernel, [shares[far]] * GROUP, carry, *jumps, damps[far],
-            scratch=[orders[far]],
-            flops=BUSY,
-        )
-        halves[far] = swap(news)
-    for far, pieces in enumerate(halves):
-        args = [kept, *pieces] + ([updated] if far else [])
-        updated = pl.pallas_call(
-            functools.partial(finish_kernel, far),
-            out_shape=f32(*own.shape),
-            in_specs=[VMEM] * (1 + GROUP) + [ANY] * far,
-            out_specs=ANY,
-            scratch_shapes=[
-                pltpu.VMEM((3, 2 * sizes[far], rows, width), jnp.float32),
-                pltpu.SemaphoreType.DMA,
-            ],
-            input_output_aliases={1 + GROUP: 0} if far else {},
-            compiler_params=PARAMS,
-            cost_estimate=pl.CostEstimate(flops=BUSY, bytes_accessed=1 << 20, transcendentals=0),
-        )(*args)
+    orders = [pltpu.VMEM((GROUP, *share.shape), jnp.float32) for share in shares]
+    halves[0][0] = after(halves[0][0], halves[1][0])
+    total = call(early_kernel, shares[0], *halves[0], damp, scratch=[orders[0]], flops=BUSY)
+    total = call(
+        total_kernel, whole_share, total, *halves[1], damp, scratch=[orders[1]], flops=BUSY
+    )
+    carry = onward(total, 1)
+    if groups > 2:
+        carry = jnp.where(team < 1, 0.0, carry)
+        fade, distance = damp[:, None] ** GROUP, 1
+        while distance < groups - 1:
+            carry = carry + jnp.where(team < distance, 0.0, fade * onward(carry, distance))
+            distance, fade = 2 * distance, fade * fade
+    news = call(
+        spread_kernel, [whole_share] * GROUP, carry, *halves[0], *halves[1], damp, scratch=[order]
+    )
+    pieces = swap(news)
+    whole = [pltpu.VMEM(own.shape, jnp.float32), pltpu.SemaphoreType.DMA]
+    updated = pl.pallas_call(
+        first_kernel,
+        out_shape=f32(*own.shape),
+        in_specs=[VMEM],
+        out_specs=ANY,
+        scratch_shapes=whole,
+        compiler_params=PARAMS,
+        cost_estimate=pl.CostEstimate(flops=BUSY, bytes_accessed=1 << 20, transcendentals=0),
+    )(after(kept, pieces[1]))
+    updated = pl.pallas_call(
+        finish_kernel,
+        out_shape=f32(*own.shape),
+        in_specs=[VMEM] * GROUP + [ANY],
+        out_specs=ANY,
+        scratch_shapes=whole,
+        input_output_aliases={GROUP: 0},
+        compiler_params=PARAMS,
+    )(*pieces, updated)
     return updated[None]
 
 

time: 30.6 us -> 30 us (0.980); the launches traced: 30.5 us -> 29.5 us
  starting transfers between devices: 22.7 us -> 16.5 us
  waiting for transfers between devices: 2.82 us -> 8.65 us
  Pallas kernels: 3.89 us -> 3.26 us
    ppermute x12 -> x9, starting transfers between devices: 14.2 us -> 10.7 us  [swap(): lax.ppermute(parts[k], 'tm', [(i, i ^ partner(k)) for i in range(slices)])]
    ppermute x2 -> x1, waiting for transfers between devices: 0.01 us -> 2.94 us  [onward(): lax.ppermute(value, 'tm', [(i, (i + step) % slices) for i in range(slices)])]
    ppermute x12 -> x9, waiting for transfers between devices: 2.81 us -> 5.7 us  [swap(): lax.ppermute(parts[k], 'tm', [(i, i ^ partner(k)) for i in range(slices)])]
    ppermute x2 -> x1, starting transfers between devices: 5.31 us -> 2.65 us  [onward(): lax.ppermute(value, 'tm', [(i, (i + step) % slices) for i in range(slices)])]
    pallas_call x2, Pallas kernels: 1.4 us -> 0.79 us  [the longest x1 0.78 us: shards(): pl.pallas_call(first_kernel, out_shape=f32(*own.shape), in_specs=[VMEM],...]
    pallas_call x8 -> x7, Pallas kernels: 2.48 us -> 2.47 us  [call(): pl.pallas_call(kernel, out_shape=out_shape, in_specs=[VMEM] * len(args),...]
  transfers between devices with their start and end apart: 16 -> 12, of which waited for: 5 -> 6; matrix products, arithmetic and copies ran while one was open for 0% -> 0% of each run, Pallas kernels for 10% -> 10%
where the time goes in v4:
time: 30 us; the launch traced here: 29.5 us
  starting transfers between devices  16.5 us (55%)
  waiting for transfers between devices  8.65 us (29%)
  Pallas kernels  3.26 us (11%)
  local copies, waits for them, and re-layouts  1 us (3%)
    ppermute x9, starting transfers between devices, swap(): lax.ppermute(parts[k], 'tm', [(i, i ^ partner(k)) for i in range(slices)])  10.7 us
    ppermute x9, waiting for transfers between devices, swap(): lax.ppermute(parts[k], 'tm', [(i, i ^ partner(k)) for i in range(slices)])  5.7 us
    ppermute x2, starting transfers between devices, halo(): return lax.ppermute(value, 'gz', [(i, j % slabs) for i, j in pairs])  3.16 us
    ppermute x1, waiting for transfers between devices, onward(): lax.ppermute(value, 'tm', [(i, (i + step) % slices) for i in range(slices)])  2.94 us
    ppermute x1, starting transfers between devices, onward(): lax.ppermute(value, 'tm', [(i, (i + step) % slices) for i in range(slices)])  2.65 us
    pallas_call x7, Pallas kernels, call(): pl.pallas_call(kernel, out_shape=out_shape, in_specs=[VMEM] * len(args),...  2.47 us
    unnamed x4, local copies, waits for them, and re-layouts  1 us
    pallas_call x1, Pallas kernels, shards(): pl.pallas_call(first_kernel, out_shape=f32(*own.shape), in_specs=[VMEM],...  0.78 us
  transfers between devices with their start and end apart: 12, of which 6 were waited for; matrix products, arithmetic and copies ran while one was open for 0% of the time, Pallas kernels for 10%

profile of v4, /device:TPU:0, one launch (start us, length us, event | category | flops | bytes accessed | tf_op | source)
XLA Modules:
  0.0 29.5 jit_solution(10357849927273260882)
XLA Ops:
  0.0 0.0 copy-start
  0.0 1.0 %copy-done = f32[1,3,16,16,128]{4,3,2,1,0:T(8,128)S(1)} copy-done((f32[1,3,16,16,128]{4,3,2,1,0:T(8,128)S(1)}, f32[1,3,16,16,128]{4,3,2,1,0:T(8,128)}, u32[]{:S(2)}) %copy-start) | copy-done | bytes 393240
  1.0 0.5 %collective-permute-start = (f32[3,6,16,128]{3,2,1,0:T(8,128)S(1)}, f32[3,6,16,128]{3,2,1,0:T(8,128)S(1)}, u32[]{:S(2)}, u32[]{:S(2)}) collective-permute-start(f32[3,6,16,128]{3,2,1,0:T(8,128)S(1)} %get-tuple-element.26), channel_id=1, source_target_pairs={{0,1},{1,0},{2,3},{3,2},{4,5},{5,4},{6,7},{7,6},{8,9},{9,8},{10,11... | collective-permute-start | bytes 442376 | tf_op jit(solution)/shard_map/ppermute | solution.py:338
  1.5 2.6 %collective-permute-start.1 = (f32[3,6,16,128]{3,2,1,0:T(8,128)S(1)}, f32[3,6,16,128]{3,2,1,0:T(8,128)S(1)}, u32[]{:S(2)}, u32[]{:S(2)}) collective-permute-start(f32[3,6,16,128]{3,2,1,0:T(8,128)S(1)} %get-tuple-element.31), channel_id=1, source_target_pairs={{0,3},{1,2},{2,1},{3,0},{4,7},{5,6},{6,5},{7,4},{8,11},{9,10},{10,... | collective-permute-start | bytes 442376 | tf_op jit(solution)/shard_map/ppermute | solution.py:338
  4.2 0.0 copy-done.1
  4.2 0.8 %shard_map.29 = (f32[6,2,3,3,2,8,128]{6,5,4,3,2,1,0:T(8,128)S(1)}, f32[4,3,2,8,128]{4,3,2,1,0:T(8,128)S(1)}, f32[2,6,3,2,8,128]{5,4,3,2,1,0:T(8,128)S(1)}, f32[8...) custom-call(f32[3,16,16,128]{3,2,1,0:T(8,128)S(1)} %bitcast.3, f32[16,16,128]{2,1,0:T(8,128)S(1)} %copy-done.1), custom_call_target="tpu_custom_call" | custom-call | flops 67108864 | bytes 1048576 | tf_op jit(solution)/shard_map/pallas_call | solution.py:26
  5.0 0.0 collective-permute-done.face_ref
  5.1 0.7 %shard_map.30 = (f32[5,3,8,128]{3,2,1,0:T(8,128)S(1)}, f32[5,3,8,128]{3,2,1,0:T(8,128)S(1)}, f32[5,3,8,128]{3,2,1,0:T(8,128)S(1)}, f32[5,3,8,128]{3,2,1,0:T(8,128)S(1)}) custom-call(f32[3,6,16,128]{3,2,1,0:T(8,128)S(1)} %collective-permute-done.face_ref, f32[6,2,3,3,2,8,128]{6,5,4,3,2,1,0:T(8,128)S(1)} %get-tuple-element.27.edges, ...), custom_call_target="tpu_custom_call" | custom-call | flops 4294967296 | bytes 1048576 | tf_op jit(solution)/shard_map/pallas_call | solution.py:26
  5.8 2.6 %collective-permute-start.2 = (f32[5,3,8,128]{3,2,1,0:T(8,128)S(1)}, f32[5,3,8,128]{3,2,1,0:T(8,128)S(1)}, u32[]{:S(2)}, u32[]{:S(2)}) collective-permute-start(f32[5,3,8,128]{3,2,1,0:T(8,128)S(1)} %get-tuple-element.34), channel_id=1, source_target_pairs={{0,12},{4,8},{8,4},{12,0},{16,28},{20,24},{24,20},{28,16},{1,13},{... | collective-permute-start | bytes 184328 | tf_op jit(solution)/shard_map/ppermute | solution.py:342
  8.4 0.4 %collective-permute-start.3 = (f32[5,3,8,128]{3,2,1,0:T(8,128)S(1)}, f32[5,3,8,128]{3,2,1,0:T(8,128)S(1)}, u32[]{:S(2)}, u32[]{:S(2)}) collective-permute-start(f32[5,3,8,128]{3,2,1,0:T(8,128)S(1)} %get-tuple-element.35), channel_id=1, source_target_pairs={{0,8},{4,12},{8,0},{12,4},{16,24},{20,28},{24,16},{28,20},{1,9},{5... | collective-permute-start | bytes 184328 | tf_op jit(solution)/shard_map/ppermute | solution.py:342
  8.8 0.5 %collective-permute-start.4 = (f32[5,3,8,128]{3,2,1,0:T(8,128)S(1)}, f32[5,3,8,128]{3,2,1,0:T(8,128)S(1)}, u32[]{:S(2)}, u32[]{:S(2)}) collective-permute-start(f32[5,3,8,128]{3,2,1,0:T(8,128)S(1)} %get-tuple-element.36), channel_id=1, source_target_pairs={{0,4},{4,0},{8,12},{12,8},{16,20},{20,16},{24,28},{28,24},{1,5},{5... | collective-permute-start | bytes 184328 | tf_op jit(solution)/shard_map/ppermute | solution.py:342
  9.3 0.0 collective-permute-done.1.face_ref
  9.3 0.7 %shard_map.31 = (f32[3,3,8,128]{3,2,1,0:T(8,128)S(1)}, f32[3,3,8,128]{3,2,1,0:T(8,128)S(1)}, f32[3,3,8,128]{3,2,1,0:T(8,128)S(1)}, f32[3,3,8,128]{3,2,1,0:T(8,128)S(1)}) custom-call(f32[3,6,16,128]{3,2,1,0:T(8,128)S(1)} %collective-permute-done.1.face_ref, f32[6,2,3,3,2,8,128]{6,5,4,3,2,1,0:T(8,128)S(1)} %get-tuple-element.27.edges, ...), custom_call_target="tpu_custom_call" | custom-call | flops 4294967296 | bytes 1048576 | tf_op jit(solution)/shard_map/pallas_call | solution.py:26
  10.0 2.6 %collective-permute-start.5 = (f32[3,3,8,128]{3,2,1,0:T(8,128)S(1)}, f32[3,3,8,128]{3,2,1,0:T(8,128)S(1)}, u32[]{:S(2)}, u32[]{:S(2)}) collective-permute-start(f32[3,3,8,128]{3,2,1,0:T(8,128)S(1)} %get-tuple-element.38), channel_id=1, source_target_pairs={{0,12},{4,8},{8,4},{12,0},{16,28},{20,24},{24,20},{28,16},{1,13},{... | collective-permute-start | bytes 110600 | tf_op jit(solution)/shard_map/ppermute | solution.py:342
  12.6 0.4 %collective-permute-start.6 = (f32[3,3,8,128]{3,2,1,0:T(8,128)S(1)}, f32[3,3,8,128]{3,2,1,0:T(8,128)S(1)}, u32[]{:S(2)}, u32[]{:S(2)}) collective-permute-start(f32[3,3,8,128]{3,2,1,0:T(8,128)S(1)} %get-tuple-element.39), channel_id=1, source_target_pairs={{0,8},{4,12},{8,0},{12,4},{16,24},{20,28},{24,16},{28,20},{1,9},{5... | collective-permute-start | bytes 110600 | tf_op jit(solution)/shard_map/ppermute | solution.py:342
  13.1 0.0 collective-permute-done.2.refs_1_.refs_2_
  13.1 0.5 %collective-permute-start.7 = (f32[3,3,8,128]{3,2,1,0:T(8,128)S(1)}, f32[3,3,8,128]{3,2,1,0:T(8,128)S(1)}, u32[]{:S(2)}, u32[]{:S(2)}) collective-permute-start(f32[3,3,8,128]{3,2,1,0:T(8,128)S(1)} %get-tuple-element.40), channel_id=1, source_target_pairs={{0,4},{4,0},{8,12},{12,8},{16,20},{20,16},{24,28},{28,24},{1,5},{5... | collective-permute-start | bytes 110600 | tf_op jit(solution)/shard_map/ppermute | solution.py:342
  13.6 0.0 collective-permute-done.3.refs_2_.refs_3_
  13.6 0.0 collective-permute-done.4.refs_3_.refs_4_
  13.7 1.4 %collective-permute-done.5.refs_1_.refs_6_ = f32[3,3,8,128]{3,2,1,0:T(8,128)S(1)} collective-permute-done((f32[3,3,8,128]{3,2,1,0:T(8,128)S(1)}, f32[3,3,8,128]{3,2,1,0:T(8,128)S(1)}, u32[]{:S(2)}, u32[]{:S(2)}) %collective-permute-start.5) | collective-permute-done | bytes 36896 | tf_op jit(solution)/shard_map/ppermute | solution.py:342
  15.1 1.5 %collective-permute-done.6.refs_2_.refs_7_ = f32[3,3,8,128]{3,2,1,0:T(8,128)S(1)} collective-permute-done((f32[3,3,8,128]{3,2,1,0:T(8,128)S(1)}, f32[3,3,8,128]{3,2,1,0:T(8,128)S(1)}, u32[]{:S(2)}, u32[]{:S(2)}) %collective-permute-start.6) | collective-permute-done | bytes 36896 | tf_op jit(solution)/shard_map/ppermute | solution.py:342
  16.6 0.5 %collective-permute-done.7.refs_3_.refs_8_ = f32[3,3,8,128]{3,2,1,0:T(8,128)S(1)} collective-permute-done((f32[3,3,8,128]{3,2,1,0:T(8,128)S(1)}, f32[3,3,8,128]{3,2,1,0:T(8,128)S(1)}, u32[]{:S(2)}, u32[]{:S(2)}) %collective-permute-start.7) | collective-permute-done | bytes 36896 | tf_op jit(solution)/shard_map/ppermute | solution.py:342
  17.1 2.7 %collective-permute-start.8 = (f32[8,3,8,128]{3,2,1,0:T(8,128)S(1)}, f32[8,3,8,128]{3,2,1,0:T(8,128)S(1)}, u32[]{:S(2)}, u32[]{:S(2)}) collective-permute-start(f32[8,3,8,128]{3,2,1,0:T(8,128)S(1)} %shard_map.33), channel_id=1, source_target_pairs={{0,16},{4,20},{8,24},{12,28},{16,0},{20,4},{24,8},{28,12},{1,17},{... | collective-permute-start | bytes 294920 | tf_op jit(solution)/shard_map/ppermute | solution.py:348
  19.7 2.9 %collective-permute-done.8.refs_0_ = f32[8,3,8,128]{3,2,1,0:T(8,128)S(1)} collective-permute-done((f32[8,3,8,128]{3,2,1,0:T(8,128)S(1)}, f32[8,3,8,128]{3,2,1,0:T(8,128)S(1)}, u32[]{:S(2)}, u32[]{:S(2)}) %collective-permute-start.8) | collective-permute-done | bytes 98336 | tf_op jit(solution)/shard_map/ppermute | solution.py:348
  22.7 0.1 shard_map.34
  22.8 1.8 %collective-permute-start.9 = (f32[8,3,8,128]{3,2,1,0:T(8,128)S(1)}, f32[8,3,8,128]{3,2,1,0:T(8,128)S(1)}, u32[]{:S(2)}, u32[]{:S(2)}) collective-permute-start(f32[8,3,8,128]{3,2,1,0:T(8,128)S(1)} %get-tuple-element.42), channel_id=1, source_target_pairs={{0,12},{4,8},{8,4},{12,0},{16,28},{20,24},{24,20},{28,16},{1,13},{... | collective-permute-start | bytes 294920 | tf_op jit(solution)/shard_map/ppermute | solution.py:342
  24.5 0.3 %collective-permute-start.10 = (f32[8,3,8,128]{3,2,1,0:T(8,128)S(1)}, f32[8,3,8,128]{3,2,1,0:T(8,128)S(1)}, u32[]{:S(2)}, u32[]{:S(2)}) collective-permute-start(f32[8,3,8,128]{3,2,1,0:T(8,128)S(1)} %get-tuple-element.43), channel_id=1, source_target_pairs={{0,8},{4,12},{8,0},{12,4},{16,24},{20,28},{24,16},{28,20},{1,9},{5... | collective-permute-start | bytes 294920 | tf_op jit(solution)/shard_map/ppermute | solution.py:342
  24.8 1.5 %collective-permute-start.11 = (f32[8,3,8,128]{3,2,1,0:T(8,128)S(1)}, f32[8,3,8,128]{3,2,1,0:T(8,128)S(1)}, u32[]{:S(2)}, u32[]{:S(2)}) collective-permute-start(f32[8,3,8,128]{3,2,1,0:T(8,128)S(1)} %get-tuple-element.44), channel_id=1, source_target_pairs={{0,4},{4,0},{8,12},{12,8},{16,20},{20,16},{24,28},{28,24},{1,5},{5... | collective-permute-start | bytes 294920 | tf_op jit(solution)/shard_map/ppermute | solution.py:342
  26.3 2.0 %collective-permute-done.9.refs_1_ = f32[8,3,8,128]{3,2,1,0:T(8,128)S(1)} collective-permute-done((f32[8,3,8,128]{3,2,1,0:T(8,128)S(1)}, f32[8,3,8,128]{3,2,1,0:T(8,128)S(1)}, u32[]{:S(2)}, u32[]{:S(2)}) %collective-permute-start.9) | collective-permute-done | bytes 98336 | tf_op jit(solution)/shard_map/ppermute | solution.py:342
  28.3 0.8 %shard_map.35.refs_4_ = f32[3,16,16,128]{3,2,1,0:T(8,128)} custom-call(f32[16,3,2,8,128]{4,3,2,1,0:T(8,128)S(1)} %get-tuple-element.46.kept), custom_call_target="tpu_custom_call" | custom-call | flops 4294967296 | bytes 1048576 | tf_op jit(solution)/shard_map/pallas_call | solution.py:407
  29.1 0.0 collective-permute-done.10.refs_2_
  29.1 0.3 %collective-permute-done.11.refs_3_ = f32[8,3,8,128]{3,2,1,0:T(8,128)S(1)} collective-permute-done((f32[8,3,8,128]{3,2,1,0:T(8,128)S(1)}, f32[8,3,8,128]{3,2,1,0:T(8,128)S(1)}, u32[]{:S(2)}, u32[]{:S(2)}) %collective-permute-start.11) | collective-permute-done | bytes 98336 | tf_op jit(solution)/shard_map/ppermute | solution.py:342
  (5 shorter events, 0.1 us)
Async XLA Ops:
  0.0 1.0 %copy-start = (f32[1,3,16,16,128]{4,3,2,1,0:T(8,128)S(1)}, f32[1,3,16,16,128]{4,3,2,1,0:T(8,128)}, u32[]{:S(2)}) copy-start(f32[1,3,16,16,128]{4,3,2,1,0:T(8,128)} %param.2) | copy-start | bytes 1179652
  1.0 3.2 %copy-start.1 = (f32[16,16,128]{2,1,0:T(8,128)S(1)}, f32[16,16,128]{2,1,0:T(8,128)}, u32[]{:S(2)}) copy-start(f32[16,16,128]{2,1,0:T(8,128)} %rate_ref.1) | copy-start | bytes 393220
  1.0 4.0 %collective-permute-start = (f32[3,6,16,128]{3,2,1,0:T(8,128)S(1)}, f32[3,6,16,128]{3,2,1,0:T(8,128)S(1)}, u32[]{:S(2)}, u32[]{:S(2)}) collective-permute-start(f32[3,6,16,128]{3,2,1,0:T(8,128)S(1)} %get-tuple-element.26), channel_id=1, source_target_pairs={{0,1},{1,0},{2,3},{3,2},{4,5},{5,4},{6,7},{7,6},{8,9},{9,8},{10,11... | collective-permute-start | bytes 442376 | tf_op jit(solution)/shard_map/ppermute | solution.py:338
  1.5 7.8 %collective-permute-start.1 = (f32[3,6,16,128]{3,2,1,0:T(8,128)S(1)}, f32[3,6,16,128]{3,2,1,0:T(8,128)S(1)}, u32[]{:S(2)}, u32[]{:S(2)}) collective-permute-start(f32[3,6,16,128]{3,2,1,0:T(8,128)S(1)} %get-tuple-element.31), channel_id=1, source_target_pairs={{0,3},{1,2},{2,1},{3,0},{4,7},{5,6},{6,5},{7,4},{8,11},{9,10},{10,... | collective-permute-start | bytes 442376 | tf_op jit(solution)/shard_map/ppermute | solution.py:338
  5.8 7.3 %collective-permute-start.2 = (f32[5,3,8,128]{3,2,1,0:T(8,128)S(1)}, f32[5,3,8,128]{3,2,1,0:T(8,128)S(1)}, u32[]{:S(2)}, u32[]{:S(2)}) collective-permute-start(f32[5,3,8,128]{3,2,1,0:T(8,128)S(1)} %get-tuple-element.34), channel_id=1, source_target_pairs={{0,12},{4,8},{8,4},{12,0},{16,28},{20,24},{24,20},{28,16},{1,13},{... | collective-permute-start | bytes 184328 | tf_op jit(solution)/shard_map/ppermute | solution.py:342
  8.4 5.3 %collective-permute-start.3 = (f32[5,3,8,128]{3,2,1,0:T(8,128)S(1)}, f32[5,3,8,128]{3,2,1,0:T(8,128)S(1)}, u32[]{:S(2)}, u32[]{:S(2)}) collective-permute-start(f32[5,3,8,128]{3,2,1,0:T(8,128)S(1)} %get-tuple-element.35), channel_id=1, source_target_pairs={{0,8},{4,12},{8,0},{12,4},{16,24},{20,28},{24,16},{28,20},{1,9},{5... | collective-permute-start | bytes 184328 | tf_op jit(solution)/shard_map/ppermute | solution.py:342
  8.8 4.8 %collective-permute-start.4 = (f32[5,3,8,128]{3,2,1,0:T(8,128)S(1)}, f32[5,3,8,128]{3,2,1,0:T(8,128)S(1)}, u32[]{:S(2)}, u32[]{:S(2)}) collective-permute-start(f32[5,3,8,128]{3,2,1,0:T(8,128)S(1)} %get-tuple-element.36), channel_id=1, source_target_pairs={{0,4},{4,0},{8,12},{12,8},{16,20},{20,16},{24,28},{28,24},{1,5},{5... | collective-permute-start | bytes 184328 | tf_op jit(solution)/shard_map/ppermute | solution.py:342
  10.0 5.0 %collective-permute-start.5 = (f32[3,3,8,128]{3,2,1,0:T(8,128)S(1)}, f32[3,3,8,128]{3,2,1,0:T(8,128)S(1)}, u32[]{:S(2)}, u32[]{:S(2)}) collective-permute-start(f32[3,3,8,128]{3,2,1,0:T(8,128)S(1)} %get-tuple-element.38), channel_id=1, source_target_pairs={{0,12},{4,8},{8,4},{12,0},{16,28},{20,24},{24,20},{28,16},{1,13},{... | collective-permute-start | bytes 110600 | tf_op jit(solution)/shard_map/ppermute | solution.py:342
  12.6 4.0 %collective-permute-start.6 = (f32[3,3,8,128]{3,2,1,0:T(8,128)S(1)}, f32[3,3,8,128]{3,2,1,0:T(8,128)S(1)}, u32[]{:S(2)}, u32[]{:S(2)}) collective-permute-start(f32[3,3,8,128]{3,2,1,0:T(8,128)S(1)} %get-tuple-element.39), channel_id=1, source_target_pairs={{0,8},{4,12},{8,0},{12,4},{16,24},{20,28},{24,16},{28,20},{1,9},{5... | collective-permute-start | bytes 110600 | tf_op jit(solution)/shard_map/ppermute | solution.py:342
  13.1 4.0 %collective-permute-start.7 = (f32[3,3,8,128]{3,2,1,0:T(8,128)S(1)}, f32[3,3,8,128]{3,2,1,0:T(8,128)S(1)}, u32[]{:S(2)}, u32[]{:S(2)}) collective-permute-start(f32[3,3,8,128]{3,2,1,0:T(8,128)S(1)} %get-tuple-element.40), channel_id=1, source_target_pairs={{0,4},{4,0},{8,12},{12,8},{16,20},{20,16},{24,28},{28,24},{1,5},{5... | collective-permute-start | bytes 110600 | tf_op jit(solution)/shard_map/ppermute | solution.py:342
  17.1 5.6 %collective-permute-start.8 = (f32[8,3,8,128]{3,2,1,0:T(8,128)S(1)}, f32[8,3,8,128]{3,2,1,0:T(8,128)S(1)}, u32[]{:S(2)}, u32[]{:S(2)}) collective-permute-start(f32[8,3,8,128]{3,2,1,0:T(8,128)S(1)} %shard_map.33), channel_id=1, source_target_pairs={{0,16},{4,20},{8,24},{12,28},{16,0},{20,4},{24,8},{28,12},{1,17},{... | collective-permute-start | bytes 294920 | tf_op jit(solution)/shard_map/ppermute | solution.py:348
  22.8 5.6 %collective-permute-start.9 = (f32[8,3,8,128]{3,2,1,0:T(8,128)S(1)}, f32[8,3,8,128]{3,2,1,0:T(8,128)S(1)}, u32[]{:S(2)}, u32[]{:S(2)}) collective-permute-start(f32[8,3,8,128]{3,2,1,0:T(8,128)S(1)} %get-tuple-element.42), channel_id=1, source_target_pairs={{0,12},{4,8},{8,4},{12,0},{16,28},{20,24},{24,20},{28,16},{1,13},{... | collective-permute-start | bytes 294920 | tf_op jit(solution)/shard_map/ppermute | solution.py:342
  24.5 4.6 %collective-permute-start.10 = (f32[8,3,8,128]{3,2,1,0:T(8,128)S(1)}, f32[8,3,8,128]{3,2,1,0:T(8,128)S(1)}, u32[]{:S(2)}, u32[]{:S(2)}) collective-permute-start(f32[8,3,8,128]{3,2,1,0:T(8,128)S(1)} %get-tuple-element.43), channel_id=1, source_target_pairs={{0,8},{4,12},{8,0},{12,4},{16,24},{20,28},{24,16},{28,20},{1,9},{5... | collective-permute-start | bytes 294920 | tf_op jit(solution)/shard_map/ppermute | solution.py:342
  24.8 4.6 %collective-permute-start.11 = (f32[8,3,8,128]{3,2,1,0:T(8,128)S(1)}, f32[8,3,8,128]{3,2,1,0:T(8,128)S(1)}, u32[]{:S(2)}, u32[]{:S(2)}) collective-permute-start(f32[8,3,8,128]{3,2,1,0:T(8,128)S(1)} %get-tuple-element.44), channel_id=1, source_target_pairs={{0,4},{4,0},{8,12},{12,8},{16,20},{20,16},{24,28},{28,24},{1,5},{5... | collective-permute-start | bytes 294920 | tf_op jit(solution)/shard_map/ppermute | solution.py:342

commit v5 on v3

--- a/solution.py
+++ b/solution.py
@@ -110,12 +110,19 @@
     return [[new[c][odd] + beta * base[c][odd] for odd in (0, 1)] for c in range(3)]
 
 
-def faces_kernel(own_ref, far_ref, near_ref):
+def faces_kernel(own_ref, far_ref, near_ref, sems):
     layers, width = own_ref.shape[1], near_ref.shape[1]
     near = near_side()
     top = layers - width
-    far_ref[...] = own_ref[:, pl.ds((1 - near) * top, width)]
-    near_ref[...] = own_ref[:, pl.ds(near * top, width)]
+    copies = [
+        pltpu.make_async_copy(own_ref.at[c, pl.ds(start, width)], ref.at[c], sems.at[c, j])
+        for j, (ref, start) in enumerate(((near_ref, near * top), (far_ref, (1 - near) * top)))
+        for c in range(3)
+    ]
+    for copy in copies:
+        copy.start()
+    for copy in copies:
+        copy.wait()
 
 
 def inside_kernel(own_ref, rate_ref, edges, middle, faded, early_damp, late_damp, kept, damps, inner, *fields):
@@ -323,7 +330,14 @@
         step = distance * GROUP
         return lax.ppermute(value, "tm", [(i, (i + step) % slices) for i in range(slices)])
 
-    far_face, near_face = call(faces_kernel, [face, face], own)
+    far_face, near_face = pl.pallas_call(
+        faces_kernel,
+        out_shape=[face, face],
+        in_specs=[ANY],
+        out_specs=[ANY, ANY],
+        scratch_shapes=[pltpu.SemaphoreType.DMA((3, 2))],
+        compiler_params=pltpu.CompilerParams(vmem_limit_bytes=60 << 20),
+    )(own)
     near_face = halo(near_face, [(i, i ^ 1) for i in range(slabs)])
     far_face = halo(far_face, [(i, i + 1 if i % 2 else i - 1 + slabs) for i in range(slabs)])
     row = (rows // 2, width)

time: 29.9 us -> 39.9 us (1.33)
  Pallas kernels: 3.27 us -> 13.3 us
    pallas_call x0 -> x1, Pallas kernels: none -> 10.1 us  [shards(): pl.pallas_call(faces_kernel, out_shape=[face, face], in_specs=[ANY], out_...]
    pallas_call x8 -> x7, Pallas kernels: 2.48 us -> 2.46 us  [call(): pl.pallas_call(kernel, out_shape=out_shape, in_specs=[VMEM] * len(args),...]
  transfers between devices with their start and end apart: 16 -> 16, of which waited for: 5 -> 5; matrix products, arithmetic and copies ran while one was open for 0% -> 0% of each run, Pallas kernels for 11% -> 8%
where the time goes in v5:
time: 39.9 us; the launch traced here: 39.8 us
  starting transfers between devices  22.7 us (57%)
  Pallas kernels  13.3 us (33%)
  waiting for transfers between devices  2.74 us (7%)
  local copies, waits for them, and re-layouts  0.91 us (2%)
    ppermute x12, starting transfers between devices, swap(): lax.ppermute(parts[k], 'tm', [(i, i ^ partner(k)) for i in range(slices)])  14.2 us
    pallas_call x1, Pallas kernels, shards(): pl.pallas_call(faces_kernel, out_shape=[face, face], in_specs=[ANY], out_...  10.1 us
    ppermute x2, starting transfers between devices, onward(): lax.ppermute(value, 'tm', [(i, (i + step) % slices) for i in range(slices)])  5.31 us
    ppermute x2, starting transfers between devices, halo(): return lax.ppermute(value, 'gz', [(i, j % slabs) for i, j in pairs])  3.16 us
    ppermute x12, waiting for transfers between devices, swap(): lax.ppermute(parts[k], 'tm', [(i, i ^ partner(k)) for i in range(slices)])  2.73 us
    pallas_call x7, Pallas kernels, call(): pl.pallas_call(kernel, out_shape=out_shape, in_specs=[VMEM] * len(args),...  2.46 us
    unnamed x4, local copies, waits for them, and re-layouts  0.91 us
  transfers between devices with their start and end apart: 16, of which 5 were waited for; matrix products, arithmetic and copies ran while one was open for 0% of the time, Pallas kernels for 8%

profile of v5, /device:TPU:0, one launch (start us, length us, event | category | flops | bytes accessed | tf_op | source)
XLA Modules:
  0.0 39.8 jit_solution(10959453526718710757)
XLA Ops:
  0.0 10.1 %shard_map.29 = (f32[3,6,16,128]{3,2,1,0:T(8,128)}, f32[3,6,16,128]{3,2,1,0:T(8,128)}) custom-call(f32[3,16,16,128]{3,2,1,0:T(8,128)} %bitcast.2), custom_call_target="tpu_custom_call" | custom-call | tf_op jit(solution)/shard_map/pallas_call | solution.py:333
  10.1 0.5 %collective-permute-start.1 = (f32[3,6,16,128]{3,2,1,0:T(8,128)}, f32[3,6,16,128]{3,2,1,0:T(8,128)S(1)}, u32[]{:S(2)}, u32[]{:S(2)}) collective-permute-start(f32[3,6,16,128]{3,2,1,0:T(8,128)} %get-tuple-element.38), channel_id=1, source_target_pairs={{0,1},{1,0},{2,3},{3,2},{4,5},{5,4},{6,7},{7,6},{8,9},{9,8},{10,11... | collective-permute-start | bytes 442376 | tf_op jit(solution)/shard_map/ppermute | solution.py:321
  10.6 2.6 %collective-permute-start = (f32[3,6,16,128]{3,2,1,0:T(8,128)}, f32[3,6,16,128]{3,2,1,0:T(8,128)S(1)}, u32[]{:S(2)}, u32[]{:S(2)}) collective-permute-start(f32[3,6,16,128]{3,2,1,0:T(8,128)} %get-tuple-element.33), channel_id=1, source_target_pairs={{0,3},{1,2},{2,1},{3,0},{4,7},{5,6},{6,5},{7,4},{8,11},{9,10},{10,... | collective-permute-start | bytes 442376 | tf_op jit(solution)/shard_map/ppermute | solution.py:321
  13.3 0.9 %copy-done.1 = f32[16,16,128]{2,1,0:T(8,128)S(1)} copy-done((f32[16,16,128]{2,1,0:T(8,128)S(1)}, f32[16,16,128]{2,1,0:T(8,128)}, u32[]{:S(2)}) %copy-start.1) | copy-done | bytes 131096
  14.2 0.8 %shard_map.28 = (f32[6,2,3,3,2,8,128]{6,5,4,3,2,1,0:T(8,128)S(1)}, f32[4,3,2,8,128]{4,3,2,1,0:T(8,128)S(1)}, f32[2,6,3,2,8,128]{5,4,3,2,1,0:T(8,128)S(1)}, f32[5...) custom-call(f32[3,16,16,128]{3,2,1,0:T(8,128)S(1)} %bitcast.3, ...), custom_call_target="tpu_custom_call" | custom-call | flops 67108864 | bytes 1048576 | tf_op jit(solution)/shard_map/pallas_call | solution.py:26
  15.0 0.0 collective-permute-done.1.face_ref
  15.0 0.7 %shard_map.31 = (f32[5,3,8,128]{3,2,1,0:T(8,128)S(1)}, f32[5,3,8,128]{3,2,1,0:T(8,128)S(1)}, f32[5,3,8,128]{3,2,1,0:T(8,128)S(1)}, f32[5,3,8,128]{3,2,1,0:T(8,128)S(1)}) custom-call(f32[3,6,16,128]{3,2,1,0:T(8,128)S(1)} %collective-permute-done.1.face_ref, f32[6,2,3,3,2,8,128]{6,5,4,3,2,1,0:T(8,128)S(1)} %get-tuple-element.34.edges, ...), custom_call_target="tpu_custom_call" | custom-call | flops 4294967296 | bytes 1048576 | tf_op jit(solution)/shard_map/pallas_call | solution.py:26
  15.8 2.6 %collective-permute-start.2 = (f32[5,3,8,128]{3,2,1,0:T(8,128)S(1)}, f32[5,3,8,128]{3,2,1,0:T(8,128)S(1)}, u32[]{:S(2)}, u32[]{:S(2)}) collective-permute-start(f32[5,3,8,128]{3,2,1,0:T(8,128)S(1)} %get-tuple-element.41), channel_id=1, source_target_pairs={{0,12},{4,8},{8,4},{12,0},{16,28},{20,24},{24,20},{28,16},{1,13},{... | collective-permute-start | bytes 184328 | tf_op jit(solution)/shard_map/ppermute | solution.py:325
  18.3 0.4 %collective-permute-start.3 = (f32[5,3,8,128]{3,2,1,0:T(8,128)S(1)}, f32[5,3,8,128]{3,2,1,0:T(8,128)S(1)}, u32[]{:S(2)}, u32[]{:S(2)}) collective-permute-start(f32[5,3,8,128]{3,2,1,0:T(8,128)S(1)} %get-tuple-element.42), channel_id=1, source_target_pairs={{0,8},{4,12},{8,0},{12,4},{16,24},{20,28},{24,16},{28,20},{1,9},{5... | collective-permute-start | bytes 184328 | tf_op jit(solution)/shard_map/ppermute | solution.py:325
  18.8 0.5 %collective-permute-start.4 = (f32[5,3,8,128]{3,2,1,0:T(8,128)S(1)}, f32[5,3,8,128]{3,2,1,0:T(8,128)S(1)}, u32[]{:S(2)}, u32[]{:S(2)}) collective-permute-start(f32[5,3,8,128]{3,2,1,0:T(8,128)S(1)} %get-tuple-element.43), channel_id=1, source_target_pairs={{0,4},{4,0},{8,12},{12,8},{16,20},{20,16},{24,28},{28,24},{1,5},{5... | collective-permute-start | bytes 184328 | tf_op jit(solution)/shard_map/ppermute | solution.py:325
  19.3 0.0 collective-permute-done.face_ref
  19.3 0.7 %shard_map.30 = (f32[3,3,8,128]{3,2,1,0:T(8,128)S(1)}, f32[3,3,8,128]{3,2,1,0:T(8,128)S(1)}, f32[3,3,8,128]{3,2,1,0:T(8,128)S(1)}, f32[3,3,8,128]{3,2,1,0:T(8,128)S(1)}) custom-call(f32[3,6,16,128]{3,2,1,0:T(8,128)S(1)} %collective-permute-done.face_ref, f32[6,2,3,3,2,8,128]{6,5,4,3,2,1,0:T(8,128)S(1)} %get-tuple-element.34.edges, ...), custom_call_target="tpu_custom_call" | custom-call | flops 4294967296 | bytes 1048576 | tf_op jit(solution)/shard_map/pallas_call | solution.py:26
  20.0 2.6 %collective-permute-start.5 = (f32[3,3,8,128]{3,2,1,0:T(8,128)S(1)}, f32[3,3,8,128]{3,2,1,0:T(8,128)S(1)}, u32[]{:S(2)}, u32[]{:S(2)}) collective-permute-start(f32[3,3,8,128]{3,2,1,0:T(8,128)S(1)} %get-tuple-element.46), channel_id=1, source_target_pairs={{0,12},{4,8},{8,4},{12,0},{16,28},{20,24},{24,20},{28,16},{1,13},{... | collective-permute-start | bytes 110600 | tf_op jit(solution)/shard_map/ppermute | solution.py:325
  22.6 0.4 %collective-permute-start.6 = (f32[3,3,8,128]{3,2,1,0:T(8,128)S(1)}, f32[3,3,8,128]{3,2,1,0:T(8,128)S(1)}, u32[]{:S(2)}, u32[]{:S(2)}) collective-permute-start(f32[3,3,8,128]{3,2,1,0:T(8,128)S(1)} %get-tuple-element.47), channel_id=1, source_target_pairs={{0,8},{4,12},{8,0},{12,4},{16,24},{20,28},{24,16},{28,20},{1,9},{5... | collective-permute-start | bytes 110600 | tf_op jit(solution)/shard_map/ppermute | solution.py:325
  23.0 0.0 collective-permute-done.2.refs_1_.refs_2_
  23.0 0.5 %collective-permute-start.7 = (f32[3,3,8,128]{3,2,1,0:T(8,128)S(1)}, f32[3,3,8,128]{3,2,1,0:T(8,128)S(1)}, u32[]{:S(2)}, u32[]{:S(2)}) collective-permute-start(f32[3,3,8,128]{3,2,1,0:T(8,128)S(1)} %get-tuple-element.48), channel_id=1, source_target_pairs={{0,4},{4,0},{8,12},{12,8},{16,20},{20,16},{24,28},{28,24},{1,5},{5... | collective-permute-start | bytes 110600 | tf_op jit(solution)/shard_map/ppermute | solution.py:325
  23.6 0.1 shard_map.32
  23.6 2.7 %collective-permute-start.9 = (f32[5,3,8,128]{3,2,1,0:T(8,128)S(1)}, f32[5,3,8,128]{3,2,1,0:T(8,128)S(1)}, u32[]{:S(2)}, u32[]{:S(2)}) collective-permute-start(f32[5,3,8,128]{3,2,1,0:T(8,128)S(1)} %shard_map.32), channel_id=1, source_target_pairs={{0,16},{4,20},{8,24},{12,28},{16,0},{20,4},{24,8},{28,12},{1,17},{... | collective-permute-start | bytes 184328 | tf_op jit(solution)/shard_map/ppermute | solution.py:331
  26.3 0.3 collective-permute-done.6.refs_2_.refs_3_
  26.6 0.4 collective-permute-done.7.refs_3_.refs_4_
  27.0 2.7 %collective-permute-start.8 = (f32[3,3,8,128]{3,2,1,0:T(8,128)S(1)}, f32[3,3,8,128]{3,2,1,0:T(8,128)S(1)}, u32[]{:S(2)}, u32[]{:S(2)}) collective-permute-start(f32[3,3,8,128]{3,2,1,0:T(8,128)S(1)} %shard_map.33), channel_id=1, source_target_pairs={{0,16},{4,20},{8,24},{12,28},{16,0},{20,4},{24,8},{28,12},{1,17},{... | collective-permute-start | bytes 110600 | tf_op jit(solution)/shard_map/ppermute | solution.py:331
  29.7 0.1 shard_map.34
  29.8 2.0 %collective-permute-start.13 = (f32[5,3,8,128]{3,2,1,0:T(8,128)S(1)}, f32[5,3,8,128]{3,2,1,0:T(8,128)S(1)}, u32[]{:S(2)}, u32[]{:S(2)}) collective-permute-start(f32[5,3,8,128]{3,2,1,0:T(8,128)S(1)} %get-tuple-element.56), channel_id=1, source_target_pairs={{0,12},{4,8},{8,4},{12,0},{16,28},{20,24},{24,20},{28,16},{1,13},{... | collective-permute-start | bytes 184328 | tf_op jit(solution)/shard_map/ppermute | solution.py:325
  31.8 0.4 %collective-permute-start.14 = (f32[5,3,8,128]{3,2,1,0:T(8,128)S(1)}, f32[5,3,8,128]{3,2,1,0:T(8,128)S(1)}, u32[]{:S(2)}, u32[]{:S(2)}) collective-permute-start(f32[5,3,8,128]{3,2,1,0:T(8,128)S(1)} %get-tuple-element.57), channel_id=1, source_target_pairs={{0,8},{4,12},{8,0},{12,4},{16,24},{20,28},{24,16},{28,20},{1,9},{5... | collective-permute-start | bytes 184328 | tf_op jit(solution)/shard_map/ppermute | solution.py:325
  32.2 1.2 %collective-permute-start.15 = (f32[5,3,8,128]{3,2,1,0:T(8,128)S(1)}, f32[5,3,8,128]{3,2,1,0:T(8,128)S(1)}, u32[]{:S(2)}, u32[]{:S(2)}) collective-permute-start(f32[5,3,8,128]{3,2,1,0:T(8,128)S(1)} %get-tuple-element.58), channel_id=1, source_target_pairs={{0,4},{4,0},{8,12},{12,8},{16,20},{20,16},{24,28},{28,24},{1,5},{5... | collective-permute-start | bytes 184328 | tf_op jit(solution)/shard_map/ppermute | solution.py:325
  33.4 2.0 %collective-permute-start.10 = (f32[3,3,8,128]{3,2,1,0:T(8,128)S(1)}, f32[3,3,8,128]{3,2,1,0:T(8,128)S(1)}, u32[]{:S(2)}, u32[]{:S(2)}) collective-permute-start(f32[3,3,8,128]{3,2,1,0:T(8,128)S(1)} %get-tuple-element.53), channel_id=1, source_target_pairs={{0,12},{4,8},{8,4},{12,0},{16,28},{20,24},{24,20},{28,16},{1,13},{... | collective-permute-start | bytes 110600 | tf_op jit(solution)/shard_map/ppermute | solution.py:325
  35.4 0.4 %collective-permute-start.11 = (f32[3,3,8,128]{3,2,1,0:T(8,128)S(1)}, f32[3,3,8,128]{3,2,1,0:T(8,128)S(1)}, u32[]{:S(2)}, u32[]{:S(2)}) collective-permute-start(f32[3,3,8,128]{3,2,1,0:T(8,128)S(1)} %get-tuple-element.54), channel_id=1, source_target_pairs={{0,8},{4,12},{8,0},{12,4},{16,24},{20,28},{24,16},{28,20},{1,9},{5... | collective-permute-start | bytes 110600 | tf_op jit(solution)/shard_map/ppermute | solution.py:325
  35.8 1.2 %collective-permute-start.12 = (f32[3,3,8,128]{3,2,1,0:T(8,128)S(1)}, f32[3,3,8,128]{3,2,1,0:T(8,128)S(1)}, u32[]{:S(2)}, u32[]{:S(2)}) collective-permute-start(f32[3,3,8,128]{3,2,1,0:T(8,128)S(1)} %get-tuple-element.55), channel_id=1, source_target_pairs={{0,4},{4,0},{8,12},{12,8},{16,20},{20,16},{24,28},{28,24},{1,5},{5... | collective-permute-start | bytes 110600 | tf_op jit(solution)/shard_map/ppermute | solution.py:325
  36.9 0.8 %shard_map.36.refs_4_ = f32[3,16,16,128]{3,2,1,0:T(8,128)} custom-call(f32[16,3,2,8,128]{4,3,2,1,0:T(8,128)S(1)} %get-tuple-element.32.kept, f32[5,3,8,128]{3,2,1,0:T(8,128)S(1)} %get-tuple-element.50.refs_0_, f32[5,3,8,128]{3,2,1,0:T(8,128)S(1)} %collective-permute-done.13.refs_1_, f32[5,3,8,128]{3,2,1,0:T(8,128)S(1)} %collective-permute-done.14.refs_2_, ...), custom_call_target="tpu_custom_call" | custom-call | flops 4294967296 | bytes 1048576 | tf_op jit(solution)/shard_map/pallas_call | solution.py:405
  37.7 0.6 %collective-permute-done.10.refs_1_ = f32[3,3,8,128]{3,2,1,0:T(8,128)S(1)} collective-permute-done((f32[3,3,8,128]{3,2,1,0:T(8,128)S(1)}, f32[3,3,8,128]{3,2,1,0:T(8,128)S(1)}, u32[]{:S(2)}, u32[]{:S(2)}) %collective-permute-start.10) | collective-permute-done | bytes 36896 | tf_op jit(solution)/shard_map/ppermute | solution.py:325
  38.3 1.0 %collective-permute-done.11.refs_2_ = f32[3,3,8,128]{3,2,1,0:T(8,128)S(1)} collective-permute-done((f32[3,3,8,128]{3,2,1,0:T(8,128)S(1)}, f32[3,3,8,128]{3,2,1,0:T(8,128)S(1)}, u32[]{:S(2)}, u32[]{:S(2)}) %collective-permute-start.11) | collective-permute-done | bytes 36896 | tf_op jit(solution)/shard_map/ppermute | solution.py:325
  39.3 0.4 %collective-permute-done.12.refs_3_ = f32[3,3,8,128]{3,2,1,0:T(8,128)S(1)} collective-permute-done((f32[3,3,8,128]{3,2,1,0:T(8,128)S(1)}, f32[3,3,8,128]{3,2,1,0:T(8,128)S(1)}, u32[]{:S(2)}, u32[]{:S(2)}) %collective-permute-start.12) | collective-permute-done | bytes 36896 | tf_op jit(solution)/shard_map/ppermute | solution.py:325
  (14 shorter events, 0.1 us)
Async XLA Ops:
  0.0 13.3 %copy-start = (f32[1,3,16,16,128]{4,3,2,1,0:T(8,128)S(1)}, f32[1,3,16,16,128]{4,3,2,1,0:T(8,128)}, u32[]{:S(2)}) copy-start(f32[1,3,16,16,128]{4,3,2,1,0:T(8,128)} %param.2) | copy-start | bytes 1179652
  10.1 4.9 %collective-permute-start.1 = (f32[3,6,16,128]{3,2,1,0:T(8,128)}, f32[3,6,16,128]{3,2,1,0:T(8,128)S(1)}, u32[]{:S(2)}, u32[]{:S(2)}) collective-permute-start(f32[3,6,16,128]{3,2,1,0:T(8,128)} %get-tuple-element.38), channel_id=1, source_target_pairs={{0,1},{1,0},{2,3},{3,2},{4,5},{5,4},{6,7},{7,6},{8,9},{9,8},{10,11... | collective-permute-start | bytes 442376 | tf_op jit(solution)/shard_map/ppermute | solution.py:321
  10.6 8.7 %collective-permute-start = (f32[3,6,16,128]{3,2,1,0:T(8,128)}, f32[3,6,16,128]{3,2,1,0:T(8,128)S(1)}, u32[]{:S(2)}, u32[]{:S(2)}) collective-permute-start(f32[3,6,16,128]{3,2,1,0:T(8,128)} %get-tuple-element.33), channel_id=1, source_target_pairs={{0,3},{1,2},{2,1},{3,0},{4,7},{5,6},{6,5},{7,4},{8,11},{9,10},{10,... | collective-permute-start | bytes 442376 | tf_op jit(solution)/shard_map/ppermute | solution.py:321
  13.3 0.9 %copy-start.1 = (f32[16,16,128]{2,1,0:T(8,128)S(1)}, f32[16,16,128]{2,1,0:T(8,128)}, u32[]{:S(2)}) copy-start(f32[16,16,128]{2,1,0:T(8,128)} %rate_ref.1) | copy-start | bytes 393220
  15.8 7.3 %collective-permute-start.2 = (f32[5,3,8,128]{3,2,1,0:T(8,128)S(1)}, f32[5,3,8,128]{3,2,1,0:T(8,128)S(1)}, u32[]{:S(2)}, u32[]{:S(2)}) collective-permute-start(f32[5,3,8,128]{3,2,1,0:T(8,128)S(1)} %get-tuple-element.41), channel_id=1, source_target_pairs={{0,12},{4,8},{8,4},{12,0},{16,28},{20,24},{24,20},{28,16},{1,13},{... | collective-permute-start | bytes 184328 | tf_op jit(solution)/shard_map/ppermute | solution.py:325
  18.3 5.3 %collective-permute-start.3 = (f32[5,3,8,128]{3,2,1,0:T(8,128)S(1)}, f32[5,3,8,128]{3,2,1,0:T(8,128)S(1)}, u32[]{:S(2)}, u32[]{:S(2)}) collective-permute-start(f32[5,3,8,128]{3,2,1,0:T(8,128)S(1)} %get-tuple-element.42), channel_id=1, source_target_pairs={{0,8},{4,12},{8,0},{12,4},{16,24},{20,28},{24,16},{28,20},{1,9},{5... | collective-permute-start | bytes 184328 | tf_op jit(solution)/shard_map/ppermute | solution.py:325
  18.8 4.8 %collective-permute-start.4 = (f32[5,3,8,128]{3,2,1,0:T(8,128)S(1)}, f32[5,3,8,128]{3,2,1,0:T(8,128)S(1)}, u32[]{:S(2)}, u32[]{:S(2)}) collective-permute-start(f32[5,3,8,128]{3,2,1,0:T(8,128)S(1)} %get-tuple-element.43), channel_id=1, source_target_pairs={{0,4},{4,0},{8,12},{12,8},{16,20},{20,16},{24,28},{28,24},{1,5},{5... | collective-permute-start | bytes 184328 | tf_op jit(solution)/shard_map/ppermute | solution.py:325
  20.0 6.3 %collective-permute-start.5 = (f32[3,3,8,128]{3,2,1,0:T(8,128)S(1)}, f32[3,3,8,128]{3,2,1,0:T(8,128)S(1)}, u32[]{:S(2)}, u32[]{:S(2)}) collective-permute-start(f32[3,3,8,128]{3,2,1,0:T(8,128)S(1)} %get-tuple-element.46), channel_id=1, source_target_pairs={{0,12},{4,8},{8,4},{12,0},{16,28},{20,24},{24,20},{28,16},{1,13},{... | collective-permute-start | bytes 110600 | tf_op jit(solution)/shard_map/ppermute | solution.py:325
  22.6 4.0 %collective-permute-start.6 = (f32[3,3,8,128]{3,2,1,0:T(8,128)S(1)}, f32[3,3,8,128]{3,2,1,0:T(8,128)S(1)}, u32[]{:S(2)}, u32[]{:S(2)}) collective-permute-start(f32[3,3,8,128]{3,2,1,0:T(8,128)S(1)} %get-tuple-element.47), channel_id=1, source_target_pairs={{0,8},{4,12},{8,0},{12,4},{16,24},{20,28},{24,16},{28,20},{1,9},{5... | collective-permute-start | bytes 110600 | tf_op jit(solution)/shard_map/ppermute | solution.py:325
  23.0 4.0 %collective-permute-start.7 = (f32[3,3,8,128]{3,2,1,0:T(8,128)S(1)}, f32[3,3,8,128]{3,2,1,0:T(8,128)S(1)}, u32[]{:S(2)}, u32[]{:S(2)}) collective-permute-start(f32[3,3,8,128]{3,2,1,0:T(8,128)S(1)} %get-tuple-element.48), channel_id=1, source_target_pairs={{0,4},{4,0},{8,12},{12,8},{16,20},{20,16},{24,28},{28,24},{1,5},{5... | collective-permute-start | bytes 110600 | tf_op jit(solution)/shard_map/ppermute | solution.py:325
  23.6 6.1 %collective-permute-start.9 = (f32[5,3,8,128]{3,2,1,0:T(8,128)S(1)}, f32[5,3,8,128]{3,2,1,0:T(8,128)S(1)}, u32[]{:S(2)}, u32[]{:S(2)}) collective-permute-start(f32[5,3,8,128]{3,2,1,0:T(8,128)S(1)} %shard_map.32), channel_id=1, source_target_pairs={{0,16},{4,20},{8,24},{12,28},{16,0},{20,4},{24,8},{28,12},{1,17},{... | collective-permute-start | bytes 184328 | tf_op jit(solution)/shard_map/ppermute | solution.py:331
  27.0 6.3 %collective-permute-start.8 = (f32[3,3,8,128]{3,2,1,0:T(8,128)S(1)}, f32[3,3,8,128]{3,2,1,0:T(8,128)S(1)}, u32[]{:S(2)}, u32[]{:S(2)}) collective-permute-start(f32[3,3,8,128]{3,2,1,0:T(8,128)S(1)} %shard_map.33), channel_id=1, source_target_pairs={{0,16},{4,20},{8,24},{12,28},{16,0},{20,4},{24,8},{28,12},{1,17},{... | collective-permute-start | bytes 110600 | tf_op jit(solution)/shard_map/ppermute | solution.py:331
  29.8 6.0 %collective-permute-start.13 = (f32[5,3,8,128]{3,2,1,0:T(8,128)S(1)}, f32[5,3,8,128]{3,2,1,0:T(8,128)S(1)}, u32[]{:S(2)}, u32[]{:S(2)}) collective-permute-start(f32[5,3,8,128]{3,2,1,0:T(8,128)S(1)} %get-tuple-element.56), channel_id=1, source_target_pairs={{0,12},{4,8},{8,4},{12,0},{16,28},{20,24},{24,20},{28,16},{1,13},{... | collective-permute-start | bytes 184328 | tf_op jit(solution)/shard_map/ppermute | solution.py:325
  31.8 5.2 %collective-permute-start.14 = (f32[5,3,8,128]{3,2,1,0:T(8,128)S(1)}, f32[5,3,8,128]{3,2,1,0:T(8,128)S(1)}, u32[]{:S(2)}, u32[]{:S(2)}) collective-permute-start(f32[5,3,8,128]{3,2,1,0:T(8,128)S(1)} %get-tuple-element.57), channel_id=1, source_target_pairs={{0,8},{4,12},{8,0},{12,4},{16,24},{20,28},{24,16},{28,20},{1,9},{5... | collective-permute-start | bytes 184328 | tf_op jit(solution)/shard_map/ppermute | solution.py:325
  32.2 4.8 %collective-permute-start.15 = (f32[5,3,8,128]{3,2,1,0:T(8,128)S(1)}, f32[5,3,8,128]{3,2,1,0:T(8,128)S(1)}, u32[]{:S(2)}, u32[]{:S(2)}) collective-permute-start(f32[5,3,8,128]{3,2,1,0:T(8,128)S(1)} %get-tuple-element.58), channel_id=1, source_target_pairs={{0,4},{4,0},{8,12},{12,8},{16,20},{20,16},{24,28},{28,24},{1,5},{5... | collective-permute-start | bytes 184328 | tf_op jit(solution)/shard_map/ppermute | solution.py:325
  33.4 4.9 %collective-permute-start.10 = (f32[3,3,8,128]{3,2,1,0:T(8,128)S(1)}, f32[3,3,8,128]{3,2,1,0:T(8,128)S(1)}, u32[]{:S(2)}, u32[]{:S(2)}) collective-permute-start(f32[3,3,8,128]{3,2,1,0:T(8,128)S(1)} %get-tuple-element.53), channel_id=1, source_target_pairs={{0,12},{4,8},{8,4},{12,0},{16,28},{20,24},{24,20},{28,16},{1,13},{... | collective-permute-start | bytes 110600 | tf_op jit(solution)/shard_map/ppermute | solution.py:325
  35.4 4.0 %collective-permute-start.11 = (f32[3,3,8,128]{3,2,1,0:T(8,128)S(1)}, f32[3,3,8,128]{3,2,1,0:T(8,128)S(1)}, u32[]{:S(2)}, u32[]{:S(2)}) collective-permute-start(f32[3,3,8,128]{3,2,1,0:T(8,128)S(1)} %get-tuple-element.54), channel_id=1, source_target_pairs={{0,8},{4,12},{8,0},{12,4},{16,24},{20,28},{24,16},{28,20},{1,9},{5... | collective-permute-start | bytes 110600 | tf_op jit(solution)/shard_map/ppermute | solution.py:325
  35.8 4.0 %collective-permute-start.12 = (f32[3,3,8,128]{3,2,1,0:T(8,128)S(1)}, f32[3,3,8,128]{3,2,1,0:T(8,128)S(1)}, u32[]{:S(2)}, u32[]{:S(2)}) collective-permute-start(f32[3,3,8,128]{3,2,1,0:T(8,128)S(1)} %get-tuple-element.55), channel_id=1, source_target_pairs={{0,4},{4,0},{8,12},{12,8},{16,20},{20,16},{24,28},{28,24},{1,5},{5... | collective-permute-start | bytes 110600 | tf_op jit(solution)/shard_map/ppermute | solution.py:325

commit v6 on v4

--- a/solution.py
+++ b/solution.py
@@ -257,27 +257,21 @@
     return total
 
 
-def early_kernel(*refs):
+def total_kernel(first, *refs):
     jumps, (damp_ref, out, order) = refs[:GROUP], refs[GROUP:]
     for k in range(GROUP):
         order[lax.bitwise_xor(spot(), partner(k))] = jumps[k][...]
-    out[...] = total_of(order, damp_ref[: out.shape[0]])
-
-
-def total_kernel(early_ref, *refs):
-    jumps, (damp_ref, out, order) = refs[:GROUP], refs[GROUP:]
-    split = early_ref.shape[0]
-    for k in range(GROUP):
-        order[lax.bitwise_xor(spot(), partner(k))] = jumps[k][...]
-    out[:split] = early_ref[...]
-    out[split:] = total_of(order, damp_ref[split:])
-
-
-def spread_kernel(*refs):
-    carry_ref, early, late = refs[0], refs[1 : 1 + GROUP], refs[1 + GROUP : 1 + 2 * GROUP]
-    damp_ref, outs, order = refs[1 + 2 * GROUP], refs[2 + 2 * GROUP : -1], refs[-1]
+    out[...] = total_of(order, damp_ref[first : first + out.shape[0]])
+
+
+def spread_kernel(early_carry, late_carry, *refs):
+    early, late = refs[:GROUP], refs[GROUP : 2 * GROUP]
+    damp_ref, outs, order, carry = refs[2 * GROUP], refs[1 + 2 * GROUP : -2], refs[-2], refs[-1]
+    split = early_carry.shape[0]
     sort_in(early, late, order)
-    run(order, damp_ref[...][:, None], jnp.where(lax.axis_index("tm") < GROUP, 0.0, carry_ref[...]))
+    carry[:split] = early_carry[...]
+    carry[split:] = late_carry[...]
+    run(order, damp_ref[...][:, None], jnp.where(lax.axis_index("tm") < GROUP, 0.0, carry[...]))
     sort_out(order, outs)
 
 
@@ -387,20 +381,26 @@
         halves.append(swap(jumps))
 
     orders = [pltpu.VMEM((GROUP, *share.shape), jnp.float32) for share in shares]
-    halves[0][0] = after(halves[0][0], halves[1][0])
-    total = call(early_kernel, shares[0], *halves[0], damp, scratch=[orders[0]], flops=BUSY)
-    total = call(
-        total_kernel, whole_share, total, *halves[1], damp, scratch=[orders[1]], flops=BUSY
-    )
-    carry = onward(total, 1)
-    if groups > 2:
-        carry = jnp.where(team < 1, 0.0, carry)
-        fade, distance = damp[:, None] ** GROUP, 1
-        while distance < groups - 1:
-            carry = carry + jnp.where(team < distance, 0.0, fade * onward(carry, distance))
-            distance, fade = 2 * distance, fade * fade
+    carries, total = [], halves[1][0]
+    for far, jumps in enumerate(halves):
+        jumps[0] = after(jumps[0], total)
+        first = far * sizes[0]
+        total = call(
+            functools.partial(total_kernel, first), shares[far], *jumps, damp,
+            scratch=[orders[far]],
+            flops=BUSY,
+        )
+        carry = onward(total, 1)
+        if groups > 2:
+            carry = jnp.where(team < 1, 0.0, carry)
+            fade, distance = damp[first : first + sizes[far], None] ** GROUP, 1
+            while distance < groups - 1:
+                carry = carry + jnp.where(team < distance, 0.0, fade * onward(carry, distance))
+                distance, fade = 2 * distance, fade * fade
+        carries.append(carry)
     news = call(
-        spread_kernel, [whole_share] * GROUP, carry, *halves[0], *halves[1], damp, scratch=[order]
+        spread_kernel, [whole_share] * GROUP, *carries, *halves[0], *halves[1], damp,
+        scratch=[order, pltpu.VMEM(whole_share.shape, jnp.float32)],
     )
     pieces = swap(news)
     whole = [pltpu.VMEM(own.shape, jnp.float32), pltpu.SemaphoreType.DMA]

time: 30 us -> 29.2 us (0.973); the launches traced: 29.5 us -> 29.1 us
  waiting for transfers between devices: 8.65 us -> 5.6 us
  starting transfers between devices: 16.5 us -> 19.1 us
    ppermute x1 -> x2, starting transfers between devices: 2.65 us -> 5.31 us  [onward(): lax.ppermute(value, 'tm', [(i, (i + step) % slices) for i in range(slices)])]
    ppermute x9, waiting for transfers between devices: 5.7 us -> 3.32 us  [swap(): lax.ppermute(parts[k], 'tm', [(i, i ^ partner(k)) for i in range(slices)])]
    ppermute x1 -> x2, waiting for transfers between devices: 2.94 us -> 2.27 us  [onward(): lax.ppermute(value, 'tm', [(i, (i + step) % slices) for i in range(slices)])]
  transfers between devices with their start and end apart: 12 -> 13, of which waited for: 6 -> 6; matrix products, arithmetic and copies ran while one was open for 0% -> 0% of each run, Pallas kernels for 10% -> 11%
where the time goes in v6:
time: 29.2 us; the launch traced here: 29.1 us
  starting transfers between devices  19.1 us (65%)
  waiting for transfers between devices  5.6 us (19%)
  Pallas kernels  3.26 us (11%)
  local copies, waits for them, and re-layouts  1 us (3%)
    ppermute x9, starting transfers between devices, swap(): lax.ppermute(parts[k], 'tm', [(i, i ^ partner(k)) for i in range(slices)])  10.7 us
    ppermute x2, starting transfers between devices, onward(): lax.ppermute(value, 'tm', [(i, (i + step) % slices) for i in range(slices)])  5.31 us
    ppermute x9, waiting for transfers between devices, swap(): lax.ppermute(parts[k], 'tm', [(i, i ^ partner(k)) for i in range(slices)])  3.32 us
    ppermute x2, starting transfers between devices, halo(): return lax.ppermute(value, 'gz', [(i, j % slabs) for i, j in pairs])  3.16 us
    pallas_call x7, Pallas kernels, call(): pl.pallas_call(kernel, out_shape=out_shape, in_specs=[VMEM] * len(args),...  2.47 us
    ppermute x2, waiting for transfers between devices, onward(): lax.ppermute(value, 'tm', [(i, (i + step) % slices) for i in range(slices)])  2.27 us
    unnamed x4, local copies, waits for them, and re-layouts  1 us
    pallas_call x1, Pallas kernels, shards(): pl.pallas_call(first_kernel, out_shape=f32(*own.shape), in_specs=[VMEM],...  0.78 us
  transfers between devices with their start and end apart: 13, of which 6 were waited for; matrix products, arithmetic and copies ran while one was open for 0% of the time, Pallas kernels for 11%

profile of v6, /device:TPU:0, one launch (start us, length us, event | category | flops | bytes accessed | tf_op | source)
XLA Modules:
  0.0 29.1 jit_solution(3998681075652274822)
XLA Ops:
  0.0 1.0 %copy-done = f32[1,3,16,16,128]{4,3,2,1,0:T(8,128)S(1)} copy-done((f32[1,3,16,16,128]{4,3,2,1,0:T(8,128)S(1)}, f32[1,3,16,16,128]{4,3,2,1,0:T(8,128)}, u32[]{:S(2)}) %copy-start) | copy-done | bytes 393240
  1.0 0.5 %collective-permute-start = (f32[3,6,16,128]{3,2,1,0:T(8,128)S(1)}, f32[3,6,16,128]{3,2,1,0:T(8,128)S(1)}, u32[]{:S(2)}, u32[]{:S(2)}) collective-permute-start(f32[3,6,16,128]{3,2,1,0:T(8,128)S(1)} %get-tuple-element.27), channel_id=1, source_target_pairs={{0,1},{1,0},{2,3},{3,2},{4,5},{5,4},{6,7},{7,6},{8,9},{9,8},{10,11... | collective-permute-start | bytes 442376 | tf_op jit(solution)/shard_map/ppermute | solution.py:332
  1.5 2.6 %collective-permute-start.1 = (f32[3,6,16,128]{3,2,1,0:T(8,128)S(1)}, f32[3,6,16,128]{3,2,1,0:T(8,128)S(1)}, u32[]{:S(2)}, u32[]{:S(2)}) collective-permute-start(f32[3,6,16,128]{3,2,1,0:T(8,128)S(1)} %get-tuple-element.32), channel_id=1, source_target_pairs={{0,3},{1,2},{2,1},{3,0},{4,7},{5,6},{6,5},{7,4},{8,11},{9,10},{10,... | collective-permute-start | bytes 442376 | tf_op jit(solution)/shard_map/ppermute | solution.py:332
  4.2 0.8 %shard_map.29 = (f32[6,2,3,3,2,8,128]{6,5,4,3,2,1,0:T(8,128)S(1)}, f32[4,3,2,8,128]{4,3,2,1,0:T(8,128)S(1)}, f32[2,6,3,2,8,128]{5,4,3,2,1,0:T(8,128)S(1)}, f32[8...) custom-call(f32[3,16,16,128]{3,2,1,0:T(8,128)S(1)} %bitcast.3, f32[16,16,128]{2,1,0:T(8,128)S(1)} %copy-done.1), custom_call_target="tpu_custom_call" | custom-call | flops 67108864 | bytes 1048576 | tf_op jit(solution)/shard_map/pallas_call | solution.py:26
  5.0 0.0 collective-permute-done.face_ref
  5.1 0.7 %shard_map.30 = (f32[5,3,8,128]{3,2,1,0:T(8,128)S(1)}, f32[5,3,8,128]{3,2,1,0:T(8,128)S(1)}, f32[5,3,8,128]{3,2,1,0:T(8,128)S(1)}, f32[5,3,8,128]{3,2,1,0:T(8,128)S(1)}) custom-call(f32[3,6,16,128]{3,2,1,0:T(8,128)S(1)} %collective-permute-done.face_ref, f32[6,2,3,3,2,8,128]{6,5,4,3,2,1,0:T(8,128)S(1)} %get-tuple-element.28.edges, ...), custom_call_target="tpu_custom_call" | custom-call | flops 4294967296 | bytes 1048576 | tf_op jit(solution)/shard_map/pallas_call | solution.py:26
  5.8 2.6 %collective-permute-start.2 = (f32[5,3,8,128]{3,2,1,0:T(8,128)S(1)}, f32[5,3,8,128]{3,2,1,0:T(8,128)S(1)}, u32[]{:S(2)}, u32[]{:S(2)}) collective-permute-start(f32[5,3,8,128]{3,2,1,0:T(8,128)S(1)} %get-tuple-element.35), channel_id=1, source_target_pairs={{0,12},{4,8},{8,4},{12,0},{16,28},{20,24},{24,20},{28,16},{1,13},{... | collective-permute-start | bytes 184328 | tf_op jit(solution)/shard_map/ppermute | solution.py:336
  8.4 0.4 %collective-permute-start.3 = (f32[5,3,8,128]{3,2,1,0:T(8,128)S(1)}, f32[5,3,8,128]{3,2,1,0:T(8,128)S(1)}, u32[]{:S(2)}, u32[]{:S(2)}) collective-permute-start(f32[5,3,8,128]{3,2,1,0:T(8,128)S(1)} %get-tuple-element.36), channel_id=1, source_target_pairs={{0,8},{4,12},{8,0},{12,4},{16,24},{20,28},{24,16},{28,20},{1,9},{5... | collective-permute-start | bytes 184328 | tf_op jit(solution)/shard_map/ppermute | solution.py:336
  8.8 0.5 %collective-permute-start.4 = (f32[5,3,8,128]{3,2,1,0:T(8,128)S(1)}, f32[5,3,8,128]{3,2,1,0:T(8,128)S(1)}, u32[]{:S(2)}, u32[]{:S(2)}) collective-permute-start(f32[5,3,8,128]{3,2,1,0:T(8,128)S(1)} %get-tuple-element.37), channel_id=1, source_target_pairs={{0,4},{4,0},{8,12},{12,8},{16,20},{20,16},{24,28},{28,24},{1,5},{5... | collective-permute-start | bytes 184328 | tf_op jit(solution)/shard_map/ppermute | solution.py:336
  9.3 0.0 collective-permute-done.1.face_ref
  9.3 0.7 %shard_map.31 = (f32[3,3,8,128]{3,2,1,0:T(8,128)S(1)}, f32[3,3,8,128]{3,2,1,0:T(8,128)S(1)}, f32[3,3,8,128]{3,2,1,0:T(8,128)S(1)}, f32[3,3,8,128]{3,2,1,0:T(8,128)S(1)}) custom-call(f32[3,6,16,128]{3,2,1,0:T(8,128)S(1)} %collective-permute-done.1.face_ref, f32[6,2,3,3,2,8,128]{6,5,4,3,2,1,0:T(8,128)S(1)} %get-tuple-element.28.edges, ...), custom_call_target="tpu_custom_call" | custom-call | flops 4294967296 | bytes 1048576 | tf_op jit(solution)/shard_map/pallas_call | solution.py:26
  10.0 2.6 %collective-permute-start.6 = (f32[3,3,8,128]{3,2,1,0:T(8,128)S(1)}, f32[3,3,8,128]{3,2,1,0:T(8,128)S(1)}, u32[]{:S(2)}, u32[]{:S(2)}) collective-permute-start(f32[3,3,8,128]{3,2,1,0:T(8,128)S(1)} %get-tuple-element.40), channel_id=1, source_target_pairs={{0,12},{4,8},{8,4},{12,0},{16,28},{20,24},{24,20},{28,16},{1,13},{... | collective-permute-start | bytes 110600 | tf_op jit(solution)/shard_map/ppermute | solution.py:336
  12.6 0.4 %collective-permute-start.7 = (f32[3,3,8,128]{3,2,1,0:T(8,128)S(1)}, f32[3,3,8,128]{3,2,1,0:T(8,128)S(1)}, u32[]{:S(2)}, u32[]{:S(2)}) collective-permute-start(f32[3,3,8,128]{3,2,1,0:T(8,128)S(1)} %get-tuple-element.41), channel_id=1, source_target_pairs={{0,8},{4,12},{8,0},{12,4},{16,24},{20,28},{24,16},{28,20},{1,9},{5... | collective-permute-start | bytes 110600 | tf_op jit(solution)/shard_map/ppermute | solution.py:336
  13.1 0.0 collective-permute-done.2.refs_1_
  13.1 0.5 %collective-permute-start.8 = (f32[3,3,8,128]{3,2,1,0:T(8,128)S(1)}, f32[3,3,8,128]{3,2,1,0:T(8,128)S(1)}, u32[]{:S(2)}, u32[]{:S(2)}) collective-permute-start(f32[3,3,8,128]{3,2,1,0:T(8,128)S(1)} %get-tuple-element.42), channel_id=1, source_target_pairs={{0,4},{4,0},{8,12},{12,8},{16,20},{20,16},{24,28},{28,24},{1,5},{5... | collective-permute-start | bytes 110600 | tf_op jit(solution)/shard_map/ppermute | solution.py:336
  13.6 0.0 collective-permute-done.3.refs_2_
  13.6 0.0 collective-permute-done.4.refs_3_
  13.7 2.7 %collective-permute-start.5 = (f32[5,3,8,128]{3,2,1,0:T(8,128)S(1)}, f32[5,3,8,128]{3,2,1,0:T(8,128)S(1)}, u32[]{:S(2)}, u32[]{:S(2)}) collective-permute-start(f32[5,3,8,128]{3,2,1,0:T(8,128)S(1)} %shard_map.32), channel_id=1, source_target_pairs={{0,16},{4,20},{8,24},{12,28},{16,0},{20,4},{24,8},{28,12},{1,17},{... | collective-permute-start | bytes 184328 | tf_op jit(solution)/shard_map/ppermute | solution.py:342
  16.3 0.0 collective-permute-done.6.refs_1_.refs_5_
  16.3 0.3 %collective-permute-done.7.refs_2_.refs_6_ = f32[3,3,8,128]{3,2,1,0:T(8,128)S(1)} collective-permute-done((f32[3,3,8,128]{3,2,1,0:T(8,128)S(1)}, f32[3,3,8,128]{3,2,1,0:T(8,128)S(1)}, u32[]{:S(2)}, u32[]{:S(2)}) %collective-permute-start.7) | collective-permute-done | bytes 36896 | tf_op jit(solution)/shard_map/ppermute | solution.py:336
  16.7 0.4 %collective-permute-done.8.refs_3_.refs_7_ = f32[3,3,8,128]{3,2,1,0:T(8,128)S(1)} collective-permute-done((f32[3,3,8,128]{3,2,1,0:T(8,128)S(1)}, f32[3,3,8,128]{3,2,1,0:T(8,128)S(1)}, u32[]{:S(2)}, u32[]{:S(2)}) %collective-permute-start.8) | collective-permute-done | bytes 36896 | tf_op jit(solution)/shard_map/ppermute | solution.py:336
  17.1 2.7 %collective-permute-start.9 = (f32[3,3,8,128]{3,2,1,0:T(8,128)S(1)}, f32[3,3,8,128]{3,2,1,0:T(8,128)S(1)}, u32[]{:S(2)}, u32[]{:S(2)}) collective-permute-start(f32[3,3,8,128]{3,2,1,0:T(8,128)S(1)} %shard_map.33), channel_id=1, source_target_pairs={{0,16},{4,20},{8,24},{12,28},{16,0},{20,4},{24,8},{28,12},{1,17},{... | collective-permute-start | bytes 110600 | tf_op jit(solution)/shard_map/ppermute | solution.py:342
  19.7 2.3 %collective-permute-done.9.late_carry = f32[3,3,8,128]{3,2,1,0:T(8,128)S(1)} collective-permute-done((f32[3,3,8,128]{3,2,1,0:T(8,128)S(1)}, f32[3,3,8,128]{3,2,1,0:T(8,128)S(1)}, u32[]{:S(2)}, u32[]{:S(2)}) %collective-permute-start.9) | collective-permute-done | bytes 36896 | tf_op jit(solution)/shard_map/ppermute | solution.py:342
  22.0 0.0 collective-permute-done.5.early_carry
  22.0 0.1 shard_map.34
  22.1 1.9 %collective-permute-start.10 = (f32[8,3,8,128]{3,2,1,0:T(8,128)S(1)}, f32[8,3,8,128]{3,2,1,0:T(8,128)S(1)}, u32[]{:S(2)}, u32[]{:S(2)}) collective-permute-start(f32[8,3,8,128]{3,2,1,0:T(8,128)S(1)} %get-tuple-element.44), channel_id=1, source_target_pairs={{0,12},{4,8},{8,4},{12,0},{16,28},{20,24},{24,20},{28,16},{1,13},{... | collective-permute-start | bytes 294920 | tf_op jit(solution)/shard_map/ppermute | solution.py:336
  24.0 0.4 %collective-permute-start.11 = (f32[8,3,8,128]{3,2,1,0:T(8,128)S(1)}, f32[8,3,8,128]{3,2,1,0:T(8,128)S(1)}, u32[]{:S(2)}, u32[]{:S(2)}) collective-permute-start(f32[8,3,8,128]{3,2,1,0:T(8,128)S(1)} %get-tuple-element.45), channel_id=1, source_target_pairs={{0,8},{4,12},{8,0},{12,4},{16,24},{20,28},{24,16},{28,20},{1,9},{5... | collective-permute-start | bytes 294920 | tf_op jit(solution)/shard_map/ppermute | solution.py:336
  24.4 1.2 %collective-permute-start.12 = (f32[8,3,8,128]{3,2,1,0:T(8,128)S(1)}, f32[8,3,8,128]{3,2,1,0:T(8,128)S(1)}, u32[]{:S(2)}, u32[]{:S(2)}) collective-permute-start(f32[8,3,8,128]{3,2,1,0:T(8,128)S(1)} %get-tuple-element.46), channel_id=1, source_target_pairs={{0,4},{4,0},{8,12},{12,8},{16,20},{20,16},{24,28},{28,24},{1,5},{5... | collective-permute-start | bytes 294920 | tf_op jit(solution)/shard_map/ppermute | solution.py:336
  25.6 2.0 %collective-permute-done.10.refs_1_ = f32[8,3,8,128]{3,2,1,0:T(8,128)S(1)} collective-permute-done((f32[8,3,8,128]{3,2,1,0:T(8,128)S(1)}, f32[8,3,8,128]{3,2,1,0:T(8,128)S(1)}, u32[]{:S(2)}, u32[]{:S(2)}) %collective-permute-start.10) | collective-permute-done | bytes 98336 | tf_op jit(solution)/shard_map/ppermute | solution.py:336
  27.7 0.8 %shard_map.35.refs_4_ = f32[3,16,16,128]{3,2,1,0:T(8,128)} custom-call(f32[16,3,2,8,128]{4,3,2,1,0:T(8,128)S(1)} %get-tuple-element.48.kept), custom_call_target="tpu_custom_call" | custom-call | flops 4294967296 | bytes 1048576 | tf_op jit(solution)/shard_map/pallas_call | solution.py:407
  28.5 0.1 collective-permute-done.11.refs_2_
  28.6 0.4 %collective-permute-done.12.refs_3_ = f32[8,3,8,128]{3,2,1,0:T(8,128)S(1)} collective-permute-done((f32[8,3,8,128]{3,2,1,0:T(8,128)S(1)}, f32[8,3,8,128]{3,2,1,0:T(8,128)S(1)}, u32[]{:S(2)}, u32[]{:S(2)}) %collective-permute-start.12) | collective-permute-done | bytes 98336 | tf_op jit(solution)/shard_map/ppermute | solution.py:336
  (7 shorter events, 0.1 us)
Async XLA Ops:
  0.0 1.0 %copy-start = (f32[1,3,16,16,128]{4,3,2,1,0:T(8,128)S(1)}, f32[1,3,16,16,128]{4,3,2,1,0:T(8,128)}, u32[]{:S(2)}) copy-start(f32[1,3,16,16,128]{4,3,2,1,0:T(8,128)} %param.2) | copy-start | bytes 1179652
  1.0 3.2 %copy-start.1 = (f32[16,16,128]{2,1,0:T(8,128)S(1)}, f32[16,16,128]{2,1,0:T(8,128)}, u32[]{:S(2)}) copy-start(f32[16,16,128]{2,1,0:T(8,128)} %rate_ref.1) | copy-start | bytes 393220
  1.0 4.0 %collective-permute-start = (f32[3,6,16,128]{3,2,1,0:T(8,128)S(1)}, f32[3,6,16,128]{3,2,1,0:T(8,128)S(1)}, u32[]{:S(2)}, u32[]{:S(2)}) collective-permute-start(f32[3,6,16,128]{3,2,1,0:T(8,128)S(1)} %get-tuple-element.27), channel_id=1, source_target_pairs={{0,1},{1,0},{2,3},{3,2},{4,5},{5,4},{6,7},{7,6},{8,9},{9,8},{10,11... | collective-permute-start | bytes 442376 | tf_op jit(solution)/shard_map/ppermute | solution.py:332
  1.5 7.8 %collective-permute-start.1 = (f32[3,6,16,128]{3,2,1,0:T(8,128)S(1)}, f32[3,6,16,128]{3,2,1,0:T(8,128)S(1)}, u32[]{:S(2)}, u32[]{:S(2)}) collective-permute-start(f32[3,6,16,128]{3,2,1,0:T(8,128)S(1)} %get-tuple-element.32), channel_id=1, source_target_pairs={{0,3},{1,2},{2,1},{3,0},{4,7},{5,6},{6,5},{7,4},{8,11},{9,10},{10,... | collective-permute-start | bytes 442376 | tf_op jit(solution)/shard_map/ppermute | solution.py:332
  5.8 7.3 %collective-permute-start.2 = (f32[5,3,8,128]{3,2,1,0:T(8,128)S(1)}, f32[5,3,8,128]{3,2,1,0:T(8,128)S(1)}, u32[]{:S(2)}, u32[]{:S(2)}) collective-permute-start(f32[5,3,8,128]{3,2,1,0:T(8,128)S(1)} %get-tuple-element.35), channel_id=1, source_target_pairs={{0,12},{4,8},{8,4},{12,0},{16,28},{20,24},{24,20},{28,16},{1,13},{... | collective-permute-start | bytes 184328 | tf_op jit(solution)/shard_map/ppermute | solution.py:336
  8.4 5.3 %collective-permute-start.3 = (f32[5,3,8,128]{3,2,1,0:T(8,128)S(1)}, f32[5,3,8,128]{3,2,1,0:T(8,128)S(1)}, u32[]{:S(2)}, u32[]{:S(2)}) collective-permute-start(f32[5,3,8,128]{3,2,1,0:T(8,128)S(1)} %get-tuple-element.36), channel_id=1, source_target_pairs={{0,8},{4,12},{8,0},{12,4},{16,24},{20,28},{24,16},{28,20},{1,9},{5... | collective-permute-start | bytes 184328 | tf_op jit(solution)/shard_map/ppermute | solution.py:336
  8.8 4.8 %collective-permute-start.4 = (f32[5,3,8,128]{3,2,1,0:T(8,128)S(1)}, f32[5,3,8,128]{3,2,1,0:T(8,128)S(1)}, u32[]{:S(2)}, u32[]{:S(2)}) collective-permute-start(f32[5,3,8,128]{3,2,1,0:T(8,128)S(1)} %get-tuple-element.37), channel_id=1, source_target_pairs={{0,4},{4,0},{8,12},{12,8},{16,20},{20,16},{24,28},{28,24},{1,5},{5... | collective-permute-start | bytes 184328 | tf_op jit(solution)/shard_map/ppermute | solution.py:336
  10.0 6.3 %collective-permute-start.6 = (f32[3,3,8,128]{3,2,1,0:T(8,128)S(1)}, f32[3,3,8,128]{3,2,1,0:T(8,128)S(1)}, u32[]{:S(2)}, u32[]{:S(2)}) collective-permute-start(f32[3,3,8,128]{3,2,1,0:T(8,128)S(1)} %get-tuple-element.40), channel_id=1, source_target_pairs={{0,12},{4,8},{8,4},{12,0},{16,28},{20,24},{24,20},{28,16},{1,13},{... | collective-permute-start | bytes 110600 | tf_op jit(solution)/shard_map/ppermute | solution.py:336
  12.6 4.0 %collective-permute-start.7 = (f32[3,3,8,128]{3,2,1,0:T(8,128)S(1)}, f32[3,3,8,128]{3,2,1,0:T(8,128)S(1)}, u32[]{:S(2)}, u32[]{:S(2)}) collective-permute-start(f32[3,3,8,128]{3,2,1,0:T(8,128)S(1)} %get-tuple-element.41), channel_id=1, source_target_pairs={{0,8},{4,12},{8,0},{12,4},{16,24},{20,28},{24,16},{28,20},{1,9},{5... | collective-permute-start | bytes 110600 | tf_op jit(solution)/shard_map/ppermute | solution.py:336
  13.1 4.0 %collective-permute-start.8 = (f32[3,3,8,128]{3,2,1,0:T(8,128)S(1)}, f32[3,3,8,128]{3,2,1,0:T(8,128)S(1)}, u32[]{:S(2)}, u32[]{:S(2)}) collective-permute-start(f32[3,3,8,128]{3,2,1,0:T(8,128)S(1)} %get-tuple-element.42), channel_id=1, source_target_pairs={{0,4},{4,0},{8,12},{12,8},{16,20},{20,16},{24,28},{28,24},{1,5},{5... | collective-permute-start | bytes 110600 | tf_op jit(solution)/shard_map/ppermute | solution.py:336
  13.7 8.3 %collective-permute-start.5 = (f32[5,3,8,128]{3,2,1,0:T(8,128)S(1)}, f32[5,3,8,128]{3,2,1,0:T(8,128)S(1)}, u32[]{:S(2)}, u32[]{:S(2)}) collective-permute-start(f32[5,3,8,128]{3,2,1,0:T(8,128)S(1)} %shard_map.32), channel_id=1, source_target_pairs={{0,16},{4,20},{8,24},{12,28},{16,0},{20,4},{24,8},{28,12},{1,17},{... | collective-permute-start | bytes 184328 | tf_op jit(solution)/shard_map/ppermute | solution.py:342
  17.1 4.9 %collective-permute-start.9 = (f32[3,3,8,128]{3,2,1,0:T(8,128)S(1)}, f32[3,3,8,128]{3,2,1,0:T(8,128)S(1)}, u32[]{:S(2)}, u32[]{:S(2)}) collective-permute-start(f32[3,3,8,128]{3,2,1,0:T(8,128)S(1)} %shard_map.33), channel_id=1, source_target_pairs={{0,16},{4,20},{8,24},{12,28},{16,0},{20,4},{24,8},{28,12},{1,17},{... | collective-permute-start | bytes 110600 | tf_op jit(solution)/shard_map/ppermute | solution.py:342
  22.1 5.6 %collective-permute-start.10 = (f32[8,3,8,128]{3,2,1,0:T(8,128)S(1)}, f32[8,3,8,128]{3,2,1,0:T(8,128)S(1)}, u32[]{:S(2)}, u32[]{:S(2)}) collective-permute-start(f32[8,3,8,128]{3,2,1,0:T(8,128)S(1)} %get-tuple-element.44), channel_id=1, source_target_pairs={{0,12},{4,8},{8,4},{12,0},{16,28},{20,24},{24,20},{28,16},{1,13},{... | collective-permute-start | bytes 294920 | tf_op jit(solution)/shard_map/ppermute | solution.py:336
  24.0 4.6 %collective-permute-start.11 = (f32[8,3,8,128]{3,2,1,0:T(8,128)S(1)}, f32[8,3,8,128]{3,2,1,0:T(8,128)S(1)}, u32[]{:S(2)}, u32[]{:S(2)}) collective-permute-start(f32[8,3,8,128]{3,2,1,0:T(8,128)S(1)} %get-tuple-element.45), channel_id=1, source_target_pairs={{0,8},{4,12},{8,0},{12,4},{16,24},{20,28},{24,16},{28,20},{1,9},{5... | collective-permute-start | bytes 294920 | tf_op jit(solution)/shard_map/ppermute | solution.py:336
  24.4 4.6 %collective-permute-start.12 = (f32[8,3,8,128]{3,2,1,0:T(8,128)S(1)}, f32[8,3,8,128]{3,2,1,0:T(8,128)S(1)}, u32[]{:S(2)}, u32[]{:S(2)}) collective-permute-start(f32[8,3,8,128]{3,2,1,0:T(8,128)S(1)} %get-tuple-element.46), channel_id=1, source_target_pairs={{0,4},{4,0},{8,12},{12,8},{16,20},{20,16},{24,28},{28,24},{1,5},{5... | collective-permute-start | bytes 294920 | tf_op jit(solution)/shard_map/ppermute | solution.py:336

commit v7 on v6

--- a/solution.py
+++ b/solution.py
@@ -228,19 +228,6 @@
         out[...] = share_of(jumps, k, out.shape[0])
 
 
-def sort_in(early, late, order):
-    split = early[0].shape[0]
-    for k in range(GROUP):
-        place = lax.bitwise_xor(spot(), partner(k))
-        order[place, :split] = early[k][...]
-        order[place, split:] = late[k][...]
-
-
-def sort_out(order, outs):
-    for k in range(GROUP):
-        outs[k][...] = order[lax.bitwise_xor(spot(), partner(k))]
-
-
 def run(order, damp, total):
     for j in range(GROUP):
         jump = order[j]
@@ -264,15 +251,31 @@
     out[...] = total_of(order, damp_ref[first : first + out.shape[0]])
 
 
-def spread_kernel(early_carry, late_carry, *refs):
-    early, late = refs[:GROUP], refs[GROUP : 2 * GROUP]
-    damp_ref, outs, order, carry = refs[2 * GROUP], refs[1 + 2 * GROUP : -2], refs[-2], refs[-1]
-    split = early_carry.shape[0]
-    sort_in(early, late, order)
-    carry[:split] = early_carry[...]
-    carry[split:] = late_carry[...]
-    run(order, damp_ref[...][:, None], jnp.where(lax.axis_index("tm") < GROUP, 0.0, carry[...]))
-    sort_out(order, outs)
+def news_of(first, carry_ref, jumps, damp_ref, order):
+    for k in range(GROUP):
+        order[lax.bitwise_xor(spot(), partner(k))] = jumps[k][...]
+    damp = damp_ref[first : first + carry_ref.shape[0]][:, None]
+    run(order, damp, jnp.where(lax.axis_index("tm") < GROUP, 0.0, carry_ref[...]))
+
+
+def early_kernel(carry_ref, *refs):
+    jumps, damp_ref, outs, order = refs[:GROUP], refs[GROUP], refs[GROUP + 1 : -1], refs[-1]
+    news_of(0, carry_ref, jumps, damp_ref, order)
+    for k, out in enumerate(outs):
+        out[...] = order[lax.bitwise_xor(spot(), partner(k))]
+
+
+def late_kernel(across_ref, carry_ref, *refs):
+    jumps, damp_ref, outs, order = refs[:GROUP], refs[GROUP], refs[GROUP + 1 : -1], refs[-1]
+    split = across_ref.shape[0]
+    news_of(split, carry_ref, jumps, damp_ref, order)
+    for k, out in enumerate(outs):
+        value = order[lax.bitwise_xor(spot(), partner(k))]
+        if k == 1:
+            out[:split] = across_ref[...]
+            out[split:] = value
+        else:
+            out[...] = value
 
 
 def write(whole, out, sem):
@@ -291,28 +294,44 @@
         write(whole, out, sem)
 
 
-def finish_kernel(*refs):
-    pieces, (_, out, whole, sem) = refs[:GROUP], refs[GROUP:]
-    layers, rows = out.shape[1], out.shape[2] // 2
+def pass_kernel(back_ref, side_ref, back, side):
+    back[...] = back_ref[...]
+    side[...] = side_ref[...]
+
+
+def put(whole, held):
+    layers, rows = whole.shape[1], whole.shape[2] // 2
     split = (layers - STAGES) // 2
     near = near_side()
+    for k, first, piece in held:
+        chunk = chunk_of(k)
+        for odd in (0, 1):
+
+            @pl.when(chunk // 2 == odd)
+            def _():
+                for j in range(first, first + piece.shape[0]):
+                    if j < split:
+                        slot = lax.rem(chunk, 2) * split + j
+                    else:
+                        slot = layers - 1 - (lax.rem(chunk, 2) * (STAGES // 2) + j - split)
+                    layer = slot + near * (layers - 1 - 2 * slot)
+                    for c in range(3):
+                        whole[c, layer, pl.ds(odd, rows, stride=2), :] = piece[j - first, c]
+
+
+def gather_kernel(early_own, late_own, across, early_back, early_side, whole):
+    split = early_own.shape[0]
+    held = ((0, 0, early_own), (0, split, late_own), (1, 0, across))
+    put(whole, held + ((2, 0, early_back), (3, 0, early_side)))
+
+
+def finish_kernel(gathered, late_back, late_side, _, out, whole, sem):
+    split = (whole.shape[1] - STAGES) // 2
 
     @pl.when(lax.axis_index("tm") != 0)
     def _():
-        for k, piece in enumerate(pieces):
-            chunk = chunk_of(k)
-            for odd in (0, 1):
-
-                @pl.when(chunk // 2 == odd)
-                def _():
-                    for j in range(piece.shape[0]):
-                        if j < split:
-                            slot = lax.rem(chunk, 2) * split + j
-                        else:
-                            slot = layers - 1 - (lax.rem(chunk, 2) * (STAGES // 2) + j - split)
-                        layer = slot + near * (layers - 1 - 2 * slot)
-                        for c in range(3):
-                            whole[c, layer, pl.ds(odd, rows, stride=2), :] = piece[j, c]
+        whole[...] = gathered[...]
+        put(whole, ((2, split, late_back), (3, split, late_side)))
         write(whole, out, sem)
 
 
@@ -331,11 +350,11 @@
     def halo(value, pairs):
         return lax.ppermute(value, "gz", [(i, j % slabs) for i, j in pairs])
 
+    def exchange(value, k):
+        return lax.ppermute(value, "tm", [(i, i ^ partner(k)) for i in range(slices)])
+
     def swap(parts):
-        return [parts[0]] + [
-            lax.ppermute(parts[k], "tm", [(i, i ^ partner(k)) for i in range(slices)])
-            for k in range(1, GROUP)
-        ]
+        return [parts[0]] + [exchange(parts[k], k) for k in range(1, GROUP)]
 
     def onward(value, distance):
         step = distance * GROUP
@@ -365,7 +384,6 @@
     strip = pltpu.VMEM((STAGES + 1, STAGES, *tile), jnp.float32)
     shares = [f32(size, 3, *row) for size in sizes]
     whole_share = f32(sum(sizes), 3, *row)
-    order = pltpu.VMEM((GROUP, *whole_share.shape), jnp.float32)
 
     def after(value, earlier):
         return lax.optimization_barrier((value, earlier))[0]
@@ -398,11 +416,23 @@
                 carry = carry + jnp.where(team < distance, 0.0, fade * onward(carry, distance))
                 distance, fade = 2 * distance, fade * fade
         carries.append(carry)
-    news = call(
-        spread_kernel, [whole_share] * GROUP, *carries, *halves[0], *halves[1], damp,
-        scratch=[order, pltpu.VMEM(whole_share.shape, jnp.float32)],
+    early = call(
+        early_kernel, [shares[0]] * GROUP, carries[0], *halves[0], damp, scratch=[orders[0]],
+        flops=BUSY,
     )
-    pieces = swap(news)
+    back, side = exchange(early[2], 2), exchange(early[3], 3)
+    late = call(
+        late_kernel, [shares[1], whole_share, shares[1], shares[1]],
+        early[1], carries[1], *halves[1], damp,
+        scratch=[orders[1]],
+        flops=BUSY,
+    )
+    late = [*late[:2], *call(pass_kernel, [shares[1]] * 2, *late[2:], flops=BUSY)]
+    late_own, across, late_back, late_side = swap(late)
+    gathered = call(
+        gather_kernel, f32(*own.shape), early[0], late_own, across, back, side, flops=BUSY
+    )
+    pieces = [gathered, late_back, late_side]
     whole = [pltpu.VMEM(own.shape, jnp.float32), pltpu.SemaphoreType.DMA]
     updated = pl.pallas_call(
         first_kernel,
@@ -412,14 +442,14 @@
         scratch_shapes=whole,
         compiler_params=PARAMS,
         cost_estimate=pl.CostEstimate(flops=BUSY, bytes_accessed=1 << 20, transcendentals=0),
-    )(after(kept, pieces[1]))
+    )(after(kept, gathered))
     updated = pl.pallas_call(
         finish_kernel,
         out_shape=f32(*own.shape),
-        in_specs=[VMEM] * GROUP + [ANY],
+        in_specs=[VMEM] * len(pieces) + [ANY],
         out_specs=ANY,
         scratch_shapes=whole,
-        input_output_aliases={GROUP: 0},
+        input_output_aliases={len(pieces): 0},
         compiler_params=PARAMS,
     )(*pieces, updated)
     return updated[None]

time: 29.2 us -> 29.2 us (level)
  waiting for transfers between devices: 5.6 us -> 2.84 us
  starting transfers between devices: 19.1 us -> 21.7 us
    ppermute x9 -> x11, starting transfers between devices: 10.7 us -> 13.2 us  [exchange(): lax.ppermute(value, 'tm', [(i, i ^ partner(k)) for i in range(slices)])]
    ppermute x2, waiting for transfers between devices: 2.27 us -> 0.01 us  [onward(): lax.ppermute(value, 'tm', [(i, (i + step) % slices) for i in range(slices)])]
    ppermute x9 -> x11, waiting for transfers between devices: 3.32 us -> 2.83 us  [exchange(): lax.ppermute(value, 'tm', [(i, i ^ partner(k)) for i in range(slices)])]
    pallas_call x7 -> x10, Pallas kernels: 2.47 us -> 2.59 us  [call(): pl.pallas_call(kernel, out_shape=out_shape, in_specs=[VMEM] * len(args),...]
  transfers between devices with their start and end apart: 13 -> 15, of which waited for: 6 -> 4; matrix products, arithmetic and copies ran while one was open for 0% -> 0% of each run, Pallas kernels for 11% -> 12%
where the time goes in v7:
time: 29.2 us; the launch traced here: 29 us
  starting transfers between devices  21.7 us (74%)
  Pallas kernels  3.39 us (12%)
  waiting for transfers between devices  2.84 us (10%)
  local copies, waits for them, and re-layouts  1 us (3%)
    ppermute x11, starting transfers between devices, exchange(): lax.ppermute(value, 'tm', [(i, i ^ partner(k)) for i in range(slices)])  13.2 us
    ppermute x2, starting transfers between devices, onward(): lax.ppermute(value, 'tm', [(i, (i + step) % slices) for i in range(slices)])  5.31 us
    ppermute x2, starting transfers between devices, halo(): return lax.ppermute(value, 'gz', [(i, j % slabs) for i, j in pairs])  3.16 us
    ppermute x11, waiting for transfers between devices, exchange(): lax.ppermute(value, 'tm', [(i, i ^ partner(k)) for i in range(slices)])  2.83 us
    pallas_call x10, Pallas kernels, call(): pl.pallas_call(kernel, out_shape=out_shape, in_specs=[VMEM] * len(args),...  2.59 us
    unnamed x4, local copies, waits for them, and re-layouts  1 us
    pallas_call x1, Pallas kernels, shards(): pl.pallas_call(first_kernel, out_shape=f32(*own.shape), in_specs=[VMEM],...  0.79 us
  transfers between devices with their start and end apart: 15, of which 4 were waited for; matrix products, arithmetic and copies ran while one was open for 0% of the time, Pallas kernels for 12%

profile of v7, /device:TPU:0, one launch (start us, length us, event | category | flops | bytes accessed | tf_op | source)
XLA Modules:
  0.0 29.0 jit_solution(8636709939210404892)
XLA Ops:
  0.0 1.0 %copy-done = f32[1,3,16,16,128]{4,3,2,1,0:T(8,128)S(1)} copy-done((f32[1,3,16,16,128]{4,3,2,1,0:T(8,128)S(1)}, f32[1,3,16,16,128]{4,3,2,1,0:T(8,128)}, u32[]{:S(2)}) %copy-start) | copy-done | bytes 393240
  1.0 0.5 %collective-permute-start = (f32[3,6,16,128]{3,2,1,0:T(8,128)S(1)}, f32[3,6,16,128]{3,2,1,0:T(8,128)S(1)}, u32[]{:S(2)}, u32[]{:S(2)}) collective-permute-start(f32[3,6,16,128]{3,2,1,0:T(8,128)S(1)} %get-tuple-element.33), channel_id=1, source_target_pairs={{0,1},{1,0},{2,3},{3,2},{4,5},{5,4},{6,7},{7,6},{8,9},{9,8},{10,11... | collective-permute-start | bytes 442376 | tf_op jit(solution)/shard_map/ppermute | solution.py:351
  1.5 2.6 %collective-permute-start.1 = (f32[3,6,16,128]{3,2,1,0:T(8,128)S(1)}, f32[3,6,16,128]{3,2,1,0:T(8,128)S(1)}, u32[]{:S(2)}, u32[]{:S(2)}) collective-permute-start(f32[3,6,16,128]{3,2,1,0:T(8,128)S(1)} %get-tuple-element.38), channel_id=1, source_target_pairs={{0,3},{1,2},{2,1},{3,0},{4,7},{5,6},{6,5},{7,4},{8,11},{9,10},{10,... | collective-permute-start | bytes 442376 | tf_op jit(solution)/shard_map/ppermute | solution.py:351
  4.2 0.8 %shard_map.29 = (f32[6,2,3,3,2,8,128]{6,5,4,3,2,1,0:T(8,128)S(1)}, f32[4,3,2,8,128]{4,3,2,1,0:T(8,128)S(1)}, f32[2,6,3,2,8,128]{5,4,3,2,1,0:T(8,128)S(1)}, f32[8...) custom-call(f32[3,16,16,128]{3,2,1,0:T(8,128)S(1)} %bitcast.3, f32[16,16,128]{2,1,0:T(8,128)S(1)} %copy-done.1), custom_call_target="tpu_custom_call" | custom-call | flops 67108864 | bytes 1048576 | tf_op jit(solution)/shard_map/pallas_call | solution.py:26
  5.0 0.0 collective-permute-done.face_ref
  5.1 0.7 %shard_map.30 = (f32[5,3,8,128]{3,2,1,0:T(8,128)S(1)}, f32[5,3,8,128]{3,2,1,0:T(8,128)S(1)}, f32[5,3,8,128]{3,2,1,0:T(8,128)S(1)}, f32[5,3,8,128]{3,2,1,0:T(8,128)S(1)}) custom-call(f32[3,6,16,128]{3,2,1,0:T(8,128)S(1)} %collective-permute-done.face_ref, f32[6,2,3,3,2,8,128]{6,5,4,3,2,1,0:T(8,128)S(1)} %get-tuple-element.34.edges, ...), custom_call_target="tpu_custom_call" | custom-call | flops 4294967296 | bytes 1048576 | tf_op jit(solution)/shard_map/pallas_call | solution.py:26
  5.8 2.6 %collective-permute-start.2 = (f32[5,3,8,128]{3,2,1,0:T(8,128)S(1)}, f32[5,3,8,128]{3,2,1,0:T(8,128)S(1)}, u32[]{:S(2)}, u32[]{:S(2)}) collective-permute-start(f32[5,3,8,128]{3,2,1,0:T(8,128)S(1)} %get-tuple-element.41), channel_id=1, source_target_pairs={{0,12},{4,8},{8,4},{12,0},{16,28},{20,24},{24,20},{28,16},{1,13},{... | collective-permute-start | bytes 184328 | tf_op jit(solution)/shard_map/ppermute | solution.py:354
  8.4 0.4 %collective-permute-start.3 = (f32[5,3,8,128]{3,2,1,0:T(8,128)S(1)}, f32[5,3,8,128]{3,2,1,0:T(8,128)S(1)}, u32[]{:S(2)}, u32[]{:S(2)}) collective-permute-start(f32[5,3,8,128]{3,2,1,0:T(8,128)S(1)} %get-tuple-element.42), channel_id=1, source_target_pairs={{0,8},{4,12},{8,0},{12,4},{16,24},{20,28},{24,16},{28,20},{1,9},{5... | collective-permute-start | bytes 184328 | tf_op jit(solution)/shard_map/ppermute | solution.py:354
  8.8 0.5 %collective-permute-start.4 = (f32[5,3,8,128]{3,2,1,0:T(8,128)S(1)}, f32[5,3,8,128]{3,2,1,0:T(8,128)S(1)}, u32[]{:S(2)}, u32[]{:S(2)}) collective-permute-start(f32[5,3,8,128]{3,2,1,0:T(8,128)S(1)} %get-tuple-element.43), channel_id=1, source_target_pairs={{0,4},{4,0},{8,12},{12,8},{16,20},{20,16},{24,28},{28,24},{1,5},{5... | collective-permute-start | bytes 184328 | tf_op jit(solution)/shard_map/ppermute | solution.py:354
  9.3 0.7 %shard_map.31 = (f32[3,3,8,128]{3,2,1,0:T(8,128)S(1)}, f32[3,3,8,128]{3,2,1,0:T(8,128)S(1)}, f32[3,3,8,128]{3,2,1,0:T(8,128)S(1)}, f32[3,3,8,128]{3,2,1,0:T(8,128)S(1)}) custom-call(f32[3,6,16,128]{3,2,1,0:T(8,128)S(1)} %collective-permute-done.1.face_ref, f32[6,2,3,3,2,8,128]{6,5,4,3,2,1,0:T(8,128)S(1)} %get-tuple-element.34.edges, ...), custom_call_target="tpu_custom_call" | custom-call | flops 4294967296 | bytes 1048576 | tf_op jit(solution)/shard_map/pallas_call | solution.py:26
  10.0 2.6 %collective-permute-start.6 = (f32[3,3,8,128]{3,2,1,0:T(8,128)S(1)}, f32[3,3,8,128]{3,2,1,0:T(8,128)S(1)}, u32[]{:S(2)}, u32[]{:S(2)}) collective-permute-start(f32[3,3,8,128]{3,2,1,0:T(8,128)S(1)} %get-tuple-element.48), channel_id=1, source_target_pairs={{0,12},{4,8},{8,4},{12,0},{16,28},{20,24},{24,20},{28,16},{1,13},{... | collective-permute-start | bytes 110600 | tf_op jit(solution)/shard_map/ppermute | solution.py:354
  12.6 0.4 %collective-permute-start.7 = (f32[3,3,8,128]{3,2,1,0:T(8,128)S(1)}, f32[3,3,8,128]{3,2,1,0:T(8,128)S(1)}, u32[]{:S(2)}, u32[]{:S(2)}) collective-permute-start(f32[3,3,8,128]{3,2,1,0:T(8,128)S(1)} %get-tuple-element.49), channel_id=1, source_target_pairs={{0,8},{4,12},{8,0},{12,4},{16,24},{20,28},{24,16},{28,20},{1,9},{5... | collective-permute-start | bytes 110600 | tf_op jit(solution)/shard_map/ppermute | solution.py:354
  13.1 0.0 collective-permute-done.2.refs_1_
  13.1 0.5 %collective-permute-start.8 = (f32[3,3,8,128]{3,2,1,0:T(8,128)S(1)}, f32[3,3,8,128]{3,2,1,0:T(8,128)S(1)}, u32[]{:S(2)}, u32[]{:S(2)}) collective-permute-start(f32[3,3,8,128]{3,2,1,0:T(8,128)S(1)} %get-tuple-element.50), channel_id=1, source_target_pairs={{0,4},{4,0},{8,12},{12,8},{16,20},{20,16},{24,28},{28,24},{1,5},{5... | collective-permute-start | bytes 110600 | tf_op jit(solution)/shard_map/ppermute | solution.py:354
  13.7 2.7 %collective-permute-start.5 = (f32[5,3,8,128]{3,2,1,0:T(8,128)S(1)}, f32[5,3,8,128]{3,2,1,0:T(8,128)S(1)}, u32[]{:S(2)}, u32[]{:S(2)}) collective-permute-start(f32[5,3,8,128]{3,2,1,0:T(8,128)S(1)} %shard_map.32), channel_id=1, source_target_pairs={{0,16},{4,20},{8,24},{12,28},{16,0},{20,4},{24,8},{28,12},{1,17},{... | collective-permute-start | bytes 184328 | tf_op jit(solution)/shard_map/ppermute | solution.py:361
  16.3 0.0 collective-permute-done.6.refs_1_
  16.3 0.3 %collective-permute-done.7.refs_2_ = f32[3,3,8,128]{3,2,1,0:T(8,128)S(1)} collective-permute-done((f32[3,3,8,128]{3,2,1,0:T(8,128)S(1)}, f32[3,3,8,128]{3,2,1,0:T(8,128)S(1)}, u32[]{:S(2)}, u32[]{:S(2)}) %collective-permute-start.7) | collective-permute-done | bytes 36896 | tf_op jit(solution)/shard_map/ppermute | solution.py:354
  16.7 0.4 %collective-permute-done.8.refs_3_ = f32[3,3,8,128]{3,2,1,0:T(8,128)S(1)} collective-permute-done((f32[3,3,8,128]{3,2,1,0:T(8,128)S(1)}, f32[3,3,8,128]{3,2,1,0:T(8,128)S(1)}, u32[]{:S(2)}, u32[]{:S(2)}) %collective-permute-start.8) | collective-permute-done | bytes 36896 | tf_op jit(solution)/shard_map/ppermute | solution.py:354
  17.1 2.7 %collective-permute-start.9 = (f32[3,3,8,128]{3,2,1,0:T(8,128)S(1)}, f32[3,3,8,128]{3,2,1,0:T(8,128)S(1)}, u32[]{:S(2)}, u32[]{:S(2)}) collective-permute-start(f32[3,3,8,128]{3,2,1,0:T(8,128)S(1)} %shard_map.34), channel_id=1, source_target_pairs={{0,16},{4,20},{8,24},{12,28},{16,0},{20,4},{24,8},{28,12},{1,17},{... | collective-permute-start | bytes 110600 | tf_op jit(solution)/shard_map/ppermute | solution.py:361
  19.7 0.1 shard_map.33
  19.8 1.6 %collective-permute-start.11 = (f32[5,3,8,128]{3,2,1,0:T(8,128)S(1)}, f32[5,3,8,128]{3,2,1,0:T(8,128)S(1)}, u32[]{:S(2)}, u32[]{:S(2)}) collective-permute-start(f32[5,3,8,128]{3,2,1,0:T(8,128)S(1)} %get-tuple-element.53), channel_id=1, source_target_pairs={{0,8},{4,12},{8,0},{12,4},{16,24},{20,28},{24,16},{28,20},{1,9},{5... | collective-permute-start | bytes 184328 | tf_op jit(solution)/shard_map/ppermute | solution.py:354
  21.4 0.9 %collective-permute-start.12 = (f32[5,3,8,128]{3,2,1,0:T(8,128)S(1)}, f32[5,3,8,128]{3,2,1,0:T(8,128)S(1)}, u32[]{:S(2)}, u32[]{:S(2)}) collective-permute-start(f32[5,3,8,128]{3,2,1,0:T(8,128)S(1)} %get-tuple-element.54), channel_id=1, source_target_pairs={{0,4},{4,0},{8,12},{12,8},{16,20},{20,16},{24,28},{28,24},{1,5},{5... | collective-permute-start | bytes 184328 | tf_op jit(solution)/shard_map/ppermute | solution.py:354
  22.4 0.0 collective-permute-done.9.carry_ref
  22.4 1.5 %collective-permute-start.10 = (f32[8,3,8,128]{3,2,1,0:T(8,128)S(1)}, f32[8,3,8,128]{3,2,1,0:T(8,128)S(1)}, u32[]{:S(2)}, u32[]{:S(2)}) collective-permute-start(f32[8,3,8,128]{3,2,1,0:T(8,128)S(1)} %get-tuple-element.52), channel_id=1, source_target_pairs={{0,12},{4,8},{8,4},{12,0},{16,28},{20,24},{24,20},{28,16},{1,13},{... | collective-permute-start | bytes 294920 | tf_op jit(solution)/shard_map/ppermute | solution.py:354
  23.9 1.1 %collective-permute-start.13 = (f32[3,3,8,128]{3,2,1,0:T(8,128)S(1)}, f32[3,3,8,128]{3,2,1,0:T(8,128)S(1)}, u32[]{:S(2)}, u32[]{:S(2)}) collective-permute-start(f32[3,3,8,128]{3,2,1,0:T(8,128)S(1)} %get-tuple-element.57), channel_id=1, source_target_pairs={{0,8},{4,12},{8,0},{12,4},{16,24},{20,28},{24,16},{28,20},{1,9},{5... | collective-permute-start | bytes 110600 | tf_op jit(solution)/shard_map/ppermute | solution.py:354
  25.0 0.9 %collective-permute-start.14 = (f32[3,3,8,128]{3,2,1,0:T(8,128)S(1)}, f32[3,3,8,128]{3,2,1,0:T(8,128)S(1)}, u32[]{:S(2)}, u32[]{:S(2)}) collective-permute-start(f32[3,3,8,128]{3,2,1,0:T(8,128)S(1)} %get-tuple-element.58), channel_id=1, source_target_pairs={{0,4},{4,0},{8,12},{12,8},{16,20},{20,16},{24,28},{28,24},{1,5},{5... | collective-permute-start | bytes 110600 | tf_op jit(solution)/shard_map/ppermute | solution.py:354
  26.0 0.0 collective-permute-done.11.early_back
  26.0 0.0 collective-permute-done.12.early_side
  26.0 2.0 %collective-permute-done.10.across = f32[8,3,8,128]{3,2,1,0:T(8,128)S(1)} collective-permute-done((f32[8,3,8,128]{3,2,1,0:T(8,128)S(1)}, f32[8,3,8,128]{3,2,1,0:T(8,128)S(1)}, u32[]{:S(2)}, u32[]{:S(2)}) %collective-permute-start.10) | collective-permute-done | bytes 98336 | tf_op jit(solution)/shard_map/ppermute | solution.py:354
  28.0 0.1 shard_map.36.gathered
  28.1 0.8 %shard_map.38._ = f32[3,16,16,128]{3,2,1,0:T(8,128)} custom-call(f32[16,3,2,8,128]{4,3,2,1,0:T(8,128)S(1)} %get-tuple-element.60.kept), custom_call_target="tpu_custom_call" | custom-call | flops 4294967296 | bytes 1048576 | tf_op jit(solution)/shard_map/pallas_call | solution.py:437
  28.9 0.1 collective-permute-done.14.late_side
  (14 shorter events, 0.2 us)
Async XLA Ops:
  0.0 1.0 %copy-start = (f32[1,3,16,16,128]{4,3,2,1,0:T(8,128)S(1)}, f32[1,3,16,16,128]{4,3,2,1,0:T(8,128)}, u32[]{:S(2)}) copy-start(f32[1,3,16,16,128]{4,3,2,1,0:T(8,128)} %param.2) | copy-start | bytes 1179652
  1.0 3.2 %copy-start.1 = (f32[16,16,128]{2,1,0:T(8,128)S(1)}, f32[16,16,128]{2,1,0:T(8,128)}, u32[]{:S(2)}) copy-start(f32[16,16,128]{2,1,0:T(8,128)} %rate_ref.1) | copy-start | bytes 393220
  1.0 4.0 %collective-permute-start = (f32[3,6,16,128]{3,2,1,0:T(8,128)S(1)}, f32[3,6,16,128]{3,2,1,0:T(8,128)S(1)}, u32[]{:S(2)}, u32[]{:S(2)}) collective-permute-start(f32[3,6,16,128]{3,2,1,0:T(8,128)S(1)} %get-tuple-element.33), channel_id=1, source_target_pairs={{0,1},{1,0},{2,3},{3,2},{4,5},{5,4},{6,7},{7,6},{8,9},{9,8},{10,11... | collective-permute-start | bytes 442376 | tf_op jit(solution)/shard_map/ppermute | solution.py:351
  1.5 7.8 %collective-permute-start.1 = (f32[3,6,16,128]{3,2,1,0:T(8,128)S(1)}, f32[3,6,16,128]{3,2,1,0:T(8,128)S(1)}, u32[]{:S(2)}, u32[]{:S(2)}) collective-permute-start(f32[3,6,16,128]{3,2,1,0:T(8,128)S(1)} %get-tuple-element.38), channel_id=1, source_target_pairs={{0,3},{1,2},{2,1},{3,0},{4,7},{5,6},{6,5},{7,4},{8,11},{9,10},{10,... | collective-permute-start | bytes 442376 | tf_op jit(solution)/shard_map/ppermute | solution.py:351
  5.8 7.3 %collective-permute-start.2 = (f32[5,3,8,128]{3,2,1,0:T(8,128)S(1)}, f32[5,3,8,128]{3,2,1,0:T(8,128)S(1)}, u32[]{:S(2)}, u32[]{:S(2)}) collective-permute-start(f32[5,3,8,128]{3,2,1,0:T(8,128)S(1)} %get-tuple-element.41), channel_id=1, source_target_pairs={{0,12},{4,8},{8,4},{12,0},{16,28},{20,24},{24,20},{28,16},{1,13},{... | collective-permute-start | bytes 184328 | tf_op jit(solution)/shard_map/ppermute | solution.py:354
  8.4 5.3 %collective-permute-start.3 = (f32[5,3,8,128]{3,2,1,0:T(8,128)S(1)}, f32[5,3,8,128]{3,2,1,0:T(8,128)S(1)}, u32[]{:S(2)}, u32[]{:S(2)}) collective-permute-start(f32[5,3,8,128]{3,2,1,0:T(8,128)S(1)} %get-tuple-element.42), channel_id=1, source_target_pairs={{0,8},{4,12},{8,0},{12,4},{16,24},{20,28},{24,16},{28,20},{1,9},{5... | collective-permute-start | bytes 184328 | tf_op jit(solution)/shard_map/ppermute | solution.py:354
  8.8 4.8 %collective-permute-start.4 = (f32[5,3,8,128]{3,2,1,0:T(8,128)S(1)}, f32[5,3,8,128]{3,2,1,0:T(8,128)S(1)}, u32[]{:S(2)}, u32[]{:S(2)}) collective-permute-start(f32[5,3,8,128]{3,2,1,0:T(8,128)S(1)} %get-tuple-element.43), channel_id=1, source_target_pairs={{0,4},{4,0},{8,12},{12,8},{16,20},{20,16},{24,28},{28,24},{1,5},{5... | collective-permute-start | bytes 184328 | tf_op jit(solution)/shard_map/ppermute | solution.py:354
  10.0 6.3 %collective-permute-start.6 = (f32[3,3,8,128]{3,2,1,0:T(8,128)S(1)}, f32[3,3,8,128]{3,2,1,0:T(8,128)S(1)}, u32[]{:S(2)}, u32[]{:S(2)}) collective-permute-start(f32[3,3,8,128]{3,2,1,0:T(8,128)S(1)} %get-tuple-element.48), channel_id=1, source_target_pairs={{0,12},{4,8},{8,4},{12,0},{16,28},{20,24},{24,20},{28,16},{1,13},{... | collective-permute-start | bytes 110600 | tf_op jit(solution)/shard_map/ppermute | solution.py:354
  12.6 4.0 %collective-permute-start.7 = (f32[3,3,8,128]{3,2,1,0:T(8,128)S(1)}, f32[3,3,8,128]{3,2,1,0:T(8,128)S(1)}, u32[]{:S(2)}, u32[]{:S(2)}) collective-permute-start(f32[3,3,8,128]{3,2,1,0:T(8,128)S(1)} %get-tuple-element.49), channel_id=1, source_target_pairs={{0,8},{4,12},{8,0},{12,4},{16,24},{20,28},{24,16},{28,20},{1,9},{5... | collective-permute-start | bytes 110600 | tf_op jit(solution)/shard_map/ppermute | solution.py:354
  13.1 4.0 %collective-permute-start.8 = (f32[3,3,8,128]{3,2,1,0:T(8,128)S(1)}, f32[3,3,8,128]{3,2,1,0:T(8,128)S(1)}, u32[]{:S(2)}, u32[]{:S(2)}) collective-permute-start(f32[3,3,8,128]{3,2,1,0:T(8,128)S(1)} %get-tuple-element.50), channel_id=1, source_target_pairs={{0,4},{4,0},{8,12},{12,8},{16,20},{20,16},{24,28},{28,24},{1,5},{5... | collective-permute-start | bytes 110600 | tf_op jit(solution)/shard_map/ppermute | solution.py:354
  13.7 6.1 %collective-permute-start.5 = (f32[5,3,8,128]{3,2,1,0:T(8,128)S(1)}, f32[5,3,8,128]{3,2,1,0:T(8,128)S(1)}, u32[]{:S(2)}, u32[]{:S(2)}) collective-permute-start(f32[5,3,8,128]{3,2,1,0:T(8,128)S(1)} %shard_map.32), channel_id=1, source_target_pairs={{0,16},{4,20},{8,24},{12,28},{16,0},{20,4},{24,8},{28,12},{1,17},{... | collective-permute-start | bytes 184328 | tf_op jit(solution)/shard_map/ppermute | solution.py:361
  17.1 5.3 %collective-permute-start.9 = (f32[3,3,8,128]{3,2,1,0:T(8,128)S(1)}, f32[3,3,8,128]{3,2,1,0:T(8,128)S(1)}, u32[]{:S(2)}, u32[]{:S(2)}) collective-permute-start(f32[3,3,8,128]{3,2,1,0:T(8,128)S(1)} %shard_map.34), channel_id=1, source_target_pairs={{0,16},{4,20},{8,24},{12,28},{16,0},{20,4},{24,8},{28,12},{1,17},{... | collective-permute-start | bytes 110600 | tf_op jit(solution)/shard_map/ppermute | solution.py:361
  19.8 6.2 %collective-permute-start.11 = (f32[5,3,8,128]{3,2,1,0:T(8,128)S(1)}, f32[5,3,8,128]{3,2,1,0:T(8,128)S(1)}, u32[]{:S(2)}, u32[]{:S(2)}) collective-permute-start(f32[5,3,8,128]{3,2,1,0:T(8,128)S(1)} %get-tuple-element.53), channel_id=1, source_target_pairs={{0,8},{4,12},{8,0},{12,4},{16,24},{20,28},{24,16},{28,20},{1,9},{5... | collective-permute-start | bytes 184328 | tf_op jit(solution)/shard_map/ppermute | solution.py:354
  21.4 4.5 %collective-permute-start.12 = (f32[5,3,8,128]{3,2,1,0:T(8,128)S(1)}, f32[5,3,8,128]{3,2,1,0:T(8,128)S(1)}, u32[]{:S(2)}, u32[]{:S(2)}) collective-permute-start(f32[5,3,8,128]{3,2,1,0:T(8,128)S(1)} %get-tuple-element.54), channel_id=1, source_target_pairs={{0,4},{4,0},{8,12},{12,8},{16,20},{20,16},{24,28},{28,24},{1,5},{5... | collective-permute-start | bytes 184328 | tf_op jit(solution)/shard_map/ppermute | solution.py:354
  22.4 5.6 %collective-permute-start.10 = (f32[8,3,8,128]{3,2,1,0:T(8,128)S(1)}, f32[8,3,8,128]{3,2,1,0:T(8,128)S(1)}, u32[]{:S(2)}, u32[]{:S(2)}) collective-permute-start(f32[8,3,8,128]{3,2,1,0:T(8,128)S(1)} %get-tuple-element.52), channel_id=1, source_target_pairs={{0,12},{4,8},{8,4},{12,0},{16,28},{20,24},{24,20},{28,16},{1,13},{... | collective-permute-start | bytes 294920 | tf_op jit(solution)/shard_map/ppermute | solution.py:354
  23.9 5.0 %collective-permute-start.13 = (f32[3,3,8,128]{3,2,1,0:T(8,128)S(1)}, f32[3,3,8,128]{3,2,1,0:T(8,128)S(1)}, u32[]{:S(2)}, u32[]{:S(2)}) collective-permute-start(f32[3,3,8,128]{3,2,1,0:T(8,128)S(1)} %get-tuple-element.57), channel_id=1, source_target_pairs={{0,8},{4,12},{8,0},{12,4},{16,24},{20,28},{24,16},{28,20},{1,9},{5... | collective-permute-start | bytes 110600 | tf_op jit(solution)/shard_map/ppermute | solution.py:354
  25.0 4.0 %collective-permute-start.14 = (f32[3,3,8,128]{3,2,1,0:T(8,128)S(1)}, f32[3,3,8,128]{3,2,1,0:T(8,128)S(1)}, u32[]{:S(2)}, u32[]{:S(2)}) collective-permute-start(f32[3,3,8,128]{3,2,1,0:T(8,128)S(1)} %get-tuple-element.58), channel_id=1, source_target_pairs={{0,4},{4,0},{8,12},{12,8},{16,20},{20,16},{24,28},{28,24},{1,5},{5... | collective-permute-start | bytes 110600 | tf_op jit(solution)/shard_map/ppermute | solution.py:354

commit v8 on v7

--- a/solution.py
+++ b/solution.py
@@ -265,14 +265,14 @@
         out[...] = order[lax.bitwise_xor(spot(), partner(k))]
 
 
-def late_kernel(across_ref, carry_ref, *refs):
+def late_kernel(across_ref, back_ref, carry_ref, *refs):
     jumps, damp_ref, outs, order = refs[:GROUP], refs[GROUP], refs[GROUP + 1 : -1], refs[-1]
     split = across_ref.shape[0]
     news_of(split, carry_ref, jumps, damp_ref, order)
     for k, out in enumerate(outs):
         value = order[lax.bitwise_xor(spot(), partner(k))]
-        if k == 1:
-            out[:split] = across_ref[...]
+        if k in (1, 2):
+            out[:split] = (across_ref if k == 1 else back_ref)[...]
             out[split:] = value
         else:
             out[...] = value
@@ -294,8 +294,7 @@
         write(whole, out, sem)
 
 
-def pass_kernel(back_ref, side_ref, back, side):
-    back[...] = back_ref[...]
+def pass_kernel(side_ref, side):
     side[...] = side_ref[...]
 
 
@@ -319,19 +318,19 @@
                         whole[c, layer, pl.ds(odd, rows, stride=2), :] = piece[j - first, c]
 
 
-def gather_kernel(early_own, late_own, across, early_back, early_side, whole):
+def gather_kernel(early_own, late_own, across, back, early_side, whole):
     split = early_own.shape[0]
-    held = ((0, 0, early_own), (0, split, late_own), (1, 0, across))
-    put(whole, held + ((2, 0, early_back), (3, 0, early_side)))
-
-
-def finish_kernel(gathered, late_back, late_side, _, out, whole, sem):
+    held = ((0, 0, early_own), (0, split, late_own), (1, 0, across), (3, 0, early_side))
+    put(whole, held + ((2, 0, back),))
+
+
+def finish_kernel(gathered, late_side, _, out, whole, sem):
     split = (whole.shape[1] - STAGES) // 2
 
     @pl.when(lax.axis_index("tm") != 0)
     def _():
         whole[...] = gathered[...]
-        put(whole, ((2, split, late_back), (3, split, late_side)))
+        put(whole, ((3, split, late_side),))
         write(whole, out, sem)
 
 
@@ -420,19 +419,19 @@
         early_kernel, [shares[0]] * GROUP, carries[0], *halves[0], damp, scratch=[orders[0]],
         flops=BUSY,
     )
-    back, side = exchange(early[2], 2), exchange(early[3], 3)
+    side = exchange(early[3], 3)
     late = call(
-        late_kernel, [shares[1], whole_share, shares[1], shares[1]],
-        early[1], carries[1], *halves[1], damp,
+        late_kernel, [shares[1], whole_share, whole_share, shares[1]],
+        early[1], early[2], carries[1], *halves[1], damp,
         scratch=[orders[1]],
         flops=BUSY,
     )
-    late = [*late[:2], *call(pass_kernel, [shares[1]] * 2, *late[2:], flops=BUSY)]
-    late_own, across, late_back, late_side = swap(late)
+    late = [*late[:3], call(pass_kernel, shares[1], late[3], flops=BUSY)]
+    late_own, across, back, late_side = swap(late)
     gathered = call(
         gather_kernel, f32(*own.shape), early[0], late_own, across, back, side, flops=BUSY
     )
-    pieces = [gathered, late_back, late_side]
+    pieces = [gathered, late_side]
     whole = [pltpu.VMEM(own.shape, jnp.float32), pltpu.SemaphoreType.DMA]
     updated = pl.pallas_call(
         first_kernel,
@@ -442,7 +441,7 @@
         scratch_shapes=whole,
         compiler_params=PARAMS,
         cost_estimate=pl.CostEstimate(flops=BUSY, bytes_accessed=1 << 20, transcendentals=0),
-    )(after(kept, gathered))
+    )(after(kept, early[0]))
     updated = pl.pallas_call(
         finish_kernel,
         out_shape=f32(*own.shape),

time: 29.2 us -> 28.8 us (0.986)
  starting transfers between devices: 21.7 us -> 19.3 us
  waiting for transfers between devices: 2.84 us -> 4.87 us
    ppermute x11 -> x10, starting transfers between devices: 13.2 us -> 10.9 us  [exchange(): lax.ppermute(value, 'tm', [(i, i ^ partner(k)) for i in range(slices)])]
    ppermute x2, waiting for transfers between devices: 0.01 us -> 1.2 us  [onward(): lax.ppermute(value, 'tm', [(i, (i + step) % slices) for i in range(slices)])]
    ppermute x11 -> x10, waiting for transfers between devices: 2.83 us -> 3.66 us  [exchange(): lax.ppermute(value, 'tm', [(i, i ^ partner(k)) for i in range(slices)])]
  transfers between devices with their start and end apart: 15 -> 14, of which waited for: 4 -> 5; matrix products, arithmetic and copies ran while one was open for 0% -> 0% of each run, Pallas kernels for 12% -> 12%
where the time goes in v8:
time: 28.8 us; the launch traced here: 28.7 us
  starting transfers between devices  19.3 us (67%)
  waiting for transfers between devices  4.87 us (17%)
  Pallas kernels  3.41 us (12%)
  local copies, waits for them, and re-layouts  1 us (3%)
    ppermute x10, starting transfers between devices, exchange(): lax.ppermute(value, 'tm', [(i, i ^ partner(k)) for i in range(slices)])  10.9 us
    ppermute x2, starting transfers between devices, onward(): lax.ppermute(value, 'tm', [(i, (i + step) % slices) for i in range(slices)])  5.31 us
    ppermute x10, waiting for transfers between devices, exchange(): lax.ppermute(value, 'tm', [(i, i ^ partner(k)) for i in range(slices)])  3.66 us
    ppermute x2, starting transfers between devices, halo(): return lax.ppermute(value, 'gz', [(i, j % slabs) for i, j in pairs])  3.16 us
    pallas_call x10, Pallas kernels, call(): pl.pallas_call(kernel, out_shape=out_shape, in_specs=[VMEM] * len(args),...  2.59 us
    ppermute x2, waiting for transfers between devices, onward(): lax.ppermute(value, 'tm', [(i, (i + step) % slices) for i in range(slices)])  1.2 us
    unnamed x4, local copies, waits for them, and re-layouts  1 us
    pallas_call x1, Pallas kernels, shards(): pl.pallas_call(first_kernel, out_shape=f32(*own.shape), in_specs=[VMEM],...  0.79 us
  transfers between devices with their start and end apart: 14, of which 5 were waited for; matrix products, arithmetic and copies ran while one was open for 0% of the time, Pallas kernels for 12%

profile of v8, /device:TPU:0, one launch (start us, length us, event | category | flops | bytes accessed | tf_op | source)
XLA Modules:
  0.0 28.7 jit_solution(14227622001470485799)
XLA Ops:
  0.0 1.0 %copy-done = f32[1,3,16,16,128]{4,3,2,1,0:T(8,128)S(1)} copy-done((f32[1,3,16,16,128]{4,3,2,1,0:T(8,128)S(1)}, f32[1,3,16,16,128]{4,3,2,1,0:T(8,128)}, u32[]{:S(2)}) %copy-start) | copy-done | bytes 393240
  1.0 0.5 %collective-permute-start = (f32[3,6,16,128]{3,2,1,0:T(8,128)S(1)}, f32[3,6,16,128]{3,2,1,0:T(8,128)S(1)}, u32[]{:S(2)}, u32[]{:S(2)}) collective-permute-start(f32[3,6,16,128]{3,2,1,0:T(8,128)S(1)} %get-tuple-element.31), channel_id=1, source_target_pairs={{0,1},{1,0},{2,3},{3,2},{4,5},{5,4},{6,7},{7,6},{8,9},{9,8},{10,11... | collective-permute-start | bytes 442376 | tf_op jit(solution)/shard_map/ppermute | solution.py:350
  1.5 2.6 %collective-permute-start.1 = (f32[3,6,16,128]{3,2,1,0:T(8,128)S(1)}, f32[3,6,16,128]{3,2,1,0:T(8,128)S(1)}, u32[]{:S(2)}, u32[]{:S(2)}) collective-permute-start(f32[3,6,16,128]{3,2,1,0:T(8,128)S(1)} %get-tuple-element.36), channel_id=1, source_target_pairs={{0,3},{1,2},{2,1},{3,0},{4,7},{5,6},{6,5},{7,4},{8,11},{9,10},{10,... | collective-permute-start | bytes 442376 | tf_op jit(solution)/shard_map/ppermute | solution.py:350
  4.2 0.8 %shard_map.29 = (f32[6,2,3,3,2,8,128]{6,5,4,3,2,1,0:T(8,128)S(1)}, f32[4,3,2,8,128]{4,3,2,1,0:T(8,128)S(1)}, f32[2,6,3,2,8,128]{5,4,3,2,1,0:T(8,128)S(1)}, f32[8...) custom-call(f32[3,16,16,128]{3,2,1,0:T(8,128)S(1)} %bitcast.3, f32[16,16,128]{2,1,0:T(8,128)S(1)} %copy-done.1), custom_call_target="tpu_custom_call" | custom-call | flops 67108864 | bytes 1048576 | tf_op jit(solution)/shard_map/pallas_call | solution.py:26
  5.0 0.0 collective-permute-done.face_ref
  5.1 0.7 %shard_map.30 = (f32[5,3,8,128]{3,2,1,0:T(8,128)S(1)}, f32[5,3,8,128]{3,2,1,0:T(8,128)S(1)}, f32[5,3,8,128]{3,2,1,0:T(8,128)S(1)}, f32[5,3,8,128]{3,2,1,0:T(8,128)S(1)}) custom-call(f32[3,6,16,128]{3,2,1,0:T(8,128)S(1)} %collective-permute-done.face_ref, f32[6,2,3,3,2,8,128]{6,5,4,3,2,1,0:T(8,128)S(1)} %get-tuple-element.32.edges, ...), custom_call_target="tpu_custom_call" | custom-call | flops 4294967296 | bytes 1048576 | tf_op jit(solution)/shard_map/pallas_call | solution.py:26
  5.8 2.6 %collective-permute-start.2 = (f32[5,3,8,128]{3,2,1,0:T(8,128)S(1)}, f32[5,3,8,128]{3,2,1,0:T(8,128)S(1)}, u32[]{:S(2)}, u32[]{:S(2)}) collective-permute-start(f32[5,3,8,128]{3,2,1,0:T(8,128)S(1)} %get-tuple-element.39), channel_id=1, source_target_pairs={{0,12},{4,8},{8,4},{12,0},{16,28},{20,24},{24,20},{28,16},{1,13},{... | collective-permute-start | bytes 184328 | tf_op jit(solution)/shard_map/ppermute | solution.py:353
  8.4 0.4 %collective-permute-start.3 = (f32[5,3,8,128]{3,2,1,0:T(8,128)S(1)}, f32[5,3,8,128]{3,2,1,0:T(8,128)S(1)}, u32[]{:S(2)}, u32[]{:S(2)}) collective-permute-start(f32[5,3,8,128]{3,2,1,0:T(8,128)S(1)} %get-tuple-element.40), channel_id=1, source_target_pairs={{0,8},{4,12},{8,0},{12,4},{16,24},{20,28},{24,16},{28,20},{1,9},{5... | collective-permute-start | bytes 184328 | tf_op jit(solution)/shard_map/ppermute | solution.py:353
  8.8 0.5 %collective-permute-start.4 = (f32[5,3,8,128]{3,2,1,0:T(8,128)S(1)}, f32[5,3,8,128]{3,2,1,0:T(8,128)S(1)}, u32[]{:S(2)}, u32[]{:S(2)}) collective-permute-start(f32[5,3,8,128]{3,2,1,0:T(8,128)S(1)} %get-tuple-element.41), channel_id=1, source_target_pairs={{0,4},{4,0},{8,12},{12,8},{16,20},{20,16},{24,28},{28,24},{1,5},{5... | collective-permute-start | bytes 184328 | tf_op jit(solution)/shard_map/ppermute | solution.py:353
  9.3 0.7 %shard_map.31 = (f32[3,3,8,128]{3,2,1,0:T(8,128)S(1)}, f32[3,3,8,128]{3,2,1,0:T(8,128)S(1)}, f32[3,3,8,128]{3,2,1,0:T(8,128)S(1)}, f32[3,3,8,128]{3,2,1,0:T(8,128)S(1)}) custom-call(f32[3,6,16,128]{3,2,1,0:T(8,128)S(1)} %collective-permute-done.1.face_ref, f32[6,2,3,3,2,8,128]{6,5,4,3,2,1,0:T(8,128)S(1)} %get-tuple-element.32.edges, ...), custom_call_target="tpu_custom_call" | custom-call | flops 4294967296 | bytes 1048576 | tf_op jit(solution)/shard_map/pallas_call | solution.py:26
  10.0 2.6 %collective-permute-start.6 = (f32[3,3,8,128]{3,2,1,0:T(8,128)S(1)}, f32[3,3,8,128]{3,2,1,0:T(8,128)S(1)}, u32[]{:S(2)}, u32[]{:S(2)}) collective-permute-start(f32[3,3,8,128]{3,2,1,0:T(8,128)S(1)} %get-tuple-element.47), channel_id=1, source_target_pairs={{0,12},{4,8},{8,4},{12,0},{16,28},{20,24},{24,20},{28,16},{1,13},{... | collective-permute-start | bytes 110600 | tf_op jit(solution)/shard_map/ppermute | solution.py:353
  12.6 0.4 %collective-permute-start.7 = (f32[3,3,8,128]{3,2,1,0:T(8,128)S(1)}, f32[3,3,8,128]{3,2,1,0:T(8,128)S(1)}, u32[]{:S(2)}, u32[]{:S(2)}) collective-permute-start(f32[3,3,8,128]{3,2,1,0:T(8,128)S(1)} %get-tuple-element.48), channel_id=1, source_target_pairs={{0,8},{4,12},{8,0},{12,4},{16,24},{20,28},{24,16},{28,20},{1,9},{5... | collective-permute-start | bytes 110600 | tf_op jit(solution)/shard_map/ppermute | solution.py:353
  13.1 0.5 %collective-permute-start.8 = (f32[3,3,8,128]{3,2,1,0:T(8,128)S(1)}, f32[3,3,8,128]{3,2,1,0:T(8,128)S(1)}, u32[]{:S(2)}, u32[]{:S(2)}) collective-permute-start(f32[3,3,8,128]{3,2,1,0:T(8,128)S(1)} %get-tuple-element.49), channel_id=1, source_target_pairs={{0,4},{4,0},{8,12},{12,8},{16,20},{20,16},{24,28},{28,24},{1,5},{5... | collective-permute-start | bytes 110600 | tf_op jit(solution)/shard_map/ppermute | solution.py:353
  13.6 0.0 collective-permute-done.3.refs_2_
  13.6 0.0 collective-permute-done.4.refs_3_
  13.7 2.7 %collective-permute-start.5 = (f32[5,3,8,128]{3,2,1,0:T(8,128)S(1)}, f32[5,3,8,128]{3,2,1,0:T(8,128)S(1)}, u32[]{:S(2)}, u32[]{:S(2)}) collective-permute-start(f32[5,3,8,128]{3,2,1,0:T(8,128)S(1)} %shard_map.32), channel_id=1, source_target_pairs={{0,16},{4,20},{8,24},{12,28},{16,0},{20,4},{24,8},{28,12},{1,17},{... | collective-permute-start | bytes 184328 | tf_op jit(solution)/shard_map/ppermute | solution.py:360
  16.3 0.3 %collective-permute-done.7.refs_2_ = f32[3,3,8,128]{3,2,1,0:T(8,128)S(1)} collective-permute-done((f32[3,3,8,128]{3,2,1,0:T(8,128)S(1)}, f32[3,3,8,128]{3,2,1,0:T(8,128)S(1)}, u32[]{:S(2)}, u32[]{:S(2)}) %collective-permute-start.7) | collective-permute-done | bytes 36896 | tf_op jit(solution)/shard_map/ppermute | solution.py:353
  16.7 0.4 %collective-permute-done.8.refs_3_ = f32[3,3,8,128]{3,2,1,0:T(8,128)S(1)} collective-permute-done((f32[3,3,8,128]{3,2,1,0:T(8,128)S(1)}, f32[3,3,8,128]{3,2,1,0:T(8,128)S(1)}, u32[]{:S(2)}, u32[]{:S(2)}) %collective-permute-start.8) | collective-permute-done | bytes 36896 | tf_op jit(solution)/shard_map/ppermute | solution.py:353
  17.1 2.7 %collective-permute-start.9 = (f32[3,3,8,128]{3,2,1,0:T(8,128)S(1)}, f32[3,3,8,128]{3,2,1,0:T(8,128)S(1)}, u32[]{:S(2)}, u32[]{:S(2)}) collective-permute-start(f32[3,3,8,128]{3,2,1,0:T(8,128)S(1)} %shard_map.34), channel_id=1, source_target_pairs={{0,16},{4,20},{8,24},{12,28},{16,0},{20,4},{24,8},{28,12},{1,17},{... | collective-permute-start | bytes 110600 | tf_op jit(solution)/shard_map/ppermute | solution.py:360
  19.7 0.0 collective-permute-done.5.carry_ref
  19.7 0.1 shard_map.33
  19.8 0.8 %shard_map.38._ = f32[3,16,16,128]{3,2,1,0:T(8,128)} custom-call(f32[16,3,2,8,128]{4,3,2,1,0:T(8,128)S(1)} %get-tuple-element.56.kept), custom_call_target="tpu_custom_call" | custom-call | flops 4294967296 | bytes 1048576 | tf_op jit(solution)/shard_map/pallas_call | solution.py:436
  20.6 0.2 collective-permute-start.12
  20.8 1.2 %collective-permute-done.9.carry_ref = f32[3,3,8,128]{3,2,1,0:T(8,128)S(1)} collective-permute-done((f32[3,3,8,128]{3,2,1,0:T(8,128)S(1)}, f32[3,3,8,128]{3,2,1,0:T(8,128)S(1)}, u32[]{:S(2)}, u32[]{:S(2)}) %collective-permute-start.9) | collective-permute-done | bytes 36896 | tf_op jit(solution)/shard_map/ppermute | solution.py:360
  22.0 0.1 shard_map.35
  22.0 1.9 %collective-permute-start.10 = (f32[8,3,8,128]{3,2,1,0:T(8,128)S(1)}, f32[8,3,8,128]{3,2,1,0:T(8,128)S(1)}, u32[]{:S(2)}, u32[]{:S(2)}) collective-permute-start(f32[8,3,8,128]{3,2,1,0:T(8,128)S(1)} %get-tuple-element.51), channel_id=1, source_target_pairs={{0,12},{4,8},{8,4},{12,0},{16,28},{20,24},{24,20},{28,16},{1,13},{... | collective-permute-start | bytes 294920 | tf_op jit(solution)/shard_map/ppermute | solution.py:353
  23.9 0.5 %collective-permute-start.11 = (f32[8,3,8,128]{3,2,1,0:T(8,128)S(1)}, f32[8,3,8,128]{3,2,1,0:T(8,128)S(1)}, u32[]{:S(2)}, u32[]{:S(2)}) collective-permute-start(f32[8,3,8,128]{3,2,1,0:T(8,128)S(1)} %get-tuple-element.52), channel_id=1, source_target_pairs={{0,8},{4,12},{8,0},{12,4},{16,24},{20,28},{24,16},{28,20},{1,9},{5... | collective-permute-start | bytes 294920 | tf_op jit(solution)/shard_map/ppermute | solution.py:353
  24.4 1.2 %collective-permute-start.13 = (f32[3,3,8,128]{3,2,1,0:T(8,128)S(1)}, f32[3,3,8,128]{3,2,1,0:T(8,128)S(1)}, u32[]{:S(2)}, u32[]{:S(2)}) collective-permute-start(f32[3,3,8,128]{3,2,1,0:T(8,128)S(1)} %shard_map.37), channel_id=1, source_target_pairs={{0,4},{4,0},{8,12},{12,8},{16,20},{20,16},{24,28},{28,24},{1,5},{5... | collective-permute-start | bytes 110600 | tf_op jit(solution)/shard_map/ppermute | solution.py:353
  25.6 0.0 collective-permute-done.12.early_side
  25.6 2.0 %collective-permute-done.10.across = f32[8,3,8,128]{3,2,1,0:T(8,128)S(1)} collective-permute-done((f32[8,3,8,128]{3,2,1,0:T(8,128)S(1)}, f32[8,3,8,128]{3,2,1,0:T(8,128)S(1)}, u32[]{:S(2)}, u32[]{:S(2)}) %collective-permute-start.10) | collective-permute-done | bytes 98336 | tf_op jit(solution)/shard_map/ppermute | solution.py:353
  27.6 0.9 %collective-permute-done.11.back = f32[8,3,8,128]{3,2,1,0:T(8,128)S(1)} collective-permute-done((f32[8,3,8,128]{3,2,1,0:T(8,128)S(1)}, f32[8,3,8,128]{3,2,1,0:T(8,128)S(1)}, u32[]{:S(2)}, u32[]{:S(2)}) %collective-permute-start.11) | collective-permute-done | bytes 98336 | tf_op jit(solution)/shard_map/ppermute | solution.py:353
  28.5 0.1 shard_map.36.gathered
  (12 shorter events, 0.1 us)
Async XLA Ops:
  0.0 1.0 %copy-start = (f32[1,3,16,16,128]{4,3,2,1,0:T(8,128)S(1)}, f32[1,3,16,16,128]{4,3,2,1,0:T(8,128)}, u32[]{:S(2)}) copy-start(f32[1,3,16,16,128]{4,3,2,1,0:T(8,128)} %param.2) | copy-start | bytes 1179652
  1.0 3.2 %copy-start.1 = (f32[16,16,128]{2,1,0:T(8,128)S(1)}, f32[16,16,128]{2,1,0:T(8,128)}, u32[]{:S(2)}) copy-start(f32[16,16,128]{2,1,0:T(8,128)} %rate_ref.1) | copy-start | bytes 393220
  1.0 4.0 %collective-permute-start = (f32[3,6,16,128]{3,2,1,0:T(8,128)S(1)}, f32[3,6,16,128]{3,2,1,0:T(8,128)S(1)}, u32[]{:S(2)}, u32[]{:S(2)}) collective-permute-start(f32[3,6,16,128]{3,2,1,0:T(8,128)S(1)} %get-tuple-element.31), channel_id=1, source_target_pairs={{0,1},{1,0},{2,3},{3,2},{4,5},{5,4},{6,7},{7,6},{8,9},{9,8},{10,11... | collective-permute-start | bytes 442376 | tf_op jit(solution)/shard_map/ppermute | solution.py:350
  1.5 7.8 %collective-permute-start.1 = (f32[3,6,16,128]{3,2,1,0:T(8,128)S(1)}, f32[3,6,16,128]{3,2,1,0:T(8,128)S(1)}, u32[]{:S(2)}, u32[]{:S(2)}) collective-permute-start(f32[3,6,16,128]{3,2,1,0:T(8,128)S(1)} %get-tuple-element.36), channel_id=1, source_target_pairs={{0,3},{1,2},{2,1},{3,0},{4,7},{5,6},{6,5},{7,4},{8,11},{9,10},{10,... | collective-permute-start | bytes 442376 | tf_op jit(solution)/shard_map/ppermute | solution.py:350
  5.8 7.3 %collective-permute-start.2 = (f32[5,3,8,128]{3,2,1,0:T(8,128)S(1)}, f32[5,3,8,128]{3,2,1,0:T(8,128)S(1)}, u32[]{:S(2)}, u32[]{:S(2)}) collective-permute-start(f32[5,3,8,128]{3,2,1,0:T(8,128)S(1)} %get-tuple-element.39), channel_id=1, source_target_pairs={{0,12},{4,8},{8,4},{12,0},{16,28},{20,24},{24,20},{28,16},{1,13},{... | collective-permute-start | bytes 184328 | tf_op jit(solution)/shard_map/ppermute | solution.py:353
  8.4 5.3 %collective-permute-start.3 = (f32[5,3,8,128]{3,2,1,0:T(8,128)S(1)}, f32[5,3,8,128]{3,2,1,0:T(8,128)S(1)}, u32[]{:S(2)}, u32[]{:S(2)}) collective-permute-start(f32[5,3,8,128]{3,2,1,0:T(8,128)S(1)} %get-tuple-element.40), channel_id=1, source_target_pairs={{0,8},{4,12},{8,0},{12,4},{16,24},{20,28},{24,16},{28,20},{1,9},{5... | collective-permute-start | bytes 184328 | tf_op jit(solution)/shard_map/ppermute | solution.py:353
  8.8 4.8 %collective-permute-start.4 = (f32[5,3,8,128]{3,2,1,0:T(8,128)S(1)}, f32[5,3,8,128]{3,2,1,0:T(8,128)S(1)}, u32[]{:S(2)}, u32[]{:S(2)}) collective-permute-start(f32[5,3,8,128]{3,2,1,0:T(8,128)S(1)} %get-tuple-element.41), channel_id=1, source_target_pairs={{0,4},{4,0},{8,12},{12,8},{16,20},{20,16},{24,28},{28,24},{1,5},{5... | collective-permute-start | bytes 184328 | tf_op jit(solution)/shard_map/ppermute | solution.py:353
  10.0 6.3 %collective-permute-start.6 = (f32[3,3,8,128]{3,2,1,0:T(8,128)S(1)}, f32[3,3,8,128]{3,2,1,0:T(8,128)S(1)}, u32[]{:S(2)}, u32[]{:S(2)}) collective-permute-start(f32[3,3,8,128]{3,2,1,0:T(8,128)S(1)} %get-tuple-element.47), channel_id=1, source_target_pairs={{0,12},{4,8},{8,4},{12,0},{16,28},{20,24},{24,20},{28,16},{1,13},{... | collective-permute-start | bytes 110600 | tf_op jit(solution)/shard_map/ppermute | solution.py:353
  12.6 4.0 %collective-permute-start.7 = (f32[3,3,8,128]{3,2,1,0:T(8,128)S(1)}, f32[3,3,8,128]{3,2,1,0:T(8,128)S(1)}, u32[]{:S(2)}, u32[]{:S(2)}) collective-permute-start(f32[3,3,8,128]{3,2,1,0:T(8,128)S(1)} %get-tuple-element.48), channel_id=1, source_target_pairs={{0,8},{4,12},{8,0},{12,4},{16,24},{20,28},{24,16},{28,20},{1,9},{5... | collective-permute-start | bytes 110600 | tf_op jit(solution)/shard_map/ppermute | solution.py:353
  13.1 4.0 %collective-permute-start.8 = (f32[3,3,8,128]{3,2,1,0:T(8,128)S(1)}, f32[3,3,8,128]{3,2,1,0:T(8,128)S(1)}, u32[]{:S(2)}, u32[]{:S(2)}) collective-permute-start(f32[3,3,8,128]{3,2,1,0:T(8,128)S(1)} %get-tuple-element.49), channel_id=1, source_target_pairs={{0,4},{4,0},{8,12},{12,8},{16,20},{20,16},{24,28},{28,24},{1,5},{5... | collective-permute-start | bytes 110600 | tf_op jit(solution)/shard_map/ppermute | solution.py:353
  13.7 6.1 %collective-permute-start.5 = (f32[5,3,8,128]{3,2,1,0:T(8,128)S(1)}, f32[5,3,8,128]{3,2,1,0:T(8,128)S(1)}, u32[]{:S(2)}, u32[]{:S(2)}) collective-permute-start(f32[5,3,8,128]{3,2,1,0:T(8,128)S(1)} %shard_map.32), channel_id=1, source_target_pairs={{0,16},{4,20},{8,24},{12,28},{16,0},{20,4},{24,8},{28,12},{1,17},{... | collective-permute-start | bytes 184328 | tf_op jit(solution)/shard_map/ppermute | solution.py:360
  17.1 4.9 %collective-permute-start.9 = (f32[3,3,8,128]{3,2,1,0:T(8,128)S(1)}, f32[3,3,8,128]{3,2,1,0:T(8,128)S(1)}, u32[]{:S(2)}, u32[]{:S(2)}) collective-permute-start(f32[3,3,8,128]{3,2,1,0:T(8,128)S(1)} %shard_map.34), channel_id=1, source_target_pairs={{0,16},{4,20},{8,24},{12,28},{16,0},{20,4},{24,8},{28,12},{1,17},{... | collective-permute-start | bytes 110600 | tf_op jit(solution)/shard_map/ppermute | solution.py:360
  20.6 5.0 %collective-permute-start.12 = (f32[5,3,8,128]{3,2,1,0:T(8,128)S(1)}, f32[5,3,8,128]{3,2,1,0:T(8,128)S(1)}, u32[]{:S(2)}, u32[]{:S(2)}) collective-permute-start(f32[5,3,8,128]{3,2,1,0:T(8,128)S(1)} %get-tuple-element.53), channel_id=1, source_target_pairs={{0,4},{4,0},{8,12},{12,8},{16,20},{20,16},{24,28},{28,24},{1,5},{5... | collective-permute-start | bytes 184328 | tf_op jit(solution)/shard_map/ppermute | solution.py:353
  22.0 5.6 %collective-permute-start.10 = (f32[8,3,8,128]{3,2,1,0:T(8,128)S(1)}, f32[8,3,8,128]{3,2,1,0:T(8,128)S(1)}, u32[]{:S(2)}, u32[]{:S(2)}) collective-permute-start(f32[8,3,8,128]{3,2,1,0:T(8,128)S(1)} %get-tuple-element.51), channel_id=1, source_target_pairs={{0,12},{4,8},{8,4},{12,0},{16,28},{20,24},{24,20},{28,16},{1,13},{... | collective-permute-start | bytes 294920 | tf_op jit(solution)/shard_map/ppermute | solution.py:353
  23.9 4.6 %collective-permute-start.11 = (f32[8,3,8,128]{3,2,1,0:T(8,128)S(1)}, f32[8,3,8,128]{3,2,1,0:T(8,128)S(1)}, u32[]{:S(2)}, u32[]{:S(2)}) collective-permute-start(f32[8,3,8,128]{3,2,1,0:T(8,128)S(1)} %get-tuple-element.52), channel_id=1, source_target_pairs={{0,8},{4,12},{8,0},{12,4},{16,24},{20,28},{24,16},{28,20},{1,9},{5... | collective-permute-start | bytes 294920 | tf_op jit(solution)/shard_map/ppermute | solution.py:353
  24.4 4.3 %collective-permute-start.13 = (f32[3,3,8,128]{3,2,1,0:T(8,128)S(1)}, f32[3,3,8,128]{3,2,1,0:T(8,128)S(1)}, u32[]{:S(2)}, u32[]{:S(2)}) collective-permute-start(f32[3,3,8,128]{3,2,1,0:T(8,128)S(1)} %shard_map.37), channel_id=1, source_target_pairs={{0,4},{4,0},{8,12},{12,8},{16,20},{20,16},{24,28},{28,24},{1,5},{5... | collective-permute-start | bytes 110600 | tf_op jit(solution)/shard_map/ppermute | solution.py:353

commit v9 on v8

--- a/solution.py
+++ b/solution.py
@@ -39,7 +39,7 @@
 
 
 def partner(k):
-    return (GROUP - k) % GROUP
+    return (0, 2, 3, 1)[k]
 
 
 def spot():

time: 28.8 us -> 29.7 us (1.031)
  waiting for transfers between devices: 4.87 us -> 5.68 us
    ppermute x10, waiting for transfers between devices: 3.66 us -> 4.59 us  [exchange(): lax.ppermute(value, 'tm', [(i, i ^ partner(k)) for i in range(slices)])]
  transfers between devices with their start and end apart: 14 -> 14, of which waited for: 5 -> 7; matrix products, arithmetic and copies ran while one was open for 0% -> 0% of each run, Pallas kernels for 12% -> 11%
where the time goes in v9:
time: 29.7 us; the launch traced here: 29.6 us
  starting transfers between devices  19.5 us (66%)
  waiting for transfers between devices  5.68 us (19%)
  Pallas kernels  3.39 us (11%)
  local copies, waits for them, and re-layouts  1 us (3%)
    ppermute x10, starting transfers between devices, exchange(): lax.ppermute(value, 'tm', [(i, i ^ partner(k)) for i in range(slices)])  11 us
    ppermute x2, starting transfers between devices, onward(): lax.ppermute(value, 'tm', [(i, (i + step) % slices) for i in range(slices)])  5.31 us
    ppermute x10, waiting for transfers between devices, exchange(): lax.ppermute(value, 'tm', [(i, i ^ partner(k)) for i in range(slices)])  4.59 us
    ppermute x2, starting transfers between devices, halo(): return lax.ppermute(value, 'gz', [(i, j % slabs) for i, j in pairs])  3.16 us
    pallas_call x10, Pallas kernels, call(): pl.pallas_call(kernel, out_shape=out_shape, in_specs=[VMEM] * len(args),...  2.59 us
    ppermute x2, waiting for transfers between devices, onward(): lax.ppermute(value, 'tm', [(i, (i + step) % slices) for i in range(slices)])  1.08 us
    unnamed x4, local copies, waits for them, and re-layouts  1 us
    pallas_call x1, Pallas kernels, shards(): pl.pallas_call(first_kernel, out_shape=f32(*own.shape), in_specs=[VMEM],...  0.79 us
  transfers between devices with their start and end apart: 14, of which 7 were waited for; matrix products, arithmetic and copies ran while one was open for 0% of the time, Pallas kernels for 11%

profile of v9, /device:TPU:0, one launch (start us, length us, event | category | flops | bytes accessed | tf_op | source)
XLA Modules:
  0.0 29.6 jit_solution(16860519215339813007)
XLA Ops:
  0.0 1.0 %copy-done = f32[1,3,16,16,128]{4,3,2,1,0:T(8,128)S(1)} copy-done((f32[1,3,16,16,128]{4,3,2,1,0:T(8,128)S(1)}, f32[1,3,16,16,128]{4,3,2,1,0:T(8,128)}, u32[]{:S(2)}) %copy-start) | copy-done | bytes 393240
  1.0 0.5 %collective-permute-start = (f32[3,6,16,128]{3,2,1,0:T(8,128)S(1)}, f32[3,6,16,128]{3,2,1,0:T(8,128)S(1)}, u32[]{:S(2)}, u32[]{:S(2)}) collective-permute-start(f32[3,6,16,128]{3,2,1,0:T(8,128)S(1)} %get-tuple-element.31), channel_id=1, source_target_pairs={{0,1},{1,0},{2,3},{3,2},{4,5},{5,4},{6,7},{7,6},{8,9},{9,8},{10,11... | collective-permute-start | bytes 442376 | tf_op jit(solution)/shard_map/ppermute | solution.py:350
  1.5 2.6 %collective-permute-start.1 = (f32[3,6,16,128]{3,2,1,0:T(8,128)S(1)}, f32[3,6,16,128]{3,2,1,0:T(8,128)S(1)}, u32[]{:S(2)}, u32[]{:S(2)}) collective-permute-start(f32[3,6,16,128]{3,2,1,0:T(8,128)S(1)} %get-tuple-element.36), channel_id=1, source_target_pairs={{0,3},{1,2},{2,1},{3,0},{4,7},{5,6},{6,5},{7,4},{8,11},{9,10},{10,... | collective-permute-start | bytes 442376 | tf_op jit(solution)/shard_map/ppermute | solution.py:350
  4.2 0.8 %shard_map.29 = (f32[6,2,3,3,2,8,128]{6,5,4,3,2,1,0:T(8,128)S(1)}, f32[4,3,2,8,128]{4,3,2,1,0:T(8,128)S(1)}, f32[2,6,3,2,8,128]{5,4,3,2,1,0:T(8,128)S(1)}, f32[8...) custom-call(f32[3,16,16,128]{3,2,1,0:T(8,128)S(1)} %bitcast.3, f32[16,16,128]{2,1,0:T(8,128)S(1)} %copy-done.1), custom_call_target="tpu_custom_call" | custom-call | flops 67108864 | bytes 1048576 | tf_op jit(solution)/shard_map/pallas_call | solution.py:26
  5.0 0.0 collective-permute-done.face_ref
  5.1 0.7 %shard_map.30 = (f32[5,3,8,128]{3,2,1,0:T(8,128)S(1)}, f32[5,3,8,128]{3,2,1,0:T(8,128)S(1)}, f32[5,3,8,128]{3,2,1,0:T(8,128)S(1)}, f32[5,3,8,128]{3,2,1,0:T(8,128)S(1)}) custom-call(f32[3,6,16,128]{3,2,1,0:T(8,128)S(1)} %collective-permute-done.face_ref, f32[6,2,3,3,2,8,128]{6,5,4,3,2,1,0:T(8,128)S(1)} %get-tuple-element.32.edges, ...), custom_call_target="tpu_custom_call" | custom-call | flops 4294967296 | bytes 1048576 | tf_op jit(solution)/shard_map/pallas_call | solution.py:26
  5.8 1.6 %collective-permute-start.2 = (f32[5,3,8,128]{3,2,1,0:T(8,128)S(1)}, f32[5,3,8,128]{3,2,1,0:T(8,128)S(1)}, u32[]{:S(2)}, u32[]{:S(2)}) collective-permute-start(f32[5,3,8,128]{3,2,1,0:T(8,128)S(1)} %get-tuple-element.39), channel_id=1, source_target_pairs={{0,8},{4,12},{8,0},{12,4},{16,24},{20,28},{24,16},{28,20},{1,9},{5... | collective-permute-start | bytes 184328 | tf_op jit(solution)/shard_map/ppermute | solution.py:353
  7.4 1.4 %collective-permute-start.3 = (f32[5,3,8,128]{3,2,1,0:T(8,128)S(1)}, f32[5,3,8,128]{3,2,1,0:T(8,128)S(1)}, u32[]{:S(2)}, u32[]{:S(2)}) collective-permute-start(f32[5,3,8,128]{3,2,1,0:T(8,128)S(1)} %get-tuple-element.40), channel_id=1, source_target_pairs={{0,12},{4,8},{8,4},{12,0},{16,28},{20,24},{24,20},{28,16},{1,13},{... | collective-permute-start | bytes 184328 | tf_op jit(solution)/shard_map/ppermute | solution.py:353
  8.8 0.5 %collective-permute-start.4 = (f32[5,3,8,128]{3,2,1,0:T(8,128)S(1)}, f32[5,3,8,128]{3,2,1,0:T(8,128)S(1)}, u32[]{:S(2)}, u32[]{:S(2)}) collective-permute-start(f32[5,3,8,128]{3,2,1,0:T(8,128)S(1)} %get-tuple-element.41), channel_id=1, source_target_pairs={{0,4},{4,0},{8,12},{12,8},{16,20},{20,16},{24,28},{28,24},{1,5},{5... | collective-permute-start | bytes 184328 | tf_op jit(solution)/shard_map/ppermute | solution.py:353
  9.3 0.0 collective-permute-done.1.face_ref
  9.3 0.7 %shard_map.31 = (f32[3,3,8,128]{3,2,1,0:T(8,128)S(1)}, f32[3,3,8,128]{3,2,1,0:T(8,128)S(1)}, f32[3,3,8,128]{3,2,1,0:T(8,128)S(1)}, f32[3,3,8,128]{3,2,1,0:T(8,128)S(1)}) custom-call(f32[3,6,16,128]{3,2,1,0:T(8,128)S(1)} %collective-permute-done.1.face_ref, f32[6,2,3,3,2,8,128]{6,5,4,3,2,1,0:T(8,128)S(1)} %get-tuple-element.32.edges, ...), custom_call_target="tpu_custom_call" | custom-call | flops 4294967296 | bytes 1048576 | tf_op jit(solution)/shard_map/pallas_call | solution.py:26
  10.0 1.6 %collective-permute-start.6 = (f32[3,3,8,128]{3,2,1,0:T(8,128)S(1)}, f32[3,3,8,128]{3,2,1,0:T(8,128)S(1)}, u32[]{:S(2)}, u32[]{:S(2)}) collective-permute-start(f32[3,3,8,128]{3,2,1,0:T(8,128)S(1)} %get-tuple-element.47), channel_id=1, source_target_pairs={{0,8},{4,12},{8,0},{12,4},{16,24},{20,28},{24,16},{28,20},{1,9},{5... | collective-permute-start | bytes 110600 | tf_op jit(solution)/shard_map/ppermute | solution.py:353
  11.7 1.4 %collective-permute-start.7 = (f32[3,3,8,128]{3,2,1,0:T(8,128)S(1)}, f32[3,3,8,128]{3,2,1,0:T(8,128)S(1)}, u32[]{:S(2)}, u32[]{:S(2)}) collective-permute-start(f32[3,3,8,128]{3,2,1,0:T(8,128)S(1)} %get-tuple-element.48), channel_id=1, source_target_pairs={{0,12},{4,8},{8,4},{12,0},{16,28},{20,24},{24,20},{28,16},{1,13},{... | collective-permute-start | bytes 110600 | tf_op jit(solution)/shard_map/ppermute | solution.py:353
  13.1 0.0 collective-permute-done.2.refs_1_
  13.1 0.5 %collective-permute-start.8 = (f32[3,3,8,128]{3,2,1,0:T(8,128)S(1)}, f32[3,3,8,128]{3,2,1,0:T(8,128)S(1)}, u32[]{:S(2)}, u32[]{:S(2)}) collective-permute-start(f32[3,3,8,128]{3,2,1,0:T(8,128)S(1)} %get-tuple-element.49), channel_id=1, source_target_pairs={{0,4},{4,0},{8,12},{12,8},{16,20},{20,16},{24,28},{28,24},{1,5},{5... | collective-permute-start | bytes 110600 | tf_op jit(solution)/shard_map/ppermute | solution.py:353
  13.7 2.7 %collective-permute-start.5 = (f32[5,3,8,128]{3,2,1,0:T(8,128)S(1)}, f32[5,3,8,128]{3,2,1,0:T(8,128)S(1)}, u32[]{:S(2)}, u32[]{:S(2)}) collective-permute-start(f32[5,3,8,128]{3,2,1,0:T(8,128)S(1)} %shard_map.32), channel_id=1, source_target_pairs={{0,16},{4,20},{8,24},{12,28},{16,0},{20,4},{24,8},{28,12},{1,17},{... | collective-permute-start | bytes 184328 | tf_op jit(solution)/shard_map/ppermute | solution.py:360
  16.3 0.0 collective-permute-done.6.refs_1_
  16.3 0.2 collective-permute-done.7.refs_2_
  16.5 0.5 %collective-permute-done.8.refs_3_ = f32[3,3,8,128]{3,2,1,0:T(8,128)S(1)} collective-permute-done((f32[3,3,8,128]{3,2,1,0:T(8,128)S(1)}, f32[3,3,8,128]{3,2,1,0:T(8,128)S(1)}, u32[]{:S(2)}, u32[]{:S(2)}) %collective-permute-start.8) | collective-permute-done | bytes 36896 | tf_op jit(solution)/shard_map/ppermute | solution.py:353
  17.1 2.7 %collective-permute-start.9 = (f32[3,3,8,128]{3,2,1,0:T(8,128)S(1)}, f32[3,3,8,128]{3,2,1,0:T(8,128)S(1)}, u32[]{:S(2)}, u32[]{:S(2)}) collective-permute-start(f32[3,3,8,128]{3,2,1,0:T(8,128)S(1)} %shard_map.34), channel_id=1, source_target_pairs={{0,16},{4,20},{8,24},{12,28},{16,0},{20,4},{24,8},{28,12},{1,17},{... | collective-permute-start | bytes 110600 | tf_op jit(solution)/shard_map/ppermute | solution.py:360
  19.7 0.1 shard_map.33
  19.8 0.8 %shard_map.38._ = f32[3,16,16,128]{3,2,1,0:T(8,128)} custom-call(f32[16,3,2,8,128]{4,3,2,1,0:T(8,128)S(1)} %get-tuple-element.56.kept), custom_call_target="tpu_custom_call" | custom-call | flops 4294967296 | bytes 1048576 | tf_op jit(solution)/shard_map/pallas_call | solution.py:436
  20.6 0.3 %collective-permute-start.12 = (f32[5,3,8,128]{3,2,1,0:T(8,128)S(1)}, f32[5,3,8,128]{3,2,1,0:T(8,128)S(1)}, u32[]{:S(2)}, u32[]{:S(2)}) collective-permute-start(f32[5,3,8,128]{3,2,1,0:T(8,128)S(1)} %get-tuple-element.53), channel_id=1, source_target_pairs={{0,4},{4,0},{8,12},{12,8},{16,20},{20,16},{24,28},{28,24},{1,5},{5... | collective-permute-start | bytes 184328 | tf_op jit(solution)/shard_map/ppermute | solution.py:353
  20.9 1.1 %collective-permute-done.9.carry_ref = f32[3,3,8,128]{3,2,1,0:T(8,128)S(1)} collective-permute-done((f32[3,3,8,128]{3,2,1,0:T(8,128)S(1)}, f32[3,3,8,128]{3,2,1,0:T(8,128)S(1)}, u32[]{:S(2)}, u32[]{:S(2)}) %collective-permute-start.9) | collective-permute-done | bytes 36896 | tf_op jit(solution)/shard_map/ppermute | solution.py:360
  22.0 1.6 %collective-permute-start.10 = (f32[8,3,8,128]{3,2,1,0:T(8,128)S(1)}, f32[8,3,8,128]{3,2,1,0:T(8,128)S(1)}, u32[]{:S(2)}, u32[]{:S(2)}) collective-permute-start(f32[8,3,8,128]{3,2,1,0:T(8,128)S(1)} %get-tuple-element.51), channel_id=1, source_target_pairs={{0,8},{4,12},{8,0},{12,4},{16,24},{20,28},{24,16},{28,20},{1,9},{5... | collective-permute-start | bytes 294920 | tf_op jit(solution)/shard_map/ppermute | solution.py:353
  23.7 0.9 %collective-permute-start.11 = (f32[8,3,8,128]{3,2,1,0:T(8,128)S(1)}, f32[8,3,8,128]{3,2,1,0:T(8,128)S(1)}, u32[]{:S(2)}, u32[]{:S(2)}) collective-permute-start(f32[8,3,8,128]{3,2,1,0:T(8,128)S(1)} %get-tuple-element.52), channel_id=1, source_target_pairs={{0,12},{4,8},{8,4},{12,0},{16,28},{20,24},{24,20},{28,16},{1,13},{... | collective-permute-start | bytes 294920 | tf_op jit(solution)/shard_map/ppermute | solution.py:353
  24.6 1.0 %collective-permute-start.13 = (f32[3,3,8,128]{3,2,1,0:T(8,128)S(1)}, f32[3,3,8,128]{3,2,1,0:T(8,128)S(1)}, u32[]{:S(2)}, u32[]{:S(2)}) collective-permute-start(f32[3,3,8,128]{3,2,1,0:T(8,128)S(1)} %shard_map.37), channel_id=1, source_target_pairs={{0,4},{4,0},{8,12},{12,8},{16,20},{20,16},{24,28},{28,24},{1,5},{5... | collective-permute-start | bytes 110600 | tf_op jit(solution)/shard_map/ppermute | solution.py:353
  25.6 0.5 %collective-permute-done.12.early_side = f32[5,3,8,128]{3,2,1,0:T(8,128)S(1)} collective-permute-done((f32[5,3,8,128]{3,2,1,0:T(8,128)S(1)}, f32[5,3,8,128]{3,2,1,0:T(8,128)S(1)}, u32[]{:S(2)}, u32[]{:S(2)}) %collective-permute-start.12) | collective-permute-done | bytes 61472 | tf_op jit(solution)/shard_map/ppermute | solution.py:353
  26.1 0.6 %collective-permute-done.10.across = f32[8,3,8,128]{3,2,1,0:T(8,128)S(1)} collective-permute-done((f32[8,3,8,128]{3,2,1,0:T(8,128)S(1)}, f32[8,3,8,128]{3,2,1,0:T(8,128)S(1)}, u32[]{:S(2)}, u32[]{:S(2)}) %collective-permute-start.10) | collective-permute-done | bytes 98336 | tf_op jit(solution)/shard_map/ppermute | solution.py:353
  26.7 2.6 %collective-permute-done.11.back = f32[8,3,8,128]{3,2,1,0:T(8,128)S(1)} collective-permute-done((f32[8,3,8,128]{3,2,1,0:T(8,128)S(1)}, f32[8,3,8,128]{3,2,1,0:T(8,128)S(1)}, u32[]{:S(2)}, u32[]{:S(2)}) %collective-permute-start.11) | collective-permute-done | bytes 98336 | tf_op jit(solution)/shard_map/ppermute | solution.py:353
  29.3 0.1 shard_map.36.gathered
  29.4 0.2 collective-permute-done.13.late_side
  (12 shorter events, 0.2 us)
Async XLA Ops:
  0.0 1.0 %copy-start = (f32[1,3,16,16,128]{4,3,2,1,0:T(8,128)S(1)}, f32[1,3,16,16,128]{4,3,2,1,0:T(8,128)}, u32[]{:S(2)}) copy-start(f32[1,3,16,16,128]{4,3,2,1,0:T(8,128)} %param.2) | copy-start | bytes 1179652
  1.0 3.2 %copy-start.1 = (f32[16,16,128]{2,1,0:T(8,128)S(1)}, f32[16,16,128]{2,1,0:T(8,128)}, u32[]{:S(2)}) copy-start(f32[16,16,128]{2,1,0:T(8,128)} %rate_ref.1) | copy-start | bytes 393220
  1.0 4.0 %collective-permute-start = (f32[3,6,16,128]{3,2,1,0:T(8,128)S(1)}, f32[3,6,16,128]{3,2,1,0:T(8,128)S(1)}, u32[]{:S(2)}, u32[]{:S(2)}) collective-permute-start(f32[3,6,16,128]{3,2,1,0:T(8,128)S(1)} %get-tuple-element.31), channel_id=1, source_target_pairs={{0,1},{1,0},{2,3},{3,2},{4,5},{5,4},{6,7},{7,6},{8,9},{9,8},{10,11... | collective-permute-start | bytes 442376 | tf_op jit(solution)/shard_map/ppermute | solution.py:350
  1.5 7.8 %collective-permute-start.1 = (f32[3,6,16,128]{3,2,1,0:T(8,128)S(1)}, f32[3,6,16,128]{3,2,1,0:T(8,128)S(1)}, u32[]{:S(2)}, u32[]{:S(2)}) collective-permute-start(f32[3,6,16,128]{3,2,1,0:T(8,128)S(1)} %get-tuple-element.36), channel_id=1, source_target_pairs={{0,3},{1,2},{2,1},{3,0},{4,7},{5,6},{6,5},{7,4},{8,11},{9,10},{10,... | collective-permute-start | bytes 442376 | tf_op jit(solution)/shard_map/ppermute | solution.py:350
  5.8 7.3 %collective-permute-start.2 = (f32[5,3,8,128]{3,2,1,0:T(8,128)S(1)}, f32[5,3,8,128]{3,2,1,0:T(8,128)S(1)}, u32[]{:S(2)}, u32[]{:S(2)}) collective-permute-start(f32[5,3,8,128]{3,2,1,0:T(8,128)S(1)} %get-tuple-element.39), channel_id=1, source_target_pairs={{0,8},{4,12},{8,0},{12,4},{16,24},{20,28},{24,16},{28,20},{1,9},{5... | collective-permute-start | bytes 184328 | tf_op jit(solution)/shard_map/ppermute | solution.py:353
  7.4 6.2 %collective-permute-start.3 = (f32[5,3,8,128]{3,2,1,0:T(8,128)S(1)}, f32[5,3,8,128]{3,2,1,0:T(8,128)S(1)}, u32[]{:S(2)}, u32[]{:S(2)}) collective-permute-start(f32[5,3,8,128]{3,2,1,0:T(8,128)S(1)} %get-tuple-element.40), channel_id=1, source_target_pairs={{0,12},{4,8},{8,4},{12,0},{16,28},{20,24},{24,20},{28,16},{1,13},{... | collective-permute-start | bytes 184328 | tf_op jit(solution)/shard_map/ppermute | solution.py:353
  8.8 4.8 %collective-permute-start.4 = (f32[5,3,8,128]{3,2,1,0:T(8,128)S(1)}, f32[5,3,8,128]{3,2,1,0:T(8,128)S(1)}, u32[]{:S(2)}, u32[]{:S(2)}) collective-permute-start(f32[5,3,8,128]{3,2,1,0:T(8,128)S(1)} %get-tuple-element.41), channel_id=1, source_target_pairs={{0,4},{4,0},{8,12},{12,8},{16,20},{20,16},{24,28},{28,24},{1,5},{5... | collective-permute-start | bytes 184328 | tf_op jit(solution)/shard_map/ppermute | solution.py:353
  10.0 6.3 %collective-permute-start.6 = (f32[3,3,8,128]{3,2,1,0:T(8,128)S(1)}, f32[3,3,8,128]{3,2,1,0:T(8,128)S(1)}, u32[]{:S(2)}, u32[]{:S(2)}) collective-permute-start(f32[3,3,8,128]{3,2,1,0:T(8,128)S(1)} %get-tuple-element.47), channel_id=1, source_target_pairs={{0,8},{4,12},{8,0},{12,4},{16,24},{20,28},{24,16},{28,20},{1,9},{5... | collective-permute-start | bytes 110600 | tf_op jit(solution)/shard_map/ppermute | solution.py:353
  11.7 4.9 %collective-permute-start.7 = (f32[3,3,8,128]{3,2,1,0:T(8,128)S(1)}, f32[3,3,8,128]{3,2,1,0:T(8,128)S(1)}, u32[]{:S(2)}, u32[]{:S(2)}) collective-permute-start(f32[3,3,8,128]{3,2,1,0:T(8,128)S(1)} %get-tuple-element.48), channel_id=1, source_target_pairs={{0,12},{4,8},{8,4},{12,0},{16,28},{20,24},{24,20},{28,16},{1,13},{... | collective-permute-start | bytes 110600 | tf_op jit(solution)/shard_map/ppermute | solution.py:353
  13.1 4.0 %collective-permute-start.8 = (f32[3,3,8,128]{3,2,1,0:T(8,128)S(1)}, f32[3,3,8,128]{3,2,1,0:T(8,128)S(1)}, u32[]{:S(2)}, u32[]{:S(2)}) collective-permute-start(f32[3,3,8,128]{3,2,1,0:T(8,128)S(1)} %get-tuple-element.49), channel_id=1, source_target_pairs={{0,4},{4,0},{8,12},{12,8},{16,20},{20,16},{24,28},{28,24},{1,5},{5... | collective-permute-start | bytes 110600 | tf_op jit(solution)/shard_map/ppermute | solution.py:353
  13.7 6.1 %collective-permute-start.5 = (f32[5,3,8,128]{3,2,1,0:T(8,128)S(1)}, f32[5,3,8,128]{3,2,1,0:T(8,128)S(1)}, u32[]{:S(2)}, u32[]{:S(2)}) collective-permute-start(f32[5,3,8,128]{3,2,1,0:T(8,128)S(1)} %shard_map.32), channel_id=1, source_target_pairs={{0,16},{4,20},{8,24},{12,28},{16,0},{20,4},{24,8},{28,12},{1,17},{... | collective-permute-start | bytes 184328 | tf_op jit(solution)/shard_map/ppermute | solution.py:360
  17.1 4.9 %collective-permute-start.9 = (f32[3,3,8,128]{3,2,1,0:T(8,128)S(1)}, f32[3,3,8,128]{3,2,1,0:T(8,128)S(1)}, u32[]{:S(2)}, u32[]{:S(2)}) collective-permute-start(f32[3,3,8,128]{3,2,1,0:T(8,128)S(1)} %shard_map.34), channel_id=1, source_target_pairs={{0,16},{4,20},{8,24},{12,28},{16,0},{20,4},{24,8},{28,12},{1,17},{... | collective-permute-start | bytes 110600 | tf_op jit(solution)/shard_map/ppermute | solution.py:360
  20.6 5.5 %collective-permute-start.12 = (f32[5,3,8,128]{3,2,1,0:T(8,128)S(1)}, f32[5,3,8,128]{3,2,1,0:T(8,128)S(1)}, u32[]{:S(2)}, u32[]{:S(2)}) collective-permute-start(f32[5,3,8,128]{3,2,1,0:T(8,128)S(1)} %get-tuple-element.53), channel_id=1, source_target_pairs={{0,4},{4,0},{8,12},{12,8},{16,20},{20,16},{24,28},{28,24},{1,5},{5... | collective-permute-start | bytes 184328 | tf_op jit(solution)/shard_map/ppermute | solution.py:353
  22.0 4.7 %collective-permute-start.10 = (f32[8,3,8,128]{3,2,1,0:T(8,128)S(1)}, f32[8,3,8,128]{3,2,1,0:T(8,128)S(1)}, u32[]{:S(2)}, u32[]{:S(2)}) collective-permute-start(f32[8,3,8,128]{3,2,1,0:T(8,128)S(1)} %get-tuple-element.51), channel_id=1, source_target_pairs={{0,8},{4,12},{8,0},{12,4},{16,24},{20,28},{24,16},{28,20},{1,9},{5... | collective-permute-start | bytes 294920 | tf_op jit(solution)/shard_map/ppermute | solution.py:353
  23.7 5.6 %collective-permute-start.11 = (f32[8,3,8,128]{3,2,1,0:T(8,128)S(1)}, f32[8,3,8,128]{3,2,1,0:T(8,128)S(1)}, u32[]{:S(2)}, u32[]{:S(2)}) collective-permute-start(f32[8,3,8,128]{3,2,1,0:T(8,128)S(1)} %get-tuple-element.52), channel_id=1, source_target_pairs={{0,12},{4,8},{8,4},{12,0},{16,28},{20,24},{24,20},{28,16},{1,13},{... | collective-permute-start | bytes 294920 | tf_op jit(solution)/shard_map/ppermute | solution.py:353
  24.6 5.0 %collective-permute-start.13 = (f32[3,3,8,128]{3,2,1,0:T(8,128)S(1)}, f32[3,3,8,128]{3,2,1,0:T(8,128)S(1)}, u32[]{:S(2)}, u32[]{:S(2)}) collective-permute-start(f32[3,3,8,128]{3,2,1,0:T(8,128)S(1)} %shard_map.37), channel_id=1, source_target_pairs={{0,4},{4,0},{8,12},{12,8},{16,20},{20,16},{24,28},{28,24},{1,5},{5... | collective-permute-start | bytes 110600 | tf_op jit(solution)/shard_map/ppermute | solution.py:353

commit v10 on v8

--- a/solution.py
+++ b/solution.py
@@ -208,7 +208,8 @@
                 last, here = here, ahead
         return 0
 
-    lax.fori_loop(0, STEPS, step, 0)
+    for turn in range(STEPS):
+        step(turn, 0)
     for slot in range(jumps.shape[1]):
         if slot < width:
             end, lost = load(strip, STAGES, slot), load(faded, side, slot)

time: 28.8 us -> 28.7 us (level)
  transfers between devices with their start and end apart: 14 -> 14, of which waited for: 5 -> 5; matrix products, arithmetic and copies ran while one was open for 0% -> 0% of each run, Pallas kernels for 12% -> 11%
where the time goes in v10:
time: 28.7 us; the launch traced here: 28.5 us
  starting transfers between devices  19.4 us (68%)
  waiting for transfers between devices  4.78 us (17%)
  Pallas kernels  3.24 us (11%)
  local copies, waits for them, and re-layouts  1 us (3%)
    ppermute x10, starting transfers between devices, exchange(): lax.ppermute(value, 'tm', [(i, i ^ partner(k)) for i in range(slices)])  11 us
    ppermute x2, starting transfers between devices, onward(): lax.ppermute(value, 'tm', [(i, (i + step) % slices) for i in range(slices)])  5.31 us
    ppermute x10, waiting for transfers between devices, exchange(): lax.ppermute(value, 'tm', [(i, i ^ partner(k)) for i in range(slices)])  3.67 us
    ppermute x2, starting transfers between devices, halo(): return lax.ppermute(value, 'gz', [(i, j % slabs) for i, j in pairs])  3.16 us
    pallas_call x10, Pallas kernels, call(): pl.pallas_call(kernel, out_shape=out_shape, in_specs=[VMEM] * len(args),...  2.42 us
    ppermute x2, waiting for transfers between devices, onward(): lax.ppermute(value, 'tm', [(i, (i + step) % slices) for i in range(slices)])  1.11 us
    unnamed x4, local copies, waits for them, and re-layouts  1 us
    pallas_call x1, Pallas kernels, shards(): pl.pallas_call(first_kernel, out_shape=f32(*own.shape), in_specs=[VMEM],...  0.79 us
  transfers between devices with their start and end apart: 14, of which 5 were waited for; matrix products, arithmetic and copies ran while one was open for 0% of the time, Pallas kernels for 11%

profile of v10, /device:TPU:0, one launch (start us, length us, event | category | flops | bytes accessed | tf_op | source)
XLA Modules:
  0.0 28.5 jit_solution(1568982664211683446)
XLA Ops:
  0.0 1.0 %copy-done = f32[1,3,16,16,128]{4,3,2,1,0:T(8,128)S(1)} copy-done((f32[1,3,16,16,128]{4,3,2,1,0:T(8,128)S(1)}, f32[1,3,16,16,128]{4,3,2,1,0:T(8,128)}, u32[]{:S(2)}) %copy-start) | copy-done | bytes 393240
  1.0 0.5 %collective-permute-start = (f32[3,6,16,128]{3,2,1,0:T(8,128)S(1)}, f32[3,6,16,128]{3,2,1,0:T(8,128)S(1)}, u32[]{:S(2)}, u32[]{:S(2)}) collective-permute-start(f32[3,6,16,128]{3,2,1,0:T(8,128)S(1)} %get-tuple-element.31), channel_id=1, source_target_pairs={{0,1},{1,0},{2,3},{3,2},{4,5},{5,4},{6,7},{7,6},{8,9},{9,8},{10,11... | collective-permute-start | bytes 442376 | tf_op jit(solution)/shard_map/ppermute | solution.py:351
  1.5 2.6 %collective-permute-start.1 = (f32[3,6,16,128]{3,2,1,0:T(8,128)S(1)}, f32[3,6,16,128]{3,2,1,0:T(8,128)S(1)}, u32[]{:S(2)}, u32[]{:S(2)}) collective-permute-start(f32[3,6,16,128]{3,2,1,0:T(8,128)S(1)} %get-tuple-element.36), channel_id=1, source_target_pairs={{0,3},{1,2},{2,1},{3,0},{4,7},{5,6},{6,5},{7,4},{8,11},{9,10},{10,... | collective-permute-start | bytes 442376 | tf_op jit(solution)/shard_map/ppermute | solution.py:351
  4.2 0.8 %shard_map.29 = (f32[6,2,3,3,2,8,128]{6,5,4,3,2,1,0:T(8,128)S(1)}, f32[4,3,2,8,128]{4,3,2,1,0:T(8,128)S(1)}, f32[2,6,3,2,8,128]{5,4,3,2,1,0:T(8,128)S(1)}, f32[8...) custom-call(f32[3,16,16,128]{3,2,1,0:T(8,128)S(1)} %bitcast.3, f32[16,16,128]{2,1,0:T(8,128)S(1)} %copy-done.1), custom_call_target="tpu_custom_call" | custom-call | flops 67108864 | bytes 1048576 | tf_op jit(solution)/shard_map/pallas_call | solution.py:26
  5.1 0.6 %shard_map.30 = (f32[5,3,8,128]{3,2,1,0:T(8,128)S(1)}, f32[5,3,8,128]{3,2,1,0:T(8,128)S(1)}, f32[5,3,8,128]{3,2,1,0:T(8,128)S(1)}, f32[5,3,8,128]{3,2,1,0:T(8,128)S(1)}) custom-call(f32[3,6,16,128]{3,2,1,0:T(8,128)S(1)} %collective-permute-done.face_ref, f32[6,2,3,3,2,8,128]{6,5,4,3,2,1,0:T(8,128)S(1)} %get-tuple-element.32.edges, ...), custom_call_target="tpu_custom_call" | custom-call | flops 4294967296 | bytes 1048576 | tf_op jit(solution)/shard_map/pallas_call | solution.py:26
  5.7 2.6 %collective-permute-start.2 = (f32[5,3,8,128]{3,2,1,0:T(8,128)S(1)}, f32[5,3,8,128]{3,2,1,0:T(8,128)S(1)}, u32[]{:S(2)}, u32[]{:S(2)}) collective-permute-start(f32[5,3,8,128]{3,2,1,0:T(8,128)S(1)} %get-tuple-element.39), channel_id=1, source_target_pairs={{0,12},{4,8},{8,4},{12,0},{16,28},{20,24},{24,20},{28,16},{1,13},{... | collective-permute-start | bytes 184328 | tf_op jit(solution)/shard_map/ppermute | solution.py:354
  8.3 0.4 %collective-permute-start.3 = (f32[5,3,8,128]{3,2,1,0:T(8,128)S(1)}, f32[5,3,8,128]{3,2,1,0:T(8,128)S(1)}, u32[]{:S(2)}, u32[]{:S(2)}) collective-permute-start(f32[5,3,8,128]{3,2,1,0:T(8,128)S(1)} %get-tuple-element.40), channel_id=1, source_target_pairs={{0,8},{4,12},{8,0},{12,4},{16,24},{20,28},{24,16},{28,20},{1,9},{5... | collective-permute-start | bytes 184328 | tf_op jit(solution)/shard_map/ppermute | solution.py:354
  8.7 0.5 %collective-permute-start.4 = (f32[5,3,8,128]{3,2,1,0:T(8,128)S(1)}, f32[5,3,8,128]{3,2,1,0:T(8,128)S(1)}, u32[]{:S(2)}, u32[]{:S(2)}) collective-permute-start(f32[5,3,8,128]{3,2,1,0:T(8,128)S(1)} %get-tuple-element.41), channel_id=1, source_target_pairs={{0,4},{4,0},{8,12},{12,8},{16,20},{20,16},{24,28},{28,24},{1,5},{5... | collective-permute-start | bytes 184328 | tf_op jit(solution)/shard_map/ppermute | solution.py:354
  9.3 0.0 collective-permute-done.1.face_ref
  9.3 0.6 %shard_map.31 = (f32[3,3,8,128]{3,2,1,0:T(8,128)S(1)}, f32[3,3,8,128]{3,2,1,0:T(8,128)S(1)}, f32[3,3,8,128]{3,2,1,0:T(8,128)S(1)}, f32[3,3,8,128]{3,2,1,0:T(8,128)S(1)}) custom-call(f32[3,6,16,128]{3,2,1,0:T(8,128)S(1)} %collective-permute-done.1.face_ref, f32[6,2,3,3,2,8,128]{6,5,4,3,2,1,0:T(8,128)S(1)} %get-tuple-element.32.edges, ...), custom_call_target="tpu_custom_call" | custom-call | flops 4294967296 | bytes 1048576 | tf_op jit(solution)/shard_map/pallas_call | solution.py:26
  9.9 2.6 %collective-permute-start.6 = (f32[3,3,8,128]{3,2,1,0:T(8,128)S(1)}, f32[3,3,8,128]{3,2,1,0:T(8,128)S(1)}, u32[]{:S(2)}, u32[]{:S(2)}) collective-permute-start(f32[3,3,8,128]{3,2,1,0:T(8,128)S(1)} %get-tuple-element.47), channel_id=1, source_target_pairs={{0,12},{4,8},{8,4},{12,0},{16,28},{20,24},{24,20},{28,16},{1,13},{... | collective-permute-start | bytes 110600 | tf_op jit(solution)/shard_map/ppermute | solution.py:354
  12.5 0.4 %collective-permute-start.7 = (f32[3,3,8,128]{3,2,1,0:T(8,128)S(1)}, f32[3,3,8,128]{3,2,1,0:T(8,128)S(1)}, u32[]{:S(2)}, u32[]{:S(2)}) collective-permute-start(f32[3,3,8,128]{3,2,1,0:T(8,128)S(1)} %get-tuple-element.48), channel_id=1, source_target_pairs={{0,8},{4,12},{8,0},{12,4},{16,24},{20,28},{24,16},{28,20},{1,9},{5... | collective-permute-start | bytes 110600 | tf_op jit(solution)/shard_map/ppermute | solution.py:354
  12.9 0.5 %collective-permute-start.8 = (f32[3,3,8,128]{3,2,1,0:T(8,128)S(1)}, f32[3,3,8,128]{3,2,1,0:T(8,128)S(1)}, u32[]{:S(2)}, u32[]{:S(2)}) collective-permute-start(f32[3,3,8,128]{3,2,1,0:T(8,128)S(1)} %get-tuple-element.49), channel_id=1, source_target_pairs={{0,4},{4,0},{8,12},{12,8},{16,20},{20,16},{24,28},{28,24},{1,5},{5... | collective-permute-start | bytes 110600 | tf_op jit(solution)/shard_map/ppermute | solution.py:354
  13.4 0.0 collective-permute-done.3.refs_2_
  13.4 0.0 collective-permute-done.4.refs_3_
  13.5 2.7 %collective-permute-start.5 = (f32[5,3,8,128]{3,2,1,0:T(8,128)S(1)}, f32[5,3,8,128]{3,2,1,0:T(8,128)S(1)}, u32[]{:S(2)}, u32[]{:S(2)}) collective-permute-start(f32[5,3,8,128]{3,2,1,0:T(8,128)S(1)} %shard_map.32), channel_id=1, source_target_pairs={{0,16},{4,20},{8,24},{12,28},{16,0},{20,4},{24,8},{28,12},{1,17},{... | collective-permute-start | bytes 184328 | tf_op jit(solution)/shard_map/ppermute | solution.py:361
  16.1 0.0 collective-permute-done.6.refs_1_
  16.2 0.4 %collective-permute-done.7.refs_2_ = f32[3,3,8,128]{3,2,1,0:T(8,128)S(1)} collective-permute-done((f32[3,3,8,128]{3,2,1,0:T(8,128)S(1)}, f32[3,3,8,128]{3,2,1,0:T(8,128)S(1)}, u32[]{:S(2)}, u32[]{:S(2)}) %collective-permute-start.7) | collective-permute-done | bytes 36896 | tf_op jit(solution)/shard_map/ppermute | solution.py:354
  16.6 0.3 %collective-permute-done.8.refs_3_ = f32[3,3,8,128]{3,2,1,0:T(8,128)S(1)} collective-permute-done((f32[3,3,8,128]{3,2,1,0:T(8,128)S(1)}, f32[3,3,8,128]{3,2,1,0:T(8,128)S(1)}, u32[]{:S(2)}, u32[]{:S(2)}) %collective-permute-start.8) | collective-permute-done | bytes 36896 | tf_op jit(solution)/shard_map/ppermute | solution.py:354
  16.9 2.7 %collective-permute-start.9 = (f32[3,3,8,128]{3,2,1,0:T(8,128)S(1)}, f32[3,3,8,128]{3,2,1,0:T(8,128)S(1)}, u32[]{:S(2)}, u32[]{:S(2)}) collective-permute-start(f32[3,3,8,128]{3,2,1,0:T(8,128)S(1)} %shard_map.34), channel_id=1, source_target_pairs={{0,16},{4,20},{8,24},{12,28},{16,0},{20,4},{24,8},{28,12},{1,17},{... | collective-permute-start | bytes 110600 | tf_op jit(solution)/shard_map/ppermute | solution.py:361
  19.5 0.0 collective-permute-done.5.carry_ref
  19.5 0.1 shard_map.33
  19.6 0.8 %shard_map.38._ = f32[3,16,16,128]{3,2,1,0:T(8,128)} custom-call(f32[16,3,2,8,128]{4,3,2,1,0:T(8,128)S(1)} %get-tuple-element.56.kept), custom_call_target="tpu_custom_call" | custom-call | flops 4294967296 | bytes 1048576 | tf_op jit(solution)/shard_map/pallas_call | solution.py:437
  20.4 0.3 %collective-permute-start.12 = (f32[5,3,8,128]{3,2,1,0:T(8,128)S(1)}, f32[5,3,8,128]{3,2,1,0:T(8,128)S(1)}, u32[]{:S(2)}, u32[]{:S(2)}) collective-permute-start(f32[5,3,8,128]{3,2,1,0:T(8,128)S(1)} %get-tuple-element.53), channel_id=1, source_target_pairs={{0,4},{4,0},{8,12},{12,8},{16,20},{20,16},{24,28},{28,24},{1,5},{5... | collective-permute-start | bytes 184328 | tf_op jit(solution)/shard_map/ppermute | solution.py:354
  20.7 1.1 %collective-permute-done.9.carry_ref = f32[3,3,8,128]{3,2,1,0:T(8,128)S(1)} collective-permute-done((f32[3,3,8,128]{3,2,1,0:T(8,128)S(1)}, f32[3,3,8,128]{3,2,1,0:T(8,128)S(1)}, u32[]{:S(2)}, u32[]{:S(2)}) %collective-permute-start.9) | collective-permute-done | bytes 36896 | tf_op jit(solution)/shard_map/ppermute | solution.py:361
  21.8 0.1 shard_map.35
  21.9 1.9 %collective-permute-start.10 = (f32[8,3,8,128]{3,2,1,0:T(8,128)S(1)}, f32[8,3,8,128]{3,2,1,0:T(8,128)S(1)}, u32[]{:S(2)}, u32[]{:S(2)}) collective-permute-start(f32[8,3,8,128]{3,2,1,0:T(8,128)S(1)} %get-tuple-element.51), channel_id=1, source_target_pairs={{0,12},{4,8},{8,4},{12,0},{16,28},{20,24},{24,20},{28,16},{1,13},{... | collective-permute-start | bytes 294920 | tf_op jit(solution)/shard_map/ppermute | solution.py:354
  23.8 0.4 %collective-permute-start.11 = (f32[8,3,8,128]{3,2,1,0:T(8,128)S(1)}, f32[8,3,8,128]{3,2,1,0:T(8,128)S(1)}, u32[]{:S(2)}, u32[]{:S(2)}) collective-permute-start(f32[8,3,8,128]{3,2,1,0:T(8,128)S(1)} %get-tuple-element.52), channel_id=1, source_target_pairs={{0,8},{4,12},{8,0},{12,4},{16,24},{20,28},{24,16},{28,20},{1,9},{5... | collective-permute-start | bytes 294920 | tf_op jit(solution)/shard_map/ppermute | solution.py:354
  24.2 1.2 %collective-permute-start.13 = (f32[3,3,8,128]{3,2,1,0:T(8,128)S(1)}, f32[3,3,8,128]{3,2,1,0:T(8,128)S(1)}, u32[]{:S(2)}, u32[]{:S(2)}) collective-permute-start(f32[3,3,8,128]{3,2,1,0:T(8,128)S(1)} %shard_map.37), channel_id=1, source_target_pairs={{0,4},{4,0},{8,12},{12,8},{16,20},{20,16},{24,28},{28,24},{1,5},{5... | collective-permute-start | bytes 110600 | tf_op jit(solution)/shard_map/ppermute | solution.py:354
  25.4 2.0 %collective-permute-done.10.across = f32[8,3,8,128]{3,2,1,0:T(8,128)S(1)} collective-permute-done((f32[8,3,8,128]{3,2,1,0:T(8,128)S(1)}, f32[8,3,8,128]{3,2,1,0:T(8,128)S(1)}, u32[]{:S(2)}, u32[]{:S(2)}) %collective-permute-start.10) | collective-permute-done | bytes 98336 | tf_op jit(solution)/shard_map/ppermute | solution.py:354
  27.4 0.9 %collective-permute-done.11.back = f32[8,3,8,128]{3,2,1,0:T(8,128)S(1)} collective-permute-done((f32[8,3,8,128]{3,2,1,0:T(8,128)S(1)}, f32[8,3,8,128]{3,2,1,0:T(8,128)S(1)}, u32[]{:S(2)}, u32[]{:S(2)}) %collective-permute-start.11) | collective-permute-done | bytes 98336 | tf_op jit(solution)/shard_map/ppermute | solution.py:354
  28.4 0.1 shard_map.36.gathered
  (12 shorter events, 0.1 us)
Async XLA Ops:
  0.0 1.0 %copy-start = (f32[1,3,16,16,128]{4,3,2,1,0:T(8,128)S(1)}, f32[1,3,16,16,128]{4,3,2,1,0:T(8,128)}, u32[]{:S(2)}) copy-start(f32[1,3,16,16,128]{4,3,2,1,0:T(8,128)} %param.2) | copy-start | bytes 1179652
  1.0 3.2 %copy-start.1 = (f32[16,16,128]{2,1,0:T(8,128)S(1)}, f32[16,16,128]{2,1,0:T(8,128)}, u32[]{:S(2)}) copy-start(f32[16,16,128]{2,1,0:T(8,128)} %rate_ref.1) | copy-start | bytes 393220
  1.0 4.0 %collective-permute-start = (f32[3,6,16,128]{3,2,1,0:T(8,128)S(1)}, f32[3,6,16,128]{3,2,1,0:T(8,128)S(1)}, u32[]{:S(2)}, u32[]{:S(2)}) collective-permute-start(f32[3,6,16,128]{3,2,1,0:T(8,128)S(1)} %get-tuple-element.31), channel_id=1, source_target_pairs={{0,1},{1,0},{2,3},{3,2},{4,5},{5,4},{6,7},{7,6},{8,9},{9,8},{10,11... | collective-permute-start | bytes 442376 | tf_op jit(solution)/shard_map/ppermute | solution.py:351
  1.5 7.7 %collective-permute-start.1 = (f32[3,6,16,128]{3,2,1,0:T(8,128)S(1)}, f32[3,6,16,128]{3,2,1,0:T(8,128)S(1)}, u32[]{:S(2)}, u32[]{:S(2)}) collective-permute-start(f32[3,6,16,128]{3,2,1,0:T(8,128)S(1)} %get-tuple-element.36), channel_id=1, source_target_pairs={{0,3},{1,2},{2,1},{3,0},{4,7},{5,6},{6,5},{7,4},{8,11},{9,10},{10,... | collective-permute-start | bytes 442376 | tf_op jit(solution)/shard_map/ppermute | solution.py:351
  5.7 7.2 %collective-permute-start.2 = (f32[5,3,8,128]{3,2,1,0:T(8,128)S(1)}, f32[5,3,8,128]{3,2,1,0:T(8,128)S(1)}, u32[]{:S(2)}, u32[]{:S(2)}) collective-permute-start(f32[5,3,8,128]{3,2,1,0:T(8,128)S(1)} %get-tuple-element.39), channel_id=1, source_target_pairs={{0,12},{4,8},{8,4},{12,0},{16,28},{20,24},{24,20},{28,16},{1,13},{... | collective-permute-start | bytes 184328 | tf_op jit(solution)/shard_map/ppermute | solution.py:354
  8.3 5.2 %collective-permute-start.3 = (f32[5,3,8,128]{3,2,1,0:T(8,128)S(1)}, f32[5,3,8,128]{3,2,1,0:T(8,128)S(1)}, u32[]{:S(2)}, u32[]{:S(2)}) collective-permute-start(f32[5,3,8,128]{3,2,1,0:T(8,128)S(1)} %get-tuple-element.40), channel_id=1, source_target_pairs={{0,8},{4,12},{8,0},{12,4},{16,24},{20,28},{24,16},{28,20},{1,9},{5... | collective-permute-start | bytes 184328 | tf_op jit(solution)/shard_map/ppermute | solution.py:354
  8.7 4.7 %collective-permute-start.4 = (f32[5,3,8,128]{3,2,1,0:T(8,128)S(1)}, f32[5,3,8,128]{3,2,1,0:T(8,128)S(1)}, u32[]{:S(2)}, u32[]{:S(2)}) collective-permute-start(f32[5,3,8,128]{3,2,1,0:T(8,128)S(1)} %get-tuple-element.41), channel_id=1, source_target_pairs={{0,4},{4,0},{8,12},{12,8},{16,20},{20,16},{24,28},{28,24},{1,5},{5... | collective-permute-start | bytes 184328 | tf_op jit(solution)/shard_map/ppermute | solution.py:354
  9.9 6.3 %collective-permute-start.6 = (f32[3,3,8,128]{3,2,1,0:T(8,128)S(1)}, f32[3,3,8,128]{3,2,1,0:T(8,128)S(1)}, u32[]{:S(2)}, u32[]{:S(2)}) collective-permute-start(f32[3,3,8,128]{3,2,1,0:T(8,128)S(1)} %get-tuple-element.47), channel_id=1, source_target_pairs={{0,12},{4,8},{8,4},{12,0},{16,28},{20,24},{24,20},{28,16},{1,13},{... | collective-permute-start | bytes 110600 | tf_op jit(solution)/shard_map/ppermute | solution.py:354
  12.5 4.1 %collective-permute-start.7 = (f32[3,3,8,128]{3,2,1,0:T(8,128)S(1)}, f32[3,3,8,128]{3,2,1,0:T(8,128)S(1)}, u32[]{:S(2)}, u32[]{:S(2)}) collective-permute-start(f32[3,3,8,128]{3,2,1,0:T(8,128)S(1)} %get-tuple-element.48), channel_id=1, source_target_pairs={{0,8},{4,12},{8,0},{12,4},{16,24},{20,28},{24,16},{28,20},{1,9},{5... | collective-permute-start | bytes 110600 | tf_op jit(solution)/shard_map/ppermute | solution.py:354
  12.9 4.0 %collective-permute-start.8 = (f32[3,3,8,128]{3,2,1,0:T(8,128)S(1)}, f32[3,3,8,128]{3,2,1,0:T(8,128)S(1)}, u32[]{:S(2)}, u32[]{:S(2)}) collective-permute-start(f32[3,3,8,128]{3,2,1,0:T(8,128)S(1)} %get-tuple-element.49), channel_id=1, source_target_pairs={{0,4},{4,0},{8,12},{12,8},{16,20},{20,16},{24,28},{28,24},{1,5},{5... | collective-permute-start | bytes 110600 | tf_op jit(solution)/shard_map/ppermute | solution.py:354
  13.5 6.1 %collective-permute-start.5 = (f32[5,3,8,128]{3,2,1,0:T(8,128)S(1)}, f32[5,3,8,128]{3,2,1,0:T(8,128)S(1)}, u32[]{:S(2)}, u32[]{:S(2)}) collective-permute-start(f32[5,3,8,128]{3,2,1,0:T(8,128)S(1)} %shard_map.32), channel_id=1, source_target_pairs={{0,16},{4,20},{8,24},{12,28},{16,0},{20,4},{24,8},{28,12},{1,17},{... | collective-permute-start | bytes 184328 | tf_op jit(solution)/shard_map/ppermute | solution.py:361
  16.9 4.9 %collective-permute-start.9 = (f32[3,3,8,128]{3,2,1,0:T(8,128)S(1)}, f32[3,3,8,128]{3,2,1,0:T(8,128)S(1)}, u32[]{:S(2)}, u32[]{:S(2)}) collective-permute-start(f32[3,3,8,128]{3,2,1,0:T(8,128)S(1)} %shard_map.34), channel_id=1, source_target_pairs={{0,16},{4,20},{8,24},{12,28},{16,0},{20,4},{24,8},{28,12},{1,17},{... | collective-permute-start | bytes 110600 | tf_op jit(solution)/shard_map/ppermute | solution.py:361
  20.4 5.0 %collective-permute-start.12 = (f32[5,3,8,128]{3,2,1,0:T(8,128)S(1)}, f32[5,3,8,128]{3,2,1,0:T(8,128)S(1)}, u32[]{:S(2)}, u32[]{:S(2)}) collective-permute-start(f32[5,3,8,128]{3,2,1,0:T(8,128)S(1)} %get-tuple-element.53), channel_id=1, source_target_pairs={{0,4},{4,0},{8,12},{12,8},{16,20},{20,16},{24,28},{28,24},{1,5},{5... | collective-permute-start | bytes 184328 | tf_op jit(solution)/shard_map/ppermute | solution.py:354
  21.9 5.6 %collective-permute-start.10 = (f32[8,3,8,128]{3,2,1,0:T(8,128)S(1)}, f32[8,3,8,128]{3,2,1,0:T(8,128)S(1)}, u32[]{:S(2)}, u32[]{:S(2)}) collective-permute-start(f32[8,3,8,128]{3,2,1,0:T(8,128)S(1)} %get-tuple-element.51), channel_id=1, source_target_pairs={{0,12},{4,8},{8,4},{12,0},{16,28},{20,24},{24,20},{28,16},{1,13},{... | collective-permute-start | bytes 294920 | tf_op jit(solution)/shard_map/ppermute | solution.py:354
  23.8 4.6 %collective-permute-start.11 = (f32[8,3,8,128]{3,2,1,0:T(8,128)S(1)}, f32[8,3,8,128]{3,2,1,0:T(8,128)S(1)}, u32[]{:S(2)}, u32[]{:S(2)}) collective-permute-start(f32[8,3,8,128]{3,2,1,0:T(8,128)S(1)} %get-tuple-element.52), channel_id=1, source_target_pairs={{0,8},{4,12},{8,0},{12,4},{16,24},{20,28},{24,16},{28,20},{1,9},{5... | collective-permute-start | bytes 294920 | tf_op jit(solution)/shard_map/ppermute | solution.py:354
  24.2 4.3 %collective-permute-start.13 = (f32[3,3,8,128]{3,2,1,0:T(8,128)S(1)}, f32[3,3,8,128]{3,2,1,0:T(8,128)S(1)}, u32[]{:S(2)}, u32[]{:S(2)}) collective-permute-start(f32[3,3,8,128]{3,2,1,0:T(8,128)S(1)} %shard_map.37), channel_id=1, source_target_pairs={{0,4},{4,0},{8,12},{12,8},{16,20},{20,16},{24,28},{28,24},{1,5},{5... | collective-permute-start | bytes 110600 | tf_op jit(solution)/shard_map/ppermute | solution.py:354
